TPU v7x, 256 devices: a whole 4x4x8 slice. The times are simulated.
256 devices in a mesh: member: 8 (over x, y_lo), tile: 32 (over z, y_hi, core).
Axes of the slice: x: 4, y: 4 (y_hi: 2, y_lo: 2; y = y_hi * 2 + y_lo), z: 8, core: 2. Of those that a mesh axis runs over, the one named last changes fastest.
Arguments:
- members: float32 [8, 6, 256, 512], P('member', None, 'tile'), may hold values from -6 to 6
- condition: float32 [6, 256, 512], P(None, 'tile'), may hold values from -6 to 6
- observed: float32 [6, 256, 512], P(None, 'tile'), may hold values from -6 to 6
- kernel_in: bfloat16 [9, 64, 9], replicated, may hold values from -0.625 to 0.625
- kernel_mid: bfloat16 [9, 64, 64], replicated, may hold values from -0.25 to 0.25
- kernel_out: bfloat16 [9, 6, 64], replicated, may hold values from -0.25 to 0.25
Outputs:
- pushed: float32 [8, 6, 256, 512], P('member', None, 'tile')
- energy: float32 [], replicated
- grad_in: float32 [9, 64, 9], replicated
- grad_mid: float32 [9, 64, 64], replicated
- grad_out: float32 [9, 6, 64], replicated
All inputs are finite; a program needn't handle non-finite values.
Results may differ from a plain program's by a relative error of at most 0.0004.
The roundings to bfloat16 on the way count: a program that leaves them out, or rounds other values in their place, can miss the bound.
Values may be sent and summed in bfloat16 or wider, within the bound.
No kernel may reach another device: no remote copies, remote signals or barrier semaphores. Data moves between devices by JAX's collectives and lax.ppermute only.
A program may use at most 64 MiB of HBM per device.

v0:
```python
import math

import jax
import jax.numpy as jnp
from jax import lax
from jax.sharding import PartitionSpec as P

EPSILON = 1e-06


def extended(array, sides, width):
    for axis, dim in sides:
        size, length = (lax.axis_size(axis), array.shape[dim])
        up = [(i, (i + 1) % size) for i in range(size - 1)]
        down = [(j, i) for i, j in up]
        last = lax.slice_in_dim(array, length - width, length, axis=dim)
        initial = lax.slice_in_dim(array, 0, width, axis=dim)
        before = lax.ppermute(last, axis, up)
        after = lax.ppermute(initial, axis, down)
        array = jnp.concatenate([before, array, after], axis=dim)
    return array


def passed_along(value, axis, steps):
    count = lax.axis_size(axis)
    pairs = [(source, (source + steps) % count) for source in range(count)]
    return lax.ppermute(value, axis, pairs)


def lat_weights(total_rows):
    position = jnp.arange(total_rows).astype(jnp.float32)
    radians = (-90.0 + 180.0 * (position + 0.5) / total_rows) * (jnp.pi / 180.0)
    cosine = jnp.cos(radians)
    return cosine / jnp.mean(cosine)


def silu_slope(pre_act):
    sigmoid = jax.nn.sigmoid(pre_act)
    return sigmoid * (1.0 + pre_act * (1.0 - sigmoid))


def window_at(padded, tap_index, row_count):
    row_step = tap_index // 3
    col_step = tap_index % 3
    return jnp.roll(padded[:, row_step : row_step + row_count, :], 1 - col_step, axis=2)


def convolve(padded, kernel, row_count):
    summed = None
    for tap_index in range(9):
        product = jnp.einsum(
            "oc,crl->orl",
            kernel[tap_index],
            window_at(padded, tap_index, row_count),
            preferred_element_type=jnp.float32,
        )
        summed = product if summed is None else summed + product
    return summed


def kernel_grad(grad_field, padded, row_count):
    return jnp.stack(
        [
            jnp.einsum(
                "orl,crl->oc",
                grad_field,
                window_at(padded, tap_index, row_count),
                preferred_element_type=jnp.float32,
            )
            for tap_index in range(9)
        ]
    )


def flipped(kernel):
    return jnp.transpose(kernel[::-1], (0, 2, 1))


def pad_rows(field):
    return extended(field, (("tile", 1),), 1)


def per_device(members, condition, observed, kernel_in, kernel_mid, kernel_out):
    member_state = members[0]
    row_count = member_state.shape[1]
    half_vars = member_state.shape[0] // 2
    member_count = lax.axis_size("member")
    tile_count = lax.axis_size("tile")
    total_rows = row_count * tile_count
    entries = member_state.shape[0] * total_rows * member_state.shape[2]
    lat_all = lat_weights(total_rows)
    base_row = lax.axis_index("tile") * row_count
    lat = lax.dynamic_slice_in_dim(lat_all, base_row, row_count, 0)[None, :, None]
    inputs = jnp.concatenate([member_state[:half_vars], condition], 0).astype(jnp.bfloat16)
    padded_in = pad_rows(inputs)
    pre_first = convolve(padded_in, kernel_in, row_count)
    hidden_first = jax.nn.silu(pre_first).astype(jnp.bfloat16)
    padded_first = pad_rows(hidden_first)
    pre_second = convolve(padded_first, kernel_mid, row_count)
    hidden_second = jax.nn.silu(pre_second).astype(jnp.bfloat16)
    padded_second = pad_rows(hidden_second)
    coupling = convolve(padded_second, kernel_out, row_count)
    log_scale = jnp.tanh(coupling[:half_vars])
    moving = member_state[half_vars:]
    moved = moving * jnp.exp(log_scale) + coupling[half_vars:]
    pushed = jnp.concatenate([member_state[:half_vars], moved], 0)
    others = []
    current = pushed
    for offset in range(1, member_count):
        current = passed_along(current, "member", 1)
        others.append(current)
    partials = [jnp.sum(lat * (pushed - observed) ** 2)]
    partials = partials + [jnp.sum(lat * (pushed - other_field) ** 2) for other_field in others]
    totals = [lax.psum(partial_sum, "tile") for partial_sum in partials]
    distances = [jnp.sqrt(total_sum / entries + EPSILON) for total_sum in totals]
    energy_share = distances[0] / member_count
    for offset in range(1, member_count):
        energy_share = energy_share - distances[offset] / (2.0 * member_count * member_count)
    inner = (pushed - observed) / (member_count * distances[0])
    for offset in range(1, member_count):
        inner = inner - (pushed - others[offset - 1]) / (
            member_count * member_count * distances[offset]
        )
    grad_pushed = lat * inner / math.sqrt(entries)
    upper_grad = grad_pushed[half_vars:]
    grad_scale = upper_grad * moving * jnp.exp(log_scale) * (1.0 - log_scale * log_scale)
    grad_coupling = jnp.concatenate([grad_scale, upper_grad], 0).astype(jnp.bfloat16)
    grad_last = kernel_grad(grad_coupling, padded_second, row_count)
    back_second = convolve(pad_rows(grad_coupling), flipped(kernel_out), row_count)
    grad_pre_second = (back_second * silu_slope(pre_second)).astype(jnp.bfloat16)
    padded_grad_second = pad_rows(grad_pre_second)
    grad_middle = kernel_grad(grad_pre_second, padded_first, row_count)
    back_first = convolve(padded_grad_second, flipped(kernel_mid), row_count)
    grad_pre_first = (back_first * silu_slope(pre_first)).astype(jnp.bfloat16)
    grad_first = kernel_grad(grad_pre_first, padded_in, row_count)
    energy = lax.psum(energy_share, "member")
    grad_first, grad_middle, grad_last = lax.psum(
        (grad_first, grad_middle, grad_last), ("member", "tile")
    )
    return (pushed[None], energy, grad_first, grad_middle, grad_last)


def solution(mesh):
    in_specs = (
        P("member", None, "tile", None),
        P(None, "tile", None),
        P(None, "tile", None),
        P(),
        P(),
        P(),
    )
    out_specs = (P("member", None, "tile", None), P(), P(), P(), P())
    return jax.shard_map(
        per_device, mesh=mesh, in_specs=in_specs, out_specs=out_specs, check_vma=False
    )
```

profile of v0, /device:TPU:1, one launch (start us, length us, event | category | flops | bytes accessed | tf_op | source)
XLA Modules:
  0.0 486.6 jit_solution(13000713858525988553)
XLA Ops:
  9.0 5.1 %collective-permute-start.1 = (bf16[9,1,512]{2,1,0:T(2,128)(2,1)S(1)}, bf16[9,1,512]{2,1,0:T(2,128)(2,1)S(1)}, u32[]{:S(2)}, u32[]{:S(2)}) collective-permute-start(bf16[9,1,512]{2,1,0:T(2,128)(2,1)S(1)} %get-tuple-element.99), channel_id=1, source_target_pairs={{1,0},{2,1},{3,2},{4,3},{5,4},{6,5},{7,6},{8,7},{9,8},{10,9},{11,1... | collective-permute-start | bytes 27656 | tf_op jit(solution)/shard_map/ppermute | solution.py:19
  14.1 3.0 collective-permute-start
  21.4 1.4 multiply_convert_fusion.1
  22.8 5.7 %collective-permute-start.2 = (bf16[64,1,512]{2,0,1:T(8,128)(2,1)S(1)}, bf16[64,1,512]{2,0,1:T(8,128)(2,1)S(1)}, u32[]{:S(2)}, u32[]{:S(2)}) collective-permute-start(bf16[64,1,512]{2,0,1:T(8,128)(2,1)S(1)} %get-tuple-element.77), channel_id=1, source_target_pairs={{0,1},{1,2},{2,3},{3,4},{4,5},{5,6},{6,7},{7,8},{8,9},{9,10},{10,1... | collective-permute-start | bytes 196616 | tf_op jit(solution)/shard_map/ppermute | solution.py:18
  28.6 1.9 collective-permute-start.3
  30.5 5.1 %collective-permute-done.3 = bf16[64,1,512]{2,0,1:T(8,128)(2,1)S(1)} collective-permute-done((bf16[64,1,512]{2,0,1:T(8,128)(2,1)S(1)}, bf16[64,1,512]{2,0,1:T(8,128)(2,1)S(1)}, u32[]{:S(2)}, u32[]{:S(2)}) %collective-permute-start.3) | collective-permute-done | bytes 65568 | tf_op jit(solution)/shard_map/ppermute | solution.py:19
  39.8 1.4 multiply_convert_fusion
  41.2 2.3 collective-permute-start.4
  43.5 2.0 collective-permute-start.5
  45.7 7.0 %collective-permute-done.5 = bf16[64,1,512]{2,0,1:T(8,128)(2,1)S(1)} collective-permute-done((bf16[64,1,512]{2,0,1:T(8,128)(2,1)S(1)}, bf16[64,1,512]{2,0,1:T(8,128)(2,1)S(1)}, u32[]{:S(2)}, u32[]{:S(2)}) %collective-permute-start.5) | collective-permute-done | bytes 65568 | tf_op jit(solution)/shard_map/ppermute | solution.py:19
  57.1 5.2 %collective-permute-done.6 = f32[6,8,512]{2,1,0:T(8,128)S(1)} collective-permute-done((f32[6,8,512]{2,1,0:T(8,128)S(1)}, f32[6,8,512]{2,1,0:T(8,128)S(1)}, u32[]{:S(2)}, u32[]{:S(2)}) %collective-permute-start.6) | collective-permute-done | bytes 98336 | tf_op jit(solution)/shard_map/ppermute | solution.py:27
  62.3 5.6 %collective-permute-done.7 = f32[6,8,512]{2,1,0:T(8,128)S(1)} collective-permute-done((f32[6,8,512]{2,1,0:T(8,128)S(1)}, f32[6,8,512]{2,1,0:T(8,128)S(1)}, u32[]{:S(2)}, u32[]{:S(2)}) %collective-permute-start.7) | collective-permute-done | bytes 98336 | tf_op jit(solution)/shard_map/ppermute | solution.py:27
  67.9 5.7 %collective-permute-done.8 = f32[6,8,512]{2,1,0:T(8,128)} collective-permute-done((f32[6,8,512]{2,1,0:T(8,128)S(1)}, f32[6,8,512]{2,1,0:T(8,128)}, u32[]{:S(2)}, u32[]{:S(2)}) %collective-permute-start.8) | collective-permute-done | bytes 98336 | tf_op jit(solution)/shard_map/ppermute | solution.py:27
  75.1 4.4 collective-permute-done.9
  79.6 5.8 %collective-permute-done.10 = f32[6,8,512]{2,1,0:T(8,128)S(1)} collective-permute-done((f32[6,8,512]{2,1,0:T(8,128)}, f32[6,8,512]{2,1,0:T(8,128)S(1)}, u32[]{:S(2)}, u32[]{:S(2)}) %collective-permute-start.10) | collective-permute-done | bytes 98336 | tf_op jit(solution)/shard_map/ppermute | solution.py:27
  86.1 6.0 %collective-permute-done.11 = f32[6,8,512]{2,1,0:T(8,128)S(1)} collective-permute-done((f32[6,8,512]{2,1,0:T(8,128)S(1)}, f32[6,8,512]{2,1,0:T(8,128)S(1)}, u32[]{:S(2)}, u32[]{:S(2)}) %collective-permute-start.11) | collective-permute-done | bytes 98336 | tf_op jit(solution)/shard_map/ppermute | solution.py:27
  92.1 5.6 %collective-permute-done.12 = f32[6,8,512]{2,1,0:T(8,128)S(1)} collective-permute-done((f32[6,8,512]{2,1,0:T(8,128)S(1)}, f32[6,8,512]{2,1,0:T(8,128)S(1)}, u32[]{:S(2)}, u32[]{:S(2)}) %collective-permute-start.12) | collective-permute-done | bytes 98336 | tf_op jit(solution)/shard_map/ppermute | solution.py:27
  97.7 2.5 multiply_reduce_fusion.3
  100.2 71.5 %all-reduce.1 = (f32[]{:T(128)}, f32[]{:T(128)}, f32[]{:T(128)}, f32[]{:T(128)}, f32[]{:T(128)}, /*index=5*/f32[]{:T(128)}, f32[]{:T(128)}, f32[]{:T(128)}) all-reduce(f32[]{:T(128)} %get-tuple-element.14, f32[]{:T(128)} %get-tuple-element.11, f32[]{:T(128)} %get-tuple-element.12, ...), channel_id=1, replica_groups=mesh['member'=8,'tile'=32] {'tile'}, use_global_device_ids=true, to_apply=%region_2.3 | all-reduce | flops 8 | bytes 64 | tf_op jit(solution)/shard_map/psum | solution.py:114
  177.1 1.6 divide_subtract_fusion
  179.9 2.1 collective-permute-start.14
  182.0 5.0 %collective-permute-start.13 = (bf16[6,1,512]{2,1,0:T(2,128)(2,1)S(1)}, bf16[6,1,512]{2,1,0:T(2,128)(2,1)S(1)}, u32[]{:S(2)}, u32[]{:S(2)}) collective-permute-start(bf16[6,1,512]{2,1,0:T(2,128)(2,1)S(1)} %get-tuple-element.115), channel_id=1, source_target_pairs={{0,1},{1,2},{2,3},{3,4},{4,5},{5,6},{6,7},{7,8},{8,9},{9,10},{10,1... | collective-permute-start | bytes 18440 | tf_op jit(solution)/shard_map/ppermute | solution.py:18
  187.2 13.0 %psum.92 = f32[]{:T(128)} all-reduce(f32[]{:T(128)S(6)} %sub.100), channel_id=1, replica_groups=mesh['member'=8,'tile'=32] {'member'}, use_global_device_ids=true, to_apply=%region_17.18 | all-reduce | flops 1 | bytes 8 | tf_op jit(solution)/shard_map/psum | solution.py:136
  212.6 1.0 fusion.17
  215.4 1.0 fusion.14
  216.4 5.3 %collective-permute-start.15 = (bf16[64,1,512]{2,0,1:T(8,128)(2,1)}, bf16[64,1,512]{2,0,1:T(8,128)(2,1)S(1)}, u32[]{:S(2)}, u32[]{:S(2)}) collective-permute-start(bf16[64,1,512]{2,0,1:T(8,128)(2,1)} %get-tuple-element.57), channel_id=1, source_target_pairs={{0,1},{1,2},{2,3},{3,4},{4,5},{5,6},{6,7},{7,8},{8,9},{9,10},{10,1... | collective-permute-start | bytes 196616 | tf_op jit(solution)/shard_map/ppermute | solution.py:18
  221.8 2.1 collective-permute-start.16
  227.2 1.9 collective-permute-done.16
  229.9 1.5 fusion.42
  238.5 86.6 %all-reduce = (f32[9,64,9]{1,2,0:T(8,128)}, f32[9,6,64]{2,1,0:T(8,128)}) all-reduce(f32[9,64,9]{1,2,0:T(8,128)S(1)} %fusion.21, f32[9,6,64]{2,1,0:T(8,128)S(1)} %fusion.30), channel_id=1, replica_groups=mesh['member'=8,'tile'=32] {'member','tile'}, use_global_device_ids=true, to_apply=%region_18.19 | all-reduce | flops 8640 | bytes 69120 | tf_op jit(solution)/shard_map/psum | solution.py:137
  325.2 152.9 %all-reduce.4.cloned.1.call-done = f32[9,64,64]{2,1,0:T(8,128)} async-done(((f32[9,64,64]{2,1,0:T(8,128)}), f32[9,64,64]{2,1,0:T(8,128)}) %all-reduce.4.cloned.1.call-update) | async-done | bytes 147472 | tf_op jit(solution)/shard_map/psum | solution.py:137
  478.0 1.7 copy.187
  (269 shorter events, 42.4 us)
Async XLA Ops:
  7.2 470.9 %all-reduce.4.cloned.1.call-start = ((), (), s32[]{:S(2)}) async-start(), calls=%async_computation | async-start | bytes 589824 | tf_op jit(solution)/shard_map/psum | solution.py:137
  8.9 9.3 %copy-start.68 = (bf16[9,64,9]{1,2,0:T(8,128)(2,1)S(1)}, bf16[9,64,9]{1,2,0:T(8,128)(2,1)}, u32[]{:S(2)}) copy-start(bf16[9,64,9]{1,2,0:T(8,128)(2,1)} %param.9) | copy-start | bytes 31108
  9.0 8.4 %collective-permute-start.1 = (bf16[9,1,512]{2,1,0:T(2,128)(2,1)S(1)}, bf16[9,1,512]{2,1,0:T(2,128)(2,1)S(1)}, u32[]{:S(2)}, u32[]{:S(2)}) collective-permute-start(bf16[9,1,512]{2,1,0:T(2,128)(2,1)S(1)} %get-tuple-element.99), channel_id=1, source_target_pairs={{1,0},{2,1},{3,2},{4,3},{5,4},{6,5},{7,6},{8,7},{9,8},{10,9},{11,1... | collective-permute-start | bytes 27656 | tf_op jit(solution)/shard_map/ppermute | solution.py:19
  14.1 3.9 collective-permute-start
  21.4 9.1 %copy-start.49 = (f32[1,6,8,512]{3,2,1,0:T(8,128)S(1)}, f32[1,6,8,512]{3,2,1,0:T(8,128)}, u32[]{:S(2)}) copy-start(f32[1,6,8,512]{3,2,1,0:T(8,128)} %param.6) | copy-start | bytes 294916
  22.8 7.7 %collective-permute-start.2 = (bf16[64,1,512]{2,0,1:T(8,128)(2,1)S(1)}, bf16[64,1,512]{2,0,1:T(8,128)(2,1)S(1)}, u32[]{:S(2)}, u32[]{:S(2)}) collective-permute-start(bf16[64,1,512]{2,0,1:T(8,128)(2,1)S(1)} %get-tuple-element.77), channel_id=1, source_target_pairs={{0,1},{1,2},{2,3},{3,4},{4,5},{5,6},{6,7},{7,8},{8,9},{9,10},{10,1... | collective-permute-start | bytes 196616 | tf_op jit(solution)/shard_map/ppermute | solution.py:18
  28.6 7.1 %collective-permute-start.3 = (bf16[64,1,512]{2,0,1:T(8,128)(2,1)S(1)}, bf16[64,1,512]{2,0,1:T(8,128)(2,1)S(1)}, u32[]{:S(2)}, u32[]{:S(2)}) collective-permute-start(bf16[64,1,512]{2,0,1:T(8,128)(2,1)S(1)} %get-tuple-element.78), channel_id=1, source_target_pairs={{1,0},{2,1},{3,2},{4,3},{5,4},{6,5},{7,6},{8,7},{9,8},{10,9},{11,1... | collective-permute-start | bytes 196616 | tf_op jit(solution)/shard_map/ppermute | solution.py:19
  30.5 7.5 %copy-start.12 = (bf16[64,1,512]{2,0,1:T(8,128)(2,1)}, bf16[64,1,512]{2,0,1:T(8,128)(2,1)S(1)}, u32[]{:S(2)}) copy-start(bf16[64,1,512]{2,0,1:T(8,128)(2,1)S(1)} %collective-permute-done.2) | copy-start | bytes 196612
  39.8 5.8 %copy-start.69 = (bf16[9,6,64]{2,1,0:T(8,128)(2,1)S(1)}, bf16[9,6,64]{2,1,0:T(8,128)(2,1)}, u32[]{:S(2)}) copy-start(bf16[9,6,64]{2,1,0:T(8,128)(2,1)} %param.11) | copy-start | bytes 20740
  41.2 4.5 collective-permute-start.4
  43.5 9.2 %collective-permute-start.5 = (bf16[64,1,512]{2,0,1:T(8,128)(2,1)S(1)}, bf16[64,1,512]{2,0,1:T(8,128)(2,1)S(1)}, u32[]{:S(2)}, u32[]{:S(2)}) collective-permute-start(bf16[64,1,512]{2,0,1:T(8,128)(2,1)S(1)} %get-tuple-element.68), channel_id=1, source_target_pairs={{1,0},{2,1},{3,2},{4,3},{5,4},{6,5},{7,6},{8,7},{9,8},{10,9},{11,1... | collective-permute-start | bytes 196616 | tf_op jit(solution)/shard_map/ppermute | solution.py:19
  45.7 10.2 %copy-start.52 = (bf16[64,1,512]{2,0,1:T(8,128)(2,1)}, bf16[64,1,512]{2,0,1:T(8,128)(2,1)S(1)}, u32[]{:S(2)}) copy-start(bf16[64,1,512]{2,0,1:T(8,128)(2,1)S(1)} %collective-permute-done.4) | copy-start | bytes 196612
  56.7 5.7 %collective-permute-start.6 = (f32[6,8,512]{2,1,0:T(8,128)S(1)}, f32[6,8,512]{2,1,0:T(8,128)S(1)}, u32[]{:S(2)}, u32[]{:S(2)}) collective-permute-start(f32[6,8,512]{2,1,0:T(8,128)S(1)} %pad_maximum_fusion.40), channel_id=1, source_target_pairs={{0,32},{32,64},{64,96},{96,128},{128,160},{160,192},{192,224},{224... | collective-permute-start | bytes 294920 | tf_op jit(solution)/shard_map/ppermute | solution.py:27
  62.3 11.3 %copy-start.45 = (f32[6,8,512]{2,1,0:T(8,128)}, f32[6,8,512]{2,1,0:T(8,128)S(1)}, u32[]{:S(2)}) copy-start(f32[6,8,512]{2,1,0:T(8,128)S(1)} %collective-permute-done.6) | copy-start | bytes 294916
  62.3 5.6 %collective-permute-start.7 = (f32[6,8,512]{2,1,0:T(8,128)S(1)}, f32[6,8,512]{2,1,0:T(8,128)S(1)}, u32[]{:S(2)}, u32[]{:S(2)}) collective-permute-start(f32[6,8,512]{2,1,0:T(8,128)S(1)} %collective-permute-done.6), channel_id=1, source_target_pairs={{0,32},{32,64},{64,96},{96,128},{128,160},{160,192},{192,224},{224... | collective-permute-start | bytes 294920 | tf_op jit(solution)/shard_map/ppermute | solution.py:27
  67.9 5.7 %copy-start.47 = (f32[6,8,512]{2,1,0:T(8,128)}, f32[6,8,512]{2,1,0:T(8,128)S(1)}, u32[]{:S(2)}) copy-start(f32[6,8,512]{2,1,0:T(8,128)S(1)} %collective-permute-done.7) | copy-start | bytes 294916
  67.9 5.7 %collective-permute-start.8 = (f32[6,8,512]{2,1,0:T(8,128)S(1)}, f32[6,8,512]{2,1,0:T(8,128)}, u32[]{:S(2)}, u32[]{:S(2)}) collective-permute-start(f32[6,8,512]{2,1,0:T(8,128)S(1)} %collective-permute-done.7), channel_id=1, source_target_pairs={{0,32},{32,64},{64,96},{96,128},{128,160},{160,192},{192,224},{224... | collective-permute-start | bytes 294920 | tf_op jit(solution)/shard_map/ppermute | solution.py:27
  73.6 5.9 %collective-permute-start.9 = (f32[6,8,512]{2,1,0:T(8,128)}, f32[6,8,512]{2,1,0:T(8,128)}, u32[]{:S(2)}, u32[]{:S(2)}) collective-permute-start(f32[6,8,512]{2,1,0:T(8,128)} %collective-permute-done.8), channel_id=1, source_target_pairs={{0,32},{32,64},{64,96},{96,128},{128,160},{160,192},{192,224},{224... | collective-permute-start | bytes 294920 | tf_op jit(solution)/shard_map/ppermute | solution.py:27
  73.7 103.3 %copy-start.44 = (f32[6,8,512]{2,1,0:T(8,128)S(1)}, f32[6,8,512]{2,1,0:T(8,128)}, u32[]{:S(2)}) copy-start(f32[6,8,512]{2,1,0:T(8,128)} %param.8) | copy-start | bytes 294916
  79.5 5.9 %collective-permute-start.10 = (f32[6,8,512]{2,1,0:T(8,128)}, f32[6,8,512]{2,1,0:T(8,128)S(1)}, u32[]{:S(2)}, u32[]{:S(2)}) collective-permute-start(f32[6,8,512]{2,1,0:T(8,128)} %collective-permute-done.9), channel_id=1, source_target_pairs={{0,32},{32,64},{64,96},{96,128},{128,160},{160,192},{192,224},{224... | collective-permute-start | bytes 294920 | tf_op jit(solution)/shard_map/ppermute | solution.py:27
  85.4 6.7 %collective-permute-start.11 = (f32[6,8,512]{2,1,0:T(8,128)S(1)}, f32[6,8,512]{2,1,0:T(8,128)S(1)}, u32[]{:S(2)}, u32[]{:S(2)}) collective-permute-start(f32[6,8,512]{2,1,0:T(8,128)S(1)} %collective-permute-done.10), channel_id=1, source_target_pairs={{0,32},{32,64},{64,96},{96,128},{128,160},{160,192},{192,224},{224... | collective-permute-start | bytes 294920 | tf_op jit(solution)/shard_map/ppermute | solution.py:27
  86.1 91.0 %copy-start.46 = (f32[6,8,512]{2,1,0:T(8,128)S(1)}, f32[6,8,512]{2,1,0:T(8,128)}, u32[]{:S(2)}) copy-start(f32[6,8,512]{2,1,0:T(8,128)} %copy-done.45) | copy-start | bytes 294916
  86.1 91.0 %copy-start.48 = (f32[6,8,512]{2,1,0:T(8,128)S(1)}, f32[6,8,512]{2,1,0:T(8,128)}, u32[]{:S(2)}) copy-start(f32[6,8,512]{2,1,0:T(8,128)} %copy-done.47) | copy-start | bytes 294916
  92.1 5.6 %collective-permute-start.12 = (f32[6,8,512]{2,1,0:T(8,128)S(1)}, f32[6,8,512]{2,1,0:T(8,128)S(1)}, u32[]{:S(2)}, u32[]{:S(2)}) collective-permute-start(f32[6,8,512]{2,1,0:T(8,128)S(1)} %collective-permute-done.11), channel_id=1, source_target_pairs={{0,32},{32,64},{64,96},{96,128},{128,160},{160,192},{192,224},{224... | collective-permute-start | bytes 294920 | tf_op jit(solution)/shard_map/ppermute | solution.py:27
  179.7 20.9 %copy-start.65 = (bf16[64,8,1]{2,0,1:T(8,128)(2,1)S(1)}, bf16[64,8,1]{2,0,1:T(8,128)(2,1)}, u32[]{:S(2)}) copy-start(bf16[64,8,1]{2,0,1:T(8,128)(2,1)} %copy-done.64) | copy-start | bytes 3076
  179.9 20.3 %collective-permute-start.14 = (bf16[6,1,512]{2,1,0:T(2,128)(2,1)S(1)}, bf16[6,1,512]{2,1,0:T(2,128)(2,1)S(1)}, u32[]{:S(2)}, u32[]{:S(2)}) collective-permute-start(bf16[6,1,512]{2,1,0:T(2,128)(2,1)S(1)} %get-tuple-element.114), channel_id=1, source_target_pairs={{1,0},{2,1},{3,2},{4,3},{5,4},{6,5},{7,6},{8,7},{9,8},{10,9},{11,1... | collective-permute-start | bytes 18440 | tf_op jit(solution)/shard_map/ppermute | solution.py:19
  182.0 18.2 %collective-permute-start.13 = (bf16[6,1,512]{2,1,0:T(2,128)(2,1)S(1)}, bf16[6,1,512]{2,1,0:T(2,128)(2,1)S(1)}, u32[]{:S(2)}, u32[]{:S(2)}) collective-permute-start(bf16[6,1,512]{2,1,0:T(2,128)(2,1)S(1)} %get-tuple-element.115), channel_id=1, source_target_pairs={{0,1},{1,2},{2,3},{3,4},{4,5},{5,6},{6,7},{7,8},{8,9},{9,10},{10,1... | collective-permute-start | bytes 18440 | tf_op jit(solution)/shard_map/ppermute | solution.py:18
  200.6 23.4 %copy-start.14 = (bf16[6,8,512]{2,1,0:T(8,128)(2,1)}, bf16[6,8,512]{2,1,0:T(8,128)(2,1)S(1)}, u32[]{:S(2)}) copy-start(bf16[6,8,512]{2,1,0:T(8,128)(2,1)S(1)} %get-tuple-element.111) | copy-start | bytes 147460
  214.5 9.5 %copy-start.51 = (bf16[64,1,512]{2,0,1:T(8,128)(2,1)S(1)}, bf16[64,1,512]{2,0,1:T(8,128)(2,1)}, u32[]{:S(2)}) copy-start(bf16[64,1,512]{2,0,1:T(8,128)(2,1)} %copy-done.50) | copy-start | bytes 196612
  215.4 9.4 %copy-start.17 = (bf16[64,1,512]{2,0,1:T(8,128)(2,1)S(1)}, bf16[64,1,512]{2,0,1:T(8,128)(2,1)}, u32[]{:S(2)}) copy-start(bf16[64,1,512]{2,0,1:T(8,128)(2,1)} %copy-done.16) | copy-start | bytes 196612
  216.4 10.7 %collective-permute-start.15 = (bf16[64,1,512]{2,0,1:T(8,128)(2,1)}, bf16[64,1,512]{2,0,1:T(8,128)(2,1)S(1)}, u32[]{:S(2)}, u32[]{:S(2)}) collective-permute-start(bf16[64,1,512]{2,0,1:T(8,128)(2,1)} %get-tuple-element.57), channel_id=1, source_target_pairs={{0,1},{1,2},{2,3},{3,4},{4,5},{5,6},{6,7},{7,8},{8,9},{9,10},{10,1... | collective-permute-start | bytes 196616 | tf_op jit(solution)/shard_map/ppermute | solution.py:18
  221.8 7.3 %collective-permute-start.16 = (bf16[64,1,512]{2,0,1:T(8,128)(2,1)}, bf16[64,1,512]{2,0,1:T(8,128)(2,1)S(1)}, u32[]{:S(2)}, u32[]{:S(2)}) collective-permute-start(bf16[64,1,512]{2,0,1:T(8,128)(2,1)} %get-tuple-element.58), channel_id=1, source_target_pairs={{1,0},{2,1},{3,2},{4,3},{5,4},{6,5},{7,6},{8,7},{9,8},{10,9},{11,1... | collective-permute-start | bytes 196616 | tf_op jit(solution)/shard_map/ppermute | solution.py:19
  (58 other events, 86.2 us)
Sparse Core Ops, SparseCore 0:
  227.3 250.6 all-reduce.3
where the time goes:
time: 488 us; the launch traced here: 487 us
  waiting for transfers between devices  206 us (42%)
  blocking collectives  171 us (35%)
  starting transfers between devices  35.2 us (7%)
  matrix products  30.9 us (6%)
  between operations  21.2 us (4%)
  other arithmetic  11.5 us (2%)
  local copies, waits for them, and re-layouts  11 us (2%)
    psum x1, waiting for transfers between devices, per_device(): lax.psum((grad_first, grad_middle, grad_last), ('member', 'tile'))  153 us
    psum x1, blocking collectives, per_device(): lax.psum((grad_first, grad_middle, grad_last), ('member', 'tile'))  86.6 us
    psum x1, blocking collectives, per_device(): totals = [lax.psum(partial_sum, 'tile') for partial_sum in partials]  71.5 us
    ppermute x7, waiting for transfers between devices, passed_along(): return lax.ppermute(value, axis, pairs)  38.2 us
    ppermute x5, starting transfers between devices, extended(): before = lax.ppermute(last, axis, up)  21.4 us
    dot_general x45, matrix products, convolve(): jnp.einsum('oc,crl->orl', kernel[tap_index], window_at(padded, tap_index,...  17.4 us
    ppermute x5, waiting for transfers between devices, extended(): after = lax.ppermute(initial, axis, down)  14 us
    dot_general x27, matrix products, kernel_grad(): jnp.einsum('orl,crl->oc', grad_field, window_at(padded, tap_index, row_co...  13.5 us
  transfers between devices with their start and end apart: 18, of which 12 were waited for; matrix products, arithmetic and copies ran while one was open for 2% of the time, Pallas kernels for 0%

commit v1 on v0

v1 whole, which is shorter than its diff:
```python
import math

import jax
import jax.numpy as jnp
from jax import lax
from jax.sharding import Mesh, PartitionSpec as P

EPSILON = 1e-06


HALO = 5
LANES = 128
CHUNK_ROWS = 24
TILE = ("ring", "core")


def spread(value, axes, count):
    copies = jnp.broadcast_to(value[None], (count,) + value.shape)
    return lax.all_to_all(copies, axes, 0, 0)


def lat_weights(total_rows):
    position = jnp.arange(total_rows).astype(jnp.float32)
    radians = (-90.0 + 180.0 * (position + 0.5) / total_rows) * (jnp.pi / 180.0)
    cosine = jnp.cos(radians)
    return cosine / jnp.mean(cosine)


def silu_slope(pre_act):
    sigmoid = jax.nn.sigmoid(pre_act)
    return sigmoid * (1.0 + pre_act * (1.0 - sigmoid))


def window_at(padded, tap_index, row_count):
    row_step = tap_index // 3
    col_step = tap_index % 3
    return jnp.roll(padded[:, row_step : row_step + row_count, :], 1 - col_step, axis=2)


def convolve(padded, kernel, row_count):
    summed = None
    for tap_index in range(9):
        product = jnp.einsum(
            "oc,crl->orl",
            kernel[tap_index],
            window_at(padded, tap_index, row_count),
            preferred_element_type=jnp.float32,
        )
        summed = product if summed is None else summed + product
    return summed


def kernel_grad(grad_field, padded, row_count):
    return jnp.stack(
        [
            jnp.einsum(
                "orl,crl->oc",
                grad_field,
                window_at(padded, tap_index, row_count),
                preferred_element_type=jnp.float32,
            )
            for tap_index in range(9)
        ]
    )


def flipped(kernel):
    return jnp.transpose(kernel[::-1], (0, 2, 1))


def pack(fields):
    return jnp.concatenate([field.reshape(-1, field.shape[-1]) for field in fields], 0)


def unpack(packed, shapes):
    fields, start = [], 0
    for channels, rows in shapes:
        part = packed[start : start + channels * rows]
        fields.append(part.reshape(channels, rows, packed.shape[-1]))
        start += channels * rows
    return fields


def widened(fields, tile_count):
    up = [(i, i + 1) for i in range(tile_count - 1)]
    down = [(i + 1, i) for i in range(tile_count - 1)]
    last = pack([field[:, field.shape[1] - width :] for field, width in fields])
    initial = pack([field[:, :width] for field, width in fields])
    shapes = [(field.shape[0], width) for field, width in fields]
    before = unpack(lax.ppermute(last, TILE, up), shapes)
    after = unpack(lax.ppermute(initial, TILE, down), shapes)
    return [
        jnp.concatenate([first, field, second], 1)
        for first, (field, _), second in zip(before, fields, after)
    ]


def total_over_all(flat, member_count, ring_count):
    size = 2 * member_count * CHUNK_ROWS * LANES
    blocks = jnp.pad(flat, (0, size - flat.shape[0]))
    blocks = blocks.reshape(2, member_count, CHUNK_ROWS, LANES)
    core = lax.axis_index("core")
    swap = [(0, 1), (1, 0)]
    mine = jnp.where(core == 0, blocks[0], blocks[1])
    theirs = jnp.where(core == 0, blocks[1], blocks[0])
    mine = mine + lax.ppermute(theirs, "core", swap)
    chunk = jnp.sum(lax.all_to_all(mine, "member", 0, 0), 0)
    chunk = jnp.sum(spread(chunk, "ring", ring_count), 0)
    half = spread(chunk, "member", member_count)
    other = lax.ppermute(half, "core", swap)
    first = jnp.where(core == 0, half, other)
    second = jnp.where(core == 0, other, half)
    return jnp.concatenate([first.reshape(-1), second.reshape(-1)])[: flat.shape[0]]


def per_device(members, condition, observed, kernel_in, kernel_mid, kernel_out):
    member_state = members[0]
    row_count = member_state.shape[1]
    half_vars = member_state.shape[0] // 2
    member_count = lax.axis_size("member")
    ring_count = lax.axis_size("ring")
    tile_count = ring_count * lax.axis_size("core")
    total_rows = row_count * tile_count
    entries = member_state.shape[0] * total_rows * member_state.shape[2]
    base_row = lax.axis_index(TILE) * row_count
    fixed, moving = member_state[:half_vars], member_state[half_vars:]

    def inside(extra):
        rows = base_row - extra + jnp.arange(row_count + 2 * extra)
        return ((rows >= 0) & (rows < total_rows))[None, :, None]

    lat_all = jnp.pad(lat_weights(total_rows), (2, 2))
    lat_wide = lax.dynamic_slice_in_dim(lat_all, base_row, row_count + 4, 0)[None, :, None]
    lat = lat_wide[:, 2:-2]
    fixed_wide, condition_wide, moving_wide, observed_wide = widened(
        [(fixed, HALO), (condition, HALO), (moving, 2), (observed[half_vars:], 2)], tile_count
    )
    inputs = jnp.concatenate([fixed_wide, condition_wide], 0).astype(jnp.bfloat16)
    pre_first = convolve(inputs, kernel_in, row_count + 8)
    hidden_first = jnp.where(inside(4), jax.nn.silu(pre_first), 0.0).astype(jnp.bfloat16)
    pre_second = convolve(hidden_first, kernel_mid, row_count + 6)
    hidden_second = jnp.where(inside(3), jax.nn.silu(pre_second), 0.0).astype(jnp.bfloat16)
    coupling = convolve(hidden_second, kernel_out, row_count + 4)
    log_scale = jnp.tanh(coupling[:half_vars])
    scale = jnp.exp(log_scale)
    moved = moving_wide * scale + coupling[half_vars:]
    pushed = jnp.concatenate([fixed, moved[:, 2:-2]], 0)
    everyone = spread(pack([moved, fixed]), "member", member_count)
    split = half_vars * (row_count + 4)
    lon = member_state.shape[2]
    moved_all = everyone[:, :split].reshape(member_count, half_vars, row_count + 4, lon)
    fixed_all = everyone[:, split:].reshape(member_count, half_vars, row_count, lon)
    from_moved = jnp.sum(lat * (moved[None, :, 2:-2] - moved_all[:, :, 2:-2]) ** 2, (1, 2, 3))
    from_fixed = jnp.sum(lat * (fixed[None] - fixed_all) ** 2, (1, 2, 3))
    to_observed = jnp.sum(lat * (pushed - observed) ** 2)
    partials = jnp.concatenate([from_moved + from_fixed, to_observed[None]])
    partials = jnp.pad(partials[None], ((0, 7), (0, LANES - partials.shape[0])))
    totals = jnp.sum(spread(partials, TILE, tile_count), 0)[0]
    distances = jnp.sqrt(totals / entries + EPSILON)
    to_others = distances[:member_count]
    is_other = jnp.arange(member_count) != lax.axis_index("member")
    energy_share = distances[member_count] / member_count
    energy_share = energy_share - jnp.sum(jnp.where(is_other, to_others, 0.0)) / (
        2.0 * member_count * member_count
    )
    weights = jnp.where(is_other, 1.0 / (member_count * member_count * to_others), 0.0)
    inner = (moved - observed_wide) / (member_count * distances[member_count])
    inner = inner - jnp.sum(weights[:, None, None, None] * (moved[None] - moved_all), 0)
    upper_grad = lat_wide * inner / math.sqrt(entries)
    grad_scale = upper_grad * moving_wide * scale * (1.0 - log_scale * log_scale)
    grad_coupling = jnp.concatenate([grad_scale, upper_grad], 0).astype(jnp.bfloat16)
    grad_last = kernel_grad(grad_coupling[:, 2:-2], hidden_second[:, 2:-2], row_count)
    back_second = convolve(grad_coupling, flipped(kernel_out), row_count + 2)
    grad_pre_second = back_second * silu_slope(pre_second[:, 2:-2])
    grad_pre_second = jnp.where(inside(1), grad_pre_second, 0.0).astype(jnp.bfloat16)
    grad_middle = kernel_grad(grad_pre_second[:, 1:-1], hidden_first[:, 3:-3], row_count)
    back_first = convolve(grad_pre_second, flipped(kernel_mid), row_count)
    grad_pre_first = (back_first * silu_slope(pre_first[:, 4:-4])).astype(jnp.bfloat16)
    grad_first = kernel_grad(grad_pre_first, inputs[:, 4:-4], row_count)
    parts = [grad_first, grad_middle, grad_last, energy_share[None] / tile_count]
    summed = total_over_all(
        jnp.concatenate([part.reshape(-1) for part in parts]), member_count, ring_count
    )
    results, start = [], 0
    for part in parts:
        results.append(summed[start : start + part.size].reshape(part.shape))
        start += part.size
    grad_first, grad_middle, grad_last, energy = results
    return (pushed[None], energy[0], grad_first, grad_middle, grad_last)


def solution(mesh):
    sizes = (mesh.shape["member"], mesh.shape["tile"] // 2, 2)
    fine = Mesh(mesh.devices.reshape(sizes), ("member",) + TILE)
    in_specs = (
        P("member", None, TILE, None),
        P(None, TILE, None),
        P(None, TILE, None),
        P(),
        P(),
        P(),
    )
    out_specs = (P("member", None, TILE, None), P(), P(), P(), P())
    return jax.shard_map(
        per_device, mesh=fine, in_specs=in_specs, out_specs=out_specs, check_vma=False
    )
```

time: 488 us -> 182 us (0.37)
  waiting for transfers between devices: 206 us -> 15.8 us
  blocking collectives: 171 us -> 28.4 us
  local copies, waits for them, and re-layouts: 11 us -> 41.5 us
  between operations: 21.2 us -> 4.48 us
  matrix products: 30.9 us -> 46.9 us
    psum x3 -> x0, blocking collectives: 171 us -> none  [the longest x1 86.6 us: per_device(): lax.psum((grad_first, grad_middle, grad_last), ('member', 'tile'))]
    psum x1 -> x0, waiting for transfers between devices: 153 us -> none  [per_device(): lax.psum((grad_first, grad_middle, grad_last), ('member', 'tile'))]
    ppermute x17 -> x4, waiting for transfers between devices: 52.8 us -> 2.1 us  [the longest x1 1.07 us: total_over_all(): mine = mine + lax.ppermute(theirs, 'core', swap)]
    all_to_all x0 -> x3, blocking collectives: none -> 28.4 us  [the longest x2 20.9 us: spread(): return lax.all_to_all(copies, axes, 0, 0)]
    ppermute x17 -> x4, starting transfers between devices: 35.1 us -> 13 us  [the longest x1 6.21 us: widened(): before = unpack(lax.ppermute(last, TILE, up), shapes)]
    all_to_all x0 -> x2, starting transfers between devices: none -> 18.3 us  [spread(): return lax.all_to_all(copies, axes, 0, 0)]
    slice x3 -> x14, local copies, waits for them, and re-layouts: 0.3 us -> 17.2 us  [window_at(): jnp.roll(padded[:, row_step:row_step + row_count, :], 1 - col_step, axis=2)]
    all_to_all x0 -> x2, waiting for transfers between devices: none -> 13.7 us  [spread(): return lax.all_to_all(copies, axes, 0, 0)]
  transfers between devices with their start and end apart: 18 -> 6, of which waited for: 12 -> 5; matrix products, arithmetic and copies ran while one was open for 2% -> 9% of each run, Pallas kernels for 0% -> 0%
where the time goes in v1:
time: 182 us; the launch traced here: 180 us
  matrix products  46.9 us (26%)
  local copies, waits for them, and re-layouts  41.5 us (23%)
  starting transfers between devices  31.4 us (17%)
  blocking collectives  28.4 us (16%)
  waiting for transfers between devices  15.8 us (9%)
  other arithmetic  11.8 us (6%)
  between operations  4.48 us (2%)
    dot_general x45, matrix products, convolve(): jnp.einsum('oc,crl->orl', kernel[tap_index], window_at(padded, tap_index,...  30.8 us
    all_to_all x2, blocking collectives, spread(): return lax.all_to_all(copies, axes, 0, 0)  20.9 us
    all_to_all x2, starting transfers between devices, spread(): return lax.all_to_all(copies, axes, 0, 0)  18.3 us
    slice x14, local copies, waits for them, and re-layouts, window_at(): jnp.roll(padded[:, row_step:row_step + row_count, :], 1 - col_step, axis=2)  17.2 us
    dot_general x27, matrix products, kernel_grad(): jnp.einsum('orl,crl->oc', grad_field, window_at(padded, tap_index, row_co...  16.1 us
    all_to_all x2, waiting for transfers between devices, spread(): return lax.all_to_all(copies, axes, 0, 0)  13.7 us
    all_to_all x1, blocking collectives, total_over_all(): chunk = jnp.sum(lax.all_to_all(mine, 'member', 0, 0), 0)  7.54 us
    ppermute x1, starting transfers between devices, widened(): before = unpack(lax.ppermute(last, TILE, up), shapes)  6.21 us
  transfers between devices with their start and end apart: 6, of which 5 were waited for; matrix products, arithmetic and copies ran while one was open for 9% of the time, Pallas kernels for 0%

profile of v1, /device:TPU:1, one launch (start us, length us, event | category | flops | bytes accessed | tf_op | source)
XLA Modules:
  0.0 180.3 jit_solution(1661579323931307169)
XLA Ops:
  3.6 6.2 %collective-permute-start = (f32[57,512]{1,0:T(8,128)S(1)}, f32[57,512]{1,0:T(8,128)S(1)}, u32[]{:S(2)}, u32[]{:S(2)}) collective-permute-start(f32[57,512]{1,0:T(8,128)S(1)} %pad_maximum_fusion.7), channel_id=1, source_target_pairs={{0,1},{1,2},{2,3},{3,4},{4,5},{5,6},{6,7},{7,8},{8,9},{9,10},{10,1... | collective-permute-start | bytes 350216 | tf_op jit(solution)/shard_map/ppermute | solution.py:90
  9.9 1.9 %collective-permute-start.1 = (f32[57,512]{1,0:T(8,128)S(1)}, f32[57,512]{1,0:T(8,128)S(1)}, u32[]{:S(2)}, u32[]{:S(2)}) collective-permute-start(f32[57,512]{1,0:T(8,128)S(1)} %pad_maximum_fusion.8), channel_id=1, source_target_pairs={{1,0},{2,1},{3,2},{4,3},{5,4},{6,5},{7,6},{8,7},{9,8},{10,9},{11,1... | collective-permute-start | bytes 350216 | tf_op jit(solution)/shard_map/ppermute | solution.py:91
  22.9 3.8 %select_convert_fusion = (bf16[64,16,512]{2,0,1:T(8,128)(2,1)S(1)}, f32[64,16,512]{2,0,1:T(8,128)}) fusion(pred[16]{0:T(512)(128)(4,1)S(1)} %compare_and_fusion.1, bf16[9,64,9]{1,2,0:T(8,128)(2,1)S(1)} %copy-done.63, bf16[9,16,512]{2,1,0:T(8,128)(2,1)S(1)} %get-tuple-element.169, f32[16,512,64]{1,2,0:T(8,128)S(1)} %fusion.158, ...), kind=kOutput, calls=%fused_computation.1 | convolution fusion | flops 16777216 | bytes 20075008 | tf_op jit(solution)/shard_map/oc,crl->orl/dot_general | solution.py:43
  26.7 1.2 fusion.319
  31.8 2.7 %select_convert_fusion.1 = (bf16[64,14,512]{2,0,1:T(8,128)(2,1)S(1)}, f32[64,14,512]{2,0,1:T(8,128)}) fusion(pred[14]{0:T(512)(128)(4,1)S(1)} %compare_and_fusion.2, bf16[64,14,1]{2,0,1:T(8,128)(2,1)S(1)} %get-tuple-element.50, bf16[64,14,511]{2,0,1:T(8,128)(2,1)S(1)} %get-tuple-element.44, bf16[9,64,64]{2,1,0:T(8,128)(2,1)S(1)} %copy-done.11, ...), kind=kOutput, calls=%fused_computation.3 | convolution fusion | flops 66977792 | bytes 18596352 | tf_op jit(solution)/shard_map/oc,crl->orl/dot_general | solution.py:43
  34.6 2.7 %fusion.324 = (bf16[64,12,511]{2,0,1:T(8,128)(2,1)}, bf16[64,12,511]{2,0,1:T(8,128)(2,1)S(1)}, bf16[64,12,511]{2,0,1:T(8,128)(2,1)}, bf16[64,12,511]{2,0,1:T(8,1...) fusion(bf16[64,14,512]{2,0,1:T(8,128)(2,1)S(1)} %get-tuple-element.162), kind=kLoop, calls=%fused_computation.481 | loop fusion | bytes 9418752 | tf_op jit(solution)/shard_map/jit(_roll_static)/slice | solution.py:37
  37.3 1.3 fusion.323
  39.9 1.4 fusion.333
  41.4 1.4 fusion.334
  43.6 1.8 %fusion.63 = f32[12,512,6]{1,2,0:T(8,128)S(1)} fusion(bf16[64,12,511]{2,0,1:T(8,128)(2,1)} %get-tuple-element.74, bf16[64,12,1]{2,0,1:T(8,128)(2,1)} %get-tuple-element.68, bf16[9,6,64]{2,1,0:T(8,128)(2,1)} %param.11), kind=kOutput, calls=%fused_computation.110 | convolution fusion | flops 6291456 | bytes 1132544 | tf_op jit(solution)/shard_map/oc,crl->orl/dot_general | solution.py:43
  45.4 1.5 fusion.67
  46.9 1.2 fusion.71
  49.1 1.2 fusion.79
  54.7 1.1 broadcast_in_dim.94
  55.8 4.2 %all-to-all-start = ((f32[8,60,512]{2,1,0:T(8,128)}), f32[8,60,512]{2,1,0:T(8,128)}, u32[]{:S(2)}, u32[]{:S(2)}) async-start(f32[8,60,512]{2,1,0:T(8,128)} %broadcast_in_dim.94), calls=%async_computation | async-start | bytes 2097152 | tf_op jit(solution)/shard_map/all_to_all | solution.py:19
  60.0 1.2 multiply_reduce_fusion.1
  63.5 2.3 %fusion.321 = (bf16[64,8,511]{2,0,1:T(8,128)(2,1)}, bf16[64,8,511]{2,0,1:T(8,128)(2,1)}, bf16[64,8,511]{2,0,1:T(8,128)(2,1)}, bf16[64,8,511]{2,0,1:T(8,128)(2,1)...) fusion(bf16[64,14,512]{2,0,1:T(8,128)(2,1)S(1)} %get-tuple-element.162), kind=kLoop, calls=%fused_computation.478 | loop fusion | bytes 6279168 | tf_op jit(solution)/shard_map/jit(_roll_static)/slice | solution.py:37
  65.8 2.2 %fusion.317 = (bf16[64,8,511]{2,0,1:T(8,128)(2,1)}, bf16[64,8,511]{2,0,1:T(8,128)(2,1)}, bf16[64,8,511]{2,0,1:T(8,128)(2,1)}, bf16[64,8,511]{2,0,1:T(8,128)(2,1)...) fusion(bf16[64,16,512]{2,0,1:T(8,128)(2,1)S(1)} %get-tuple-element.160), kind=kLoop, calls=%fused_computation.474 | loop fusion | bytes 6279168 | tf_op jit(solution)/shard_map/jit(_roll_static)/slice | solution.py:37
  68.0 6.0 %all-to-all-done = f32[8,60,512]{2,1,0:T(8,128)} async-done(((f32[8,60,512]{2,1,0:T(8,128)}), f32[8,60,512]{2,1,0:T(8,128)}, u32[]{:S(2)}, u32[]{:S(2)}) %all-to-all-start) | async-done | bytes 983072 | tf_op jit(solution)/shard_map/all_to_all | solution.py:19
  74.0 1.1 slice.1094
  75.8 1.3 fusion.153
  78.5 14.1 %all-to-all-start.1 = ((f32[32,8,128]{2,1,0:T(8,128)}), f32[32,8,128]{2,1,0:T(8,128)S(1)}, u32[]{:S(2)}, u32[]{:S(2)}) async-start(f32[32,8,128]{2,1,0:T(8,128)} %broadcast_in_dim.97), calls=%async_computation.1 | async-start | bytes 262144 | tf_op jit(solution)/shard_map/all_to_all | solution.py:19
  92.6 1.6 pad_maximum_fusion.23
  95.4 7.8 %all-to-all-done.1 = f32[32,8,128]{2,1,0:T(8,128)S(1)} async-done(((f32[32,8,128]{2,1,0:T(8,128)}), f32[32,8,128]{2,1,0:T(8,128)S(1)}, u32[]{:S(2)}, u32[]{:S(2)}) %all-to-all-start.1) | async-done | bytes 131104 | tf_op jit(solution)/shard_map/all_to_all | solution.py:19
  111.9 2.1 %fusion.325 = (bf16[64,8,511]{2,0,1:T(8,128)(2,1)}, bf16[64,8,511]{2,0,1:T(8,128)(2,1)}, bf16[64,8,511]{2,0,1:T(8,128)(2,1)}, bf16[64,8,511]{2,0,1:T(8,128)(2,1)...) fusion(bf16[64,10,512]{2,0,1:T(8,128)(2,1)S(1)} %fusion.5), kind=kLoop, calls=%fused_computation.482 | loop fusion | bytes 6279168 | tf_op jit(solution)/shard_map/jit(_roll_static)/slice | solution.py:37
  118.7 2.1 %fusion.15 = f32[9,64,64]{2,1,0:T(8,128)} fusion(bf16[64,10,512]{2,0,1:T(8,128)(2,1)S(1)} %fusion.5, bf16[64,8,511]{2,0,1:T(8,128)(2,1)} %get-tuple-element.37, bf16[64,8,1]{2,0,1:T(8,128)(2,1)} %get-tuple-element.43), kind=kOutput, calls=%fused_computation.44 | convolution fusion | flops 34603008 | bytes 1212416 | tf_op jit(solution)/shard_map/orl,crl->oc/dot_general | solution.py:56
  121.8 2.1 %fusion.13 = f32[9,64,64]{2,1,0:T(8,128)} fusion(f32[9,64,64]{2,1,0:T(8,128)} %fusion.14, bf16[64,10,512]{2,0,1:T(8,128)(2,1)S(1)} %fusion.5, bf16[64,8,1]{2,0,1:T(8,128)(2,1)S(1)} %copy-done.56, bf16[64,8,511]{2,0,1:T(8,128)(2,1)} %get-tuple-element.36), kind=kOutput, calls=%fused_computation.40 | convolution fusion | flops 34603008 | bytes 1213440 | tf_op jit(solution)/shard_map/orl,crl->oc/dot_general | solution.py:56
  136.4 1.3 fusion.6
  143.0 7.5 %all_to_all.25 = f32[8,24,128]{2,1,0:T(8,128)S(1)} all-to-all(f32[8,24,128]{2,1,0:T(8,128)S(1)} %add.314), channel_id=1, replica_groups=mesh['member'=8,'ring'=16,'core'=2] {'member'}, dimensions={0} | all-to-all | bytes 196608 | tf_op jit(solution)/shard_map/all_to_all | solution.py:107
  150.5 13.3 %all_to_all.26 = f32[16,24,128]{2,1,0:T(8,128)S(1)} all-to-all(f32[16,24,128]{2,1,0:T(8,128)S(1)} %broadcast_in_dim.100), channel_id=1, replica_groups=mesh['member'=8,'ring'=16,'core'=2] {'ring'}, dimensions={0} | all-to-all | bytes 393216 | tf_op jit(solution)/shard_map/all_to_all | solution.py:19
  163.9 7.6 %all_to_all.27 = f32[8,24,128]{2,1,0:T(8,128)S(1)} all-to-all(f32[8,24,128]{2,1,0:T(8,128)S(1)} %broadcast_in_dim.101), channel_id=1, replica_groups=mesh['member'=8,'ring'=16,'core'=2] {'member'}, dimensions={0} | all-to-all | bytes 196608 | tf_op jit(solution)/shard_map/all_to_all | solution.py:19
  171.5 4.6 %collective-permute-start.3 = (f32[8,24,128]{2,1,0:T(8,128)S(1)}, f32[8,24,128]{2,1,0:T(8,128)S(1)}, u32[]{:S(2)}, u32[]{:S(2)}) collective-permute-start(f32[8,24,128]{2,1,0:T(8,128)S(1)} %all_to_all.27), channel_id=1, source_target_pairs={{0,1},{1,0},{2,3},{3,2},{4,5},{5,4},{6,7},{7,6},{8,9},{9,8},{10,11... | collective-permute-start | bytes 294920 | tf_op jit(solution)/shard_map/ppermute | solution.py:110
  (315 shorter events, 63.9 us)
Async XLA Ops:
  0.6 15.4 %copy-start.6 = (f32[6,8,512]{2,1,0:T(8,128)S(1)}, f32[6,8,512]{2,1,0:T(8,128)}, u32[]{:S(2)}) copy-start(f32[6,8,512]{2,1,0:T(8,128)} %param.7) | copy-start | bytes 294916
  0.6 14.2 %copy-start.64 = (bf16[9,6,64]{2,1,0:T(8,128)(2,1)S(1)}, bf16[9,6,64]{2,1,0:T(8,128)(2,1)}, u32[]{:S(2)}) copy-start(bf16[9,6,64]{2,1,0:T(8,128)(2,1)} %param.11) | copy-start | bytes 20740
  0.7 16.1 %copy-start.11 = (bf16[9,64,64]{2,1,0:T(8,128)(2,1)S(1)}, bf16[9,64,64]{2,1,0:T(8,128)(2,1)}, u32[]{:S(2)}) copy-start(bf16[9,64,64]{2,1,0:T(8,128)(2,1)} %param.10) | copy-start | bytes 221188
  1.5 53.1 %copy-start.36 = (f32[24,512]{1,0:T(8,128)}, f32[24,512]{1,0:T(8,128)S(1)}, u32[]{:S(2)}) copy-start(f32[24,512]{1,0:T(8,128)S(1)} %get-tuple-element.147) | copy-start | bytes 147460
  3.6 14.0 %collective-permute-start = (f32[57,512]{1,0:T(8,128)S(1)}, f32[57,512]{1,0:T(8,128)S(1)}, u32[]{:S(2)}, u32[]{:S(2)}) collective-permute-start(f32[57,512]{1,0:T(8,128)S(1)} %pad_maximum_fusion.7), channel_id=1, source_target_pairs={{0,1},{1,2},{2,3},{3,4},{4,5},{5,6},{6,7},{7,8},{8,9},{9,10},{10,1... | collective-permute-start | bytes 350216 | tf_op jit(solution)/shard_map/ppermute | solution.py:90
  9.9 7.8 %collective-permute-start.1 = (f32[57,512]{1,0:T(8,128)S(1)}, f32[57,512]{1,0:T(8,128)S(1)}, u32[]{:S(2)}, u32[]{:S(2)}) collective-permute-start(f32[57,512]{1,0:T(8,128)S(1)} %pad_maximum_fusion.8), channel_id=1, source_target_pairs={{1,0},{2,1},{3,2},{4,3},{5,4},{6,5},{7,6},{8,7},{9,8},{10,9},{11,1... | collective-permute-start | bytes 350216 | tf_op jit(solution)/shard_map/ppermute | solution.py:91
  43.5 8.4 %copy-start.58 = (f32[3,2,512]{2,1,0:T(2,128)}, f32[3,2,512]{2,1,0:T(2,128)S(1)}, u32[]{:S(2)}) copy-start(f32[3,2,512]{2,1,0:T(2,128)S(1)} %reshape.181) | copy-start | bytes 36868
  43.5 3.4 %copy-start.9 = (bf16[64,12,511]{2,0,1:T(8,128)(2,1)S(1)}, bf16[64,12,511]{2,0,1:T(8,128)(2,1)}, u32[]{:S(2)}) copy-start(bf16[64,12,511]{2,0,1:T(8,128)(2,1)} %get-tuple-element.78) | copy-start | bytes 2354692
  43.6 4.6 %copy-start.8 = (bf16[64,12,511]{2,0,1:T(8,128)(2,1)S(1)}, bf16[64,12,511]{2,0,1:T(8,128)(2,1)}, u32[]{:S(2)}) copy-start(bf16[64,12,511]{2,0,1:T(8,128)(2,1)} %get-tuple-element.77) | copy-start | bytes 2354692
  43.6 4.6 %copy-start.44 = (bf16[64,12,1]{2,0,1:T(8,128)(2,1)S(1)}, bf16[64,12,1]{2,0,1:T(8,128)(2,1)}, u32[]{:S(2)}) copy-start(bf16[64,12,1]{2,0,1:T(8,128)(2,1)} %get-tuple-element.71) | copy-start | bytes 4612
  45.4 3.7 %copy-start.7 = (bf16[64,12,511]{2,0,1:T(8,128)(2,1)S(1)}, bf16[64,12,511]{2,0,1:T(8,128)(2,1)}, u32[]{:S(2)}) copy-start(bf16[64,12,511]{2,0,1:T(8,128)(2,1)} %get-tuple-element.76) | copy-start | bytes 2354692
  45.4 3.7 %copy-start.43 = (bf16[64,12,1]{2,0,1:T(8,128)(2,1)S(1)}, bf16[64,12,1]{2,0,1:T(8,128)(2,1)}, u32[]{:S(2)}) copy-start(bf16[64,12,1]{2,0,1:T(8,128)(2,1)} %get-tuple-element.70) | copy-start | bytes 4612
  53.9 6.1 %copy-start.38 = (f32[6,8,512]{2,1,0:T(8,128)S(1)}, f32[6,8,512]{2,1,0:T(8,128)}, u32[]{:S(2)}) copy-start(f32[6,8,512]{2,1,0:T(8,128)} %param.8) | copy-start | bytes 294916
  55.8 18.2 %all-to-all-start = ((f32[8,60,512]{2,1,0:T(8,128)}), f32[8,60,512]{2,1,0:T(8,128)}, u32[]{:S(2)}, u32[]{:S(2)}) async-start(f32[8,60,512]{2,1,0:T(8,128)} %broadcast_in_dim.94), calls=%async_computation | async-start | bytes 2097152 | tf_op jit(solution)/shard_map/all_to_all | solution.py:19
  68.0 7.8 %copy-start.37 = (f32[24,512]{1,0:T(8,128)S(1)}, f32[24,512]{1,0:T(8,128)}, u32[]{:S(2)}) copy-start(f32[24,512]{1,0:T(8,128)} %copy-done.36) | copy-start | bytes 147460
  68.0 7.8 %copy-start.65 = (f32[24]{0:T(128)S(1)}, f32[24]{0:T(128)}, u32[]{:S(2)}) copy-start(f32[24]{0:T(128)} %mul.127) | copy-start | bytes 292
  68.0 24.6 %copy-start.39 = (bf16[9,8,511]{2,1,0:T(8,128)(2,1)S(1)}, bf16[9,8,511]{2,1,0:T(8,128)(2,1)}, u32[]{:S(2)}) copy-start(bf16[9,8,511]{2,1,0:T(8,128)(2,1)} %get-tuple-element.94) | copy-start | bytes 220756
  68.0 26.3 %copy-start.61 = (f32[6,512]{1,0:T(8,128)S(1)}, f32[6,512]{1,0:T(8,128)}, u32[]{:S(2)}) copy-start(f32[6,512]{1,0:T(8,128)} %get-tuple-element.126) | copy-start | bytes 36868
  68.0 26.3 %copy-start.62 = (f32[6,512]{1,0:T(8,128)S(1)}, f32[6,512]{1,0:T(8,128)}, u32[]{:S(2)}) copy-start(f32[6,512]{1,0:T(8,128)} %get-tuple-element.128) | copy-start | bytes 36868
  77.1 28.5 %slice-start = ((f32[6,8,512]{2,1,0:T(8,128)}), f32[3,8,512]{2,1,0:T(8,128)S(1)}, s32[]{:S(2)}) async-start(f32[6,8,512]{2,1,0:T(8,128)} %param.8), calls=%async_computation.5 | async-start | bytes 98304 | tf_op jit(solution)/shard_map/slice | solution.py:136
  77.1 28.5 %copy-start.66 = (f32[12]{0:T(128)S(1)}, f32[12]{0:T(128)}, u32[]{:S(2)}) copy-start(f32[12]{0:T(128)} %pad_dynamic-slice_fusion) | copy-start | bytes 148
  78.5 24.7 %all-to-all-start.1 = ((f32[32,8,128]{2,1,0:T(8,128)}), f32[32,8,128]{2,1,0:T(8,128)S(1)}, u32[]{:S(2)}, u32[]{:S(2)}) async-start(f32[32,8,128]{2,1,0:T(8,128)} %broadcast_in_dim.97), calls=%async_computation.1 | async-start | bytes 262144 | tf_op jit(solution)/shard_map/all_to_all | solution.py:19
  92.6 13.1 %copy-start.59 = (f32[3,2,512]{2,1,0:T(2,128)S(1)}, f32[3,2,512]{2,1,0:T(2,128)}, u32[]{:S(2)}) copy-start(f32[3,2,512]{2,1,0:T(2,128)} %copy-done.58) | copy-start | bytes 36868
  111.9 3.8 %copy-start.29 = (bf16[64,8,511]{2,0,1:T(8,128)(2,1)S(1)}, bf16[64,8,511]{2,0,1:T(8,128)(2,1)}, u32[]{:S(2)}) copy-start(bf16[64,8,511]{2,0,1:T(8,128)(2,1)} %get-tuple-element.61) | copy-start | bytes 1569796
  111.9 3.8 %copy-start.51 = (bf16[64,8,1]{2,0,1:T(8,128)(2,1)S(1)}, bf16[64,8,1]{2,0,1:T(8,128)(2,1)}, u32[]{:S(2)}) copy-start(bf16[64,8,1]{2,0,1:T(8,128)(2,1)} %get-tuple-element.67) | copy-start | bytes 3076
  118.3 3.4 %copy-start.56 = (bf16[64,8,1]{2,0,1:T(8,128)(2,1)S(1)}, bf16[64,8,1]{2,0,1:T(8,128)(2,1)}, u32[]{:S(2)}) copy-start(bf16[64,8,1]{2,0,1:T(8,128)(2,1)} %get-tuple-element.42) | copy-start | bytes 3076
  118.7 5.1 %copy-start.23 = (bf16[64,8,511]{2,0,1:T(8,128)(2,1)S(1)}, bf16[64,8,511]{2,0,1:T(8,128)(2,1)}, u32[]{:S(2)}) copy-start(bf16[64,8,511]{2,0,1:T(8,128)(2,1)} %get-tuple-element.35) | copy-start | bytes 1569796
  118.7 5.1 %copy-start.55 = (bf16[64,8,1]{2,0,1:T(8,128)(2,1)S(1)}, bf16[64,8,1]{2,0,1:T(8,128)(2,1)}, u32[]{:S(2)}) copy-start(bf16[64,8,1]{2,0,1:T(8,128)(2,1)} %get-tuple-element.41) | copy-start | bytes 3076
  121.8 4.0 %copy-start.22 = (bf16[64,8,511]{2,0,1:T(8,128)(2,1)S(1)}, bf16[64,8,511]{2,0,1:T(8,128)(2,1)}, u32[]{:S(2)}) copy-start(bf16[64,8,511]{2,0,1:T(8,128)(2,1)} %get-tuple-element.34) | copy-start | bytes 1569796
  121.8 4.0 %copy-start.54 = (bf16[64,8,1]{2,0,1:T(8,128)(2,1)S(1)}, bf16[64,8,1]{2,0,1:T(8,128)(2,1)}, u32[]{:S(2)}) copy-start(bf16[64,8,1]{2,0,1:T(8,128)(2,1)} %get-tuple-element.40) | copy-start | bytes 3076
  141.6 1.4 collective-permute-start.2
  171.5 5.5 %collective-permute-start.3 = (f32[8,24,128]{2,1,0:T(8,128)S(1)}, f32[8,24,128]{2,1,0:T(8,128)S(1)}, u32[]{:S(2)}, u32[]{:S(2)}) collective-permute-start(f32[8,24,128]{2,1,0:T(8,128)S(1)} %all_to_all.27), channel_id=1, source_target_pairs={{0,1},{1,0},{2,3},{3,2},{4,5},{5,4},{6,7},{7,6},{8,9},{9,8},{10,11... | collective-permute-start | bytes 294920 | tf_op jit(solution)/shard_map/ppermute | solution.py:110
  (43 other events, 77.4 us)

commit v2 on v0

v2 whole, which is shorter than its diff:
```python
import functools
import math

import jax
import jax.numpy as jnp
import numpy as np
from jax import lax
from jax.experimental import pallas as pl
from jax.experimental.pallas import tpu as pltpu
from jax.sharding import Mesh, PartitionSpec as P

EPSILON = 1e-06
MEMBERS, NLAT, LON, ROWS = 8, 256, 512, 8
VARS, HALF, COND, CH = 6, 3, 6, 64
TILES, RING = 32, 16
ENTRIES = VARS * NLAT * LON
HALO = 5
FIELDS = 16
INPUTS = HALF + COND
WIDE = (ROWS + 4) * HALF
FIXED_AT = 40
CHUNK = 24
TILE = ("ring", "core")
F32, BF16 = jnp.float32, jnp.bfloat16


def spread(value, axes, count):
    copies = jnp.broadcast_to(value[None], (count,) + value.shape)
    return lax.all_to_all(copies, axes, 0, 0)


def lat_table():
    rows = np.arange(NLAT)
    cosine = np.cos((-90.0 + 180.0 * (rows + 0.5) / NLAT) * (np.pi / 180.0))
    lat = (cosine / cosine.mean()).astype(np.float32)
    padded = np.pad(lat, (2, 2))
    table = np.zeros((TILES, FIXED_AT + ROWS), np.float32)
    for tile in range(TILES):
        wide = padded[tile * ROWS : tile * ROWS + ROWS + 4]
        table[tile, :WIDE] = np.repeat(wide, HALF)
        table[tile, FIXED_AT:] = lat[tile * ROWS : (tile + 1) * ROWS]
    return table


def turned(value, step):
    return value if step == 0 else pltpu.roll(value, step % LON, 1)


def dot(left, right):
    return jnp.dot(left, right, preferred_element_type=F32)


def dot_cells(left, right):
    return lax.dot_general(left, right, (((1,), (1,)), ((), ())), preferred_element_type=F32)


def inside(base, row):
    row = base + row
    return jnp.where((row >= 0) & (row < NLAT), 1.0, 0.0).astype(F32)


def sigmoid(value):
    return 0.5 * jnp.tanh(0.5 * value) + 0.5


def loop(start, stop, body):
    lax.fori_loop(start, stop, lambda row, carry: (body(row), carry)[1], 0, unroll=2)


def forward_kernel(
    place, before, own, after, members, w_in, w_mid, w_out,
    send, pushed, kept, stack, hidden_1, slope_1, hidden_2, slope_2,
):
    base = place[1]
    for row in range(ROWS + 2 * HALO):
        if row < HALO:
            field = before[row]
        elif row < HALO + ROWS:
            field = own[row - HALO]
        else:
            field = after[row - HALO - ROWS]
        for shift in range(3):
            part = turned(field, 1 - shift).astype(BF16)
            stack[row, shift * FIELDS : (shift + 1) * FIELDS, :] = part

    def first(row, keep):
        pre = dot(w_in[...], stack[pl.ds(row, 3)].reshape(9 * FIELDS, LON))
        gate = sigmoid(pre)
        hidden_1[row] = (pre * gate * inside(base, row - 4)).astype(BF16)
        if keep:
            slope_1[row - 4] = gate * (1.0 + pre * (1.0 - gate))

    loop(0, 4, functools.partial(first, keep=False))
    loop(4, 12, functools.partial(first, keep=True))
    loop(12, 16, functools.partial(first, keep=False))

    def second(row, keep):
        part = dot(w_mid[...], hidden_1[pl.ds(row, 3)].reshape(3 * CH, LON))
        pre = turned(part[:CH], 1) + part[CH : 2 * CH] + turned(part[2 * CH :], -1)
        gate = sigmoid(pre)
        hidden_2[row] = (pre * gate * inside(base, row - 3)).astype(BF16)
        if keep:
            slope_2[row - 2] = gate * (1.0 + pre * (1.0 - gate))

    loop(0, 2, functools.partial(second, keep=False))
    loop(2, 12, functools.partial(second, keep=True))
    loop(12, 14, functools.partial(second, keep=False))

    for row in range(ROWS + 4):
        part = dot(w_out[...], hidden_2[row : row + 3].reshape(3 * CH, LON))
        both = turned(part[:16], 1) + part[16:32] + turned(part[32:], -1)
        log_scale = jnp.tanh(both[:HALF])
        if row < 2:
            field = before[row + 3]
        elif row < 2 + ROWS:
            field = own[row - 2]
        else:
            field = after[row - 2 - ROWS]
        moving = field[INPUTS : INPUTS + HALF]
        moved = moving * jnp.exp(log_scale) + both[8 : 8 + HALF]
        here = slice(row * HALF, (row + 1) * HALF)
        kept[0, here, :] = log_scale
        kept[1, here, :] = moving
        kept[2, here, :] = field[INPUTS + HALF : INPUTS + 2 * HALF]
        send[0, here, :] = moved
        if 2 <= row < 2 + ROWS:
            for var in range(HALF):
                pushed[HALF + var, row - 2 : row - 1, :] = moved[var : var + 1]
    pushed[:HALF] = members[:HALF]
    send[0, WIDE:FIXED_AT, :] = jnp.zeros((FIXED_AT - WIDE, LON), F32)
    send[0, FIXED_AT:, :] = members[:HALF].reshape(HALF * ROWS, LON)
    whole = send[0]
    for copy in range(1, MEMBERS):
        send[copy] = whole


def folded(value):
    return sum(value[..., at : at + 128] for at in range(0, LON, 128))


def distance_kernel(place, lat, fields, kept, observed, partials):
    me = place[0]
    spot = lax.broadcasted_iota(jnp.int32, (WIDE, 1), 0)
    wide = jnp.where((spot >= 2 * HALF) & (spot < WIDE - 2 * HALF), lat[:WIDE, :1], 0.0)
    low = jnp.concatenate([lat[FIXED_AT:, :1]] * HALF, 0)
    mine = fields[me]

    def weighed(moved, fixed):
        upper = jnp.sum(folded(wide * (mine[:WIDE] - moved) ** 2), 0, keepdims=True)
        lower = jnp.sum(folded(low * (mine[FIXED_AT:] - fixed) ** 2), 0, keepdims=True)
        return upper + lower

    rows = [weighed(fields[n, :WIDE], fields[n, FIXED_AT:]) for n in range(MEMBERS)]
    to_observed = weighed(kept[2], observed[:HALF].reshape(HALF * ROWS, LON))
    all_rows = jnp.concatenate(rows, 0)
    spot = lax.broadcasted_iota(jnp.int32, (MEMBERS, 128), 0)
    all_rows = jnp.where(spot == me, to_observed, all_rows)
    for tile in range(TILES):
        partials[tile] = all_rows


def backward_kernel(
    place, lat, totals, fields, kept, stack, hidden_1, slope_1, hidden_2, slope_2, w_back_2, w_back_1,
    mine, theirs, coupled, turned_2, sum_out, sum_mid, sum_in, packed,
):
    me, base, core = place[0], place[1], place[2]
    total = totals[0]
    for tile in range(1, TILES):
        total = total + totals[tile]
    distances = jnp.sqrt(jnp.sum(total, 1, keepdims=True) / ENTRIES + EPSILON)
    is_me = lax.broadcasted_iota(jnp.int32, (MEMBERS, 1), 0) == me
    shares = jnp.where(is_me, distances / MEMBERS, -distances / (2.0 * MEMBERS * MEMBERS))
    share = jnp.sum(shares, 0, keepdims=True) / TILES
    weights = 1.0 / (jnp.where(is_me, MEMBERS, MEMBERS * MEMBERS) * distances)
    own_weight = jnp.sum(jnp.where(is_me, weights, 0.0), 0, keepdims=True)
    weights = jnp.where(is_me, 0.0, weights)
    log_scale, moving, observed = kept[0], kept[1], kept[2]
    moved = fields[me, :WIDE]
    inner = (moved - observed) * own_weight
    for n in range(MEMBERS):
        inner = inner - weights[n : n + 1] * (moved - fields[n, :WIDE])
    upper = lat[:WIDE, :1] * inner / math.sqrt(ENTRIES)
    scaled = upper * moving * jnp.exp(log_scale) * (1.0 - log_scale * log_scale)
    blank = jnp.zeros((8 - HALF, LON), F32)
    for row in range(ROWS + 4):
        here = slice(row * HALF, (row + 1) * HALF)
        field = jnp.concatenate([scaled[here], blank, upper[here], blank], 0)
        for shift in range(3):
            part = turned(field, shift - 1).astype(BF16)
            coupled[row, shift * 16 : (shift + 1) * 16, :] = part

    def second(row):
        back = dot(w_back_2[...], coupled[pl.ds(row, 3)].reshape(144, LON))
        grad = back * slope_2[row] * inside(base, row - 1)
        for shift in range(3):
            part = turned(grad, shift - 1).astype(BF16)
            turned_2[row, shift * CH : (shift + 1) * CH, :] = part

    loop(0, ROWS + 2, second)
    sum_out[...] = jnp.zeros_like(sum_out)
    sum_mid[...] = jnp.zeros_like(sum_mid)
    sum_in[...] = jnp.zeros_like(sum_in)

    def last(row):
        near_2 = hidden_2[pl.ds(row + 2, 3)].reshape(3 * CH, LON)
        sum_out[...] += dot_cells(coupled[row + 2], near_2)
        near_1 = hidden_1[pl.ds(row + 3, 3)].reshape(3 * CH, LON)
        sum_mid[...] += dot_cells(turned_2[row + 1], near_1)
        back = dot(w_back_1[...], turned_2[pl.ds(row, 3)].reshape(9 * CH, LON))
        grad = (back * slope_1[row]).astype(BF16)
        near_0 = stack[pl.ds(row + 4, 3)].reshape(9 * FIELDS, LON)
        sum_in[...] += dot_cells(grad, near_0)

    loop(0, ROWS, last)
    packed[4 * CH :, :] = jnp.zeros((2 * CH, 128), F32)
    for tap in range(9):
        a, b = tap // 3, tap % 3
        at = (tap // 2) * CH
        side = slice((tap % 2) * CH, (tap % 2 + 1) * CH)
        packed[at : at + CH, side] = sum_mid[b * CH : (b + 1) * CH, a * CH : (a + 1) * CH]
        at = 4 * CH + tap * VARS
        across = slice(a * CH, (a + 1) * CH)
        packed[at : at + HALF, CH:] = sum_out[b * 16 : b * 16 + HALF, across]
        packed[at + HALF : at + VARS, CH:] = sum_out[b * 16 + 8 : b * 16 + 8 + HALF, across]
        across = slice(tap * INPUTS, (tap + 1) * INPUTS)
        packed[5 * CH :, across] = sum_in[:, tap * FIELDS : tap * FIELDS + INPUTS]
    packed[5 * CH : 5 * CH + 1, 96:97] = share
    half = MEMBERS * CHUNK
    for copy in range(2):

        @pl.when(core == copy)
        def _():
            mine[...] = packed[copy * half : (copy + 1) * half, :]
            theirs[...] = packed[(1 - copy) * half : (2 - copy) * half, :]


def unpack_kernel(place, mine, theirs, grad_in, grad_mid, grad_out, energy, packed):
    half = MEMBERS * CHUNK
    for copy in range(2):

        @pl.when(place[2] == copy)
        def _():
            packed[copy * half : (copy + 1) * half, :] = mine[...]
            packed[(1 - copy) * half : (2 - copy) * half, :] = theirs[...]

    for tap in range(9):
        at = (tap // 2) * CH
        grad_mid[tap] = packed[at : at + CH, (tap % 2) * CH : (tap % 2 + 1) * CH]
        at = 4 * CH + tap * VARS
        grad_out[tap] = packed[at : at + VARS, CH:]
        grad_in[tap] = packed[5 * CH :, tap * INPUTS : (tap + 1) * INPUTS]
    energy[...] = packed[5 * CH : 5 * CH + 1, 96:97]


def call(kernel, outs, scratch=(), flops=10**6):
    vmem = pl.BlockSpec(memory_space=pltpu.VMEM)

    def run(place, *arrays):
        return pl.pallas_call(
            kernel,
            out_shape=[jax.ShapeDtypeStruct(shape, dtype) for shape, dtype in outs],
            in_specs=[pl.BlockSpec(memory_space=pltpu.SMEM)] + [vmem] * len(arrays),
            out_specs=[vmem] * len(outs),
            scratch_shapes=[pltpu.VMEM(shape, dtype) for shape, dtype in scratch],
            compiler_params=pltpu.CompilerParams(vmem_limit_bytes=VMEM_LIMIT),
            cost_estimate=pl.CostEstimate(flops=flops, bytes_accessed=10**6, transcendentals=0),
        )(place, *arrays)

    return run


VMEM_LIMIT = 32 * 2**20


def padded_to(array, axis, size):
    pads = [(0, 0)] * array.ndim
    pads[axis] = (0, size - array.shape[axis])
    return jnp.pad(array, pads)


def weights_of(kernel_in, kernel_mid, kernel_out):
    taps_in = padded_to(kernel_in, 2, FIELDS).reshape(3, 3, CH, FIELDS)
    w_in = taps_in.transpose(2, 0, 1, 3).reshape(CH, 9 * FIELDS)
    taps_mid = kernel_mid.reshape(3, 3, CH, CH)
    w_mid = taps_mid.transpose(1, 2, 0, 3).reshape(3 * CH, 3 * CH)
    w_back_1 = taps_mid[::-1].transpose(3, 0, 1, 2).reshape(CH, 9 * CH)
    taps_out = padded_to(kernel_out.reshape(3, 3, 2, HALF, CH), 3, 8).reshape(3, 3, 16, CH)
    w_out = taps_out.transpose(1, 2, 0, 3).reshape(48, 3 * CH)
    w_back_2 = taps_out[::-1].transpose(3, 0, 1, 2).reshape(CH, 144)
    return w_in, w_mid, w_out, w_back_2, w_back_1


def per_device(members, condition, observed, kernel_in, kernel_mid, kernel_out):
    members = members[0]
    core = lax.axis_index("core")
    tile = lax.axis_index(TILE)
    place = jnp.stack([lax.axis_index("member"), tile * ROWS, core]).astype(jnp.int32)
    table = jnp.asarray(lat_table())
    lat = lax.dynamic_slice_in_dim(table, tile, 1, 0)[0]
    lat = jnp.broadcast_to(lat[:, None], (FIXED_AT + ROWS, 128))
    blank = jnp.zeros((1, ROWS, LON), F32)
    own = jnp.concatenate([members[:HALF], condition, members[HALF:], observed[HALF:], blank], 0)
    own = own.transpose(1, 0, 2)
    up = [(i, i + 1) for i in range(TILES - 1)]
    down = [(i + 1, i) for i in range(TILES - 1)]
    before = lax.ppermute(own[ROWS - HALO :], TILE, up)
    after = lax.ppermute(own[:HALO], TILE, down)
    w_in, w_mid, w_out, w_back_2, w_back_1 = weights_of(kernel_in, kernel_mid, kernel_out)
    send, pushed, kept, stack, hidden_1, slope_1, hidden_2, slope_2 = call(
        forward_kernel,
        [
            ((MEMBERS, FIXED_AT + HALF * ROWS, LON), F32),
            ((VARS, ROWS, LON), F32),
            ((3, WIDE, LON), F32),
            ((ROWS + 10, 3 * FIELDS, LON), BF16),
            ((ROWS + 8, CH, LON), BF16),
            ((ROWS, CH, LON), F32),
            ((ROWS + 6, CH, LON), BF16),
            ((ROWS + 2, CH, LON), F32),
        ],
        flops=10**9,
    )(place, before, own, after, members, w_in, w_mid, w_out)
    fields = lax.all_to_all(send, "member", 0, 0)
    (partials,) = call(distance_kernel, [((TILES, MEMBERS, 128), F32)])(
        place, lat, fields, kept, observed
    )
    totals = lax.all_to_all(partials, TILE, 0, 0)
    mine, theirs = call(
        backward_kernel,
        [((MEMBERS * CHUNK, 128), F32)] * 2,
        [
            ((ROWS + 4, 48, LON), BF16),
            ((ROWS + 2, 3 * CH, LON), BF16),
            ((48, 3 * CH), F32),
            ((3 * CH, 3 * CH), F32),
            ((CH, 9 * FIELDS), F32),
            ((6 * CH, 128), F32),
        ],
        flops=10**9,
    )(
        place, lat, totals, fields, kept, stack, hidden_1, slope_1, hidden_2, slope_2,
        w_back_2, w_back_1,
    )
    swap = [(0, 1), (1, 0)]
    mine = mine + lax.ppermute(theirs, "core", swap)
    chunk = jnp.sum(lax.all_to_all(mine.reshape(MEMBERS, CHUNK, 128), "member", 0, 0), 0)
    chunk = jnp.sum(spread(chunk, "ring", RING), 0)
    half = spread(chunk, "member", MEMBERS).reshape(MEMBERS * CHUNK, 128)
    other = lax.ppermute(half, "core", swap)
    grad_in, grad_mid, grad_out, energy = call(
        unpack_kernel,
        [((9, CH, INPUTS), F32), ((9, CH, CH), F32), ((9, VARS, CH), F32), ((1, 1), F32)],
        [((6 * CH, 128), F32)],
    )(place, half, other)
    return (pushed[None], energy[0, 0], grad_in, grad_mid, grad_out)


def solution(mesh):
    fine = Mesh(mesh.devices.reshape(MEMBERS, -1, 2), ("member",) + TILE)
    in_specs = (
        P("member", None, TILE, None),
        P(None, TILE, None),
        P(None, TILE, None),
        P(),
        P(),
        P(),
    )
    out_specs = (P("member", None, TILE, None), P(), P(), P(), P())
    return jax.shard_map(
        per_device, mesh=fine, in_specs=in_specs, out_specs=out_specs, check_vma=False
    )
```

time: 488 us -> 126 us (0.26)
  waiting for transfers between devices: 206 us -> 22.7 us
  blocking collectives: 171 us -> 30 us
  matrix products: 30.9 us -> 0 us
  between operations: 21.2 us -> 0.83 us
  Pallas kernels: 0 us -> 14.9 us
  local copies, waits for them, and re-layouts: 11 us -> 24.6 us
  other arithmetic: 11.5 us -> 0.13 us
    psum x3 -> x0, blocking collectives: 171 us -> none  [the longest x1 86.6 us: per_device(): lax.psum((grad_first, grad_middle, grad_last), ('member', 'tile'))]
    psum x1 -> x0, waiting for transfers between devices: 153 us -> none  [per_device(): lax.psum((grad_first, grad_middle, grad_last), ('member', 'tile'))]
    ppermute x17 -> x4, waiting for transfers between devices: 52.8 us -> 6.92 us  [the longest x1 4.91 us: per_device(): after = lax.ppermute(own[:HALO], TILE, down)]
    dot_general x72 -> x0, matrix products: 30.9 us -> none  [the longest x45 17.4 us: convolve(): jnp.einsum('oc,crl->orl', kernel[tap_index], window_at(padded, tap_index,...]
    all_to_all x0 -> x3, blocking collectives: none -> 30 us  [the longest x2 22.4 us: spread(): return lax.all_to_all(copies, axes, 0, 0)]
    ppermute x17 -> x4, starting transfers between devices: 35.1 us -> 12.8 us  [the longest x1 6.21 us: per_device(): before = lax.ppermute(own[ROWS - HALO:], TILE, up)]
    all_to_all x0 -> x2, starting transfers between devices: none -> 18.8 us  [the longest x1 14.5 us: per_device(): totals = lax.all_to_all(partials, TILE, 0, 0)]
    all_to_all x0 -> x2, waiting for transfers between devices: none -> 15.7 us  [the longest x1 11.1 us: per_device(): fields = lax.all_to_all(send, 'member', 0, 0)]
  transfers between devices with their start and end apart: 18 -> 6, of which waited for: 12 -> 5; matrix products, arithmetic and copies ran while one was open for 2% -> 6% of each run, Pallas kernels for 0% -> 0%
where the time goes in v2:
time: 126 us; the launch traced here: 125 us
  starting transfers between devices  31.6 us (25%)
  blocking collectives  30 us (24%)
  local copies, waits for them, and re-layouts  24.6 us (20%)
  waiting for transfers between devices  22.7 us (18%)
  Pallas kernels  14.9 us (12%)
    all_to_all x2, blocking collectives, spread(): return lax.all_to_all(copies, axes, 0, 0)  22.4 us
    pallas_call x4, Pallas kernels, run(): pl.pallas_call(kernel, out_shape=[jax.ShapeDtypeStruct(shape, dtype) for...  14.9 us
    all_to_all x1, starting transfers between devices, per_device(): totals = lax.all_to_all(partials, TILE, 0, 0)  14.5 us
    unnamed x41, local copies, waits for them, and re-layouts  14.5 us
    all_to_all x1, waiting for transfers between devices, per_device(): fields = lax.all_to_all(send, 'member', 0, 0)  11.1 us
    all_to_all x1, blocking collectives, per_device(): lax.all_to_all(mine.reshape(MEMBERS, CHUNK, 128), 'member', 0, 0)  7.54 us
    ppermute x1, starting transfers between devices, per_device(): before = lax.ppermute(own[ROWS - HALO:], TILE, up)  6.21 us
    ppermute x1, waiting for transfers between devices, per_device(): after = lax.ppermute(own[:HALO], TILE, down)  4.91 us
  transfers between devices with their start and end apart: 6, of which 5 were waited for; matrix products, arithmetic and copies ran while one was open for 6% of the time, Pallas kernels for 0%

profile of v2, /device:TPU:1, one launch (start us, length us, event | category | flops | bytes accessed | tf_op | source)
XLA Modules:
  0.0 124.6 jit_solution(10261940844220825627)
XLA Ops:
  0.7 0.9 fusion.1
  1.5 1.0 copy.35
  2.5 0.8 slice.25
  3.8 6.2 %collective-permute-start = (f32[5,16,512]{2,1,0:T(8,128)S(1)}, f32[5,16,512]{2,1,0:T(8,128)S(1)}, u32[]{:S(2)}, u32[]{:S(2)}) collective-permute-start(f32[5,16,512]{2,1,0:T(8,128)S(1)} %get-tuple-element.49), channel_id=1, source_target_pairs={{0,1},{1,2},{2,3},{3,4},{4,5},{5,6},{6,7},{7,8},{8,9},{9,10},{10,1... | collective-permute-start | bytes 491528 | tf_op jit(solution)/shard_map/ppermute | solution.py:306
  10.0 1.9 %collective-permute-start.1 = (f32[5,16,512]{2,1,0:T(8,128)S(1)}, f32[5,16,512]{2,1,0:T(8,128)S(1)}, u32[]{:S(2)}, u32[]{:S(2)}) collective-permute-start(f32[5,16,512]{2,1,0:T(8,128)S(1)} %get-tuple-element.48), channel_id=1, source_target_pairs={{1,0},{2,1},{3,2},{4,3},{5,4},{6,5},{7,6},{8,7},{9,8},{10,9},{11,1... | collective-permute-start | bytes 491528 | tf_op jit(solution)/shard_map/ppermute | solution.py:307
  13.2 4.9 %collective-permute-done.1.after = f32[5,16,512]{2,1,0:T(8,128)S(1)} collective-permute-done((f32[5,16,512]{2,1,0:T(8,128)S(1)}, f32[5,16,512]{2,1,0:T(8,128)S(1)}, u32[]{:S(2)}, u32[]{:S(2)}) %collective-permute-start.1) | collective-permute-done | bytes 163872 | tf_op jit(solution)/shard_map/ppermute | solution.py:307
  18.2 6.7 %shard_map.110 = (f32[8,64,512]{2,1,0:T(8,128)}, f32[6,8,512]{2,1,0:T(8,128)}, f32[3,36,512]{2,1,0:T(8,128)S(1)}, bf16[18,48,512]{2,1,0:T(8,128)(2,1)S(1)}, bf16...) custom-call(s32[3]{0:T(128)S(1)} %pad_add_fusion.place, ...), custom_call_target="tpu_custom_call" | custom-call | flops 1000000000 | bytes 1000000 | tf_op jit(solution)/shard_map/pallas_call | solution.py:259
  24.9 1.0 copy-done
  26.6 0.9 copy-done.5
  27.5 0.9 copy-done.7
  28.4 4.3 %all-to-all-start = ((f32[8,64,512]{2,1,0:T(8,128)}), f32[8,64,512]{2,1,0:T(8,128)S(1)}, u32[]{:S(2)}, u32[]{:S(2)}) async-start(f32[8,64,512]{2,1,0:T(8,128)} %get-tuple-element.20), calls=%async_computation | async-start | bytes 2097152 | tf_op jit(solution)/shard_map/all_to_all | solution.py:323
  33.4 11.1 %all-to-all-done.fields = f32[8,64,512]{2,1,0:T(8,128)S(1)} async-done(((f32[8,64,512]{2,1,0:T(8,128)}), f32[8,64,512]{2,1,0:T(8,128)S(1)}, u32[]{:S(2)}, u32[]{:S(2)}) %all-to-all-start) | async-done | bytes 1048608 | tf_op jit(solution)/shard_map/all_to_all | solution.py:323
  44.5 0.9 copy-done.3
  47.5 14.5 %all-to-all-start.1 = ((f32[32,8,128]{2,1,0:T(8,128)}), f32[32,8,128]{2,1,0:T(8,128)S(1)}, u32[]{:S(2)}, u32[]{:S(2)}) async-start(f32[32,8,128]{2,1,0:T(8,128)} %copy-done.9), calls=%async_computation.1 | async-start | bytes 262144 | tf_op jit(solution)/shard_map/all_to_all | solution.py:327
  62.0 1.4 %rev.6 = bf16[3,3,16,64]{3,2,1,0:T(8,128)(2,1)} reverse(bf16[3,3,16,64]{3,2,1,0:T(8,128)(2,1)} %get-tuple-element.52), dimensions={0} | reverse | bytes 36864 | tf_op jit(solution)/shard_map/rev | solution.py:289
  63.4 1.5 %copy.39.w_back_2 = bf16[64,144]{1,0:T(8,128)(2,1)} copy(bf16[64,144]{0,1:T(8,128)(2,1)} %bitcast.44) | data formatting | bytes 36864 | tf_op jit(solution)/shard_map/reshape | solution.py:289
  64.9 1.6 %rev.7 = bf16[3,3,64,64]{3,2,1,0:T(8,128)(2,1)} reverse(bf16[3,3,64,64]{3,2,1,0:T(8,128)(2,1)} %bitcast.40), dimensions={0} | reverse | bytes 147456 | tf_op jit(solution)/shard_map/rev | solution.py:286
  66.4 1.7 %copy.40.w_back_1 = bf16[64,576]{1,0:T(8,128)(2,1)} copy(bf16[64,576]{0,1:T(8,128)(2,1)} %bitcast.39) | data formatting | bytes 147456 | tf_op jit(solution)/shard_map/reshape | solution.py:286
  68.1 4.7 %all-to-all-done.1.totals = f32[32,8,128]{2,1,0:T(8,128)S(1)} async-done(((f32[32,8,128]{2,1,0:T(8,128)}), f32[32,8,128]{2,1,0:T(8,128)S(1)}, u32[]{:S(2)}, u32[]{:S(2)}) %all-to-all-start.1) | async-done | bytes 131104 | tf_op jit(solution)/shard_map/all_to_all | solution.py:327
  72.8 1.2 copy-done.1
  74.0 0.9 copy-done.4
  74.9 1.2 copy-done.6
  76.1 1.2 copy-done.8
  77.3 0.9 copy-done.10
  79.7 6.0 %shard_map.112 = (f32[192,128]{1,0:T(8,128)S(1)}, f32[192,128]{1,0:T(8,128)S(1)}) custom-call(s32[3]{0:T(128)S(1)} %pad_add_fusion.place, f32[48,128]{1,0:T(8,128)S(1)} %copy-done.12, f32[32,8,128]{2,1,0:T(8,128)S(1)} %all-to-all-done.1.totals, f32[8,64,512]{2,1,0:T(8,128)S(1)} %all-to-all-done.fields, f32[3,36,512]{2,1,0:T(8,128)S(1)} %copy-done.4, ...), custom_call_target="tpu_custom_call" | custom-call | flops 1000000000 | bytes 1000000 | tf_op jit(solution)/shard_map/pallas_call | solution.py:259
  85.9 1.1 collective-permute-done.2
  87.0 7.5 %all_to_all.25 = f32[8,24,128]{2,1,0:T(8,128)S(1)} all-to-all(f32[8,24,128]{2,1,0:T(8,128)S(1)} %bitcast.42), channel_id=1, replica_groups=mesh['member'=8,'ring'=16,'core'=2] {'member'}, dimensions={0} | all-to-all | bytes 196608 | tf_op jit(solution)/shard_map/all_to_all | solution.py:346
  94.6 14.8 %all_to_all.26 = f32[16,24,128]{2,1,0:T(8,128)S(1)} all-to-all(f32[16,24,128]{2,1,0:T(8,128)S(1)} %broadcast_in_dim.29), channel_id=1, replica_groups=mesh['member'=8,'ring'=16,'core'=2] {'ring'}, dimensions={0} | all-to-all | bytes 393216 | tf_op jit(solution)/shard_map/all_to_all | solution.py:29
  109.5 7.6 %all_to_all.27 = f32[8,24,128]{2,1,0:T(8,128)S(1)} all-to-all(f32[8,24,128]{2,1,0:T(8,128)S(1)} %broadcast_in_dim.30), channel_id=1, replica_groups=mesh['member'=8,'ring'=16,'core'=2] {'member'}, dimensions={0} | all-to-all | bytes 196608 | tf_op jit(solution)/shard_map/all_to_all | solution.py:29
  117.1 4.4 %collective-permute-start.3 = (f32[192,128]{1,0:T(8,128)S(1)}, f32[192,128]{1,0:T(8,128)S(1)}, u32[]{:S(2)}, u32[]{:S(2)}) collective-permute-start(f32[192,128]{1,0:T(8,128)S(1)} %bitcast.36), channel_id=1, source_target_pairs={{0,1},{1,0},{2,3},{3,2},{4,5},{5,4},{6,7},{7,6},{8,9},{9,8},{10,11... | collective-permute-start | bytes 294920 | tf_op jit(solution)/shard_map/ppermute | solution.py:349
  121.5 0.9 collective-permute-done.3.theirs
  122.4 1.4 %shard_map.113 = (f32[9,64,9]{2,1,0:T(8,128)S(1)}, f32[9,64,64]{2,1,0:T(8,128)}, f32[9,6,64]{2,1,0:T(8,128)}, f32[1,1]{1,0:T(1,128)}) custom-call(s32[3]{0:T(128)S(1)} %pad_add_fusion.place, f32[192,128]{1,0:T(8,128)S(1)} %bitcast.37, f32[192,128]{1,0:T(8,128)S(1)} %collective-permute-done.3.theirs), custom_call_target="tpu_custom_call" | custom-call | flops 1000000 | bytes 1000000 | tf_op jit(solution)/shard_map/pallas_call | solution.py:259
  (54 shorter events, 7.9 us)
Async XLA Ops:
  0.6 11.3 %copy-start.18 = (bf16[9,6,64]{2,1,0:T(8,128)(2,1)S(1)}, bf16[9,6,64]{2,1,0:T(8,128)(2,1)}, u32[]{:S(2)}) copy-start(bf16[9,6,64]{2,1,0:T(8,128)(2,1)} %param.12) | copy-start | bytes 20740
  0.6 12.1 %copy-start.16 = (bf16[9,64,64]{2,1,0:T(8,128)(2,1)S(1)}, bf16[9,64,64]{2,1,0:T(8,128)(2,1)}, u32[]{:S(2)}) copy-start(bf16[9,64,64]{2,1,0:T(8,128)(2,1)} %param.11) | copy-start | bytes 221188
  3.3 9.8 %copy-start.17 = (bf16[9,64,9]{1,2,0:T(8,128)(2,1)S(1)}, bf16[9,64,9]{1,2,0:T(8,128)(2,1)}, u32[]{:S(2)}) copy-start(bf16[9,64,9]{1,2,0:T(8,128)(2,1)} %param.10) | copy-start | bytes 31108
  3.3 14.8 %copy-start.15 = (f32[1,6,8,512]{3,2,1,0:T(8,128)S(1)}, f32[1,6,8,512]{3,2,1,0:T(8,128)}, u32[]{:S(2)}) copy-start(f32[1,6,8,512]{3,2,1,0:T(8,128)} %param.7) | copy-start | bytes 294916
  3.8 9.5 %collective-permute-start = (f32[5,16,512]{2,1,0:T(8,128)S(1)}, f32[5,16,512]{2,1,0:T(8,128)S(1)}, u32[]{:S(2)}, u32[]{:S(2)}) collective-permute-start(f32[5,16,512]{2,1,0:T(8,128)S(1)} %get-tuple-element.49), channel_id=1, source_target_pairs={{0,1},{1,2},{2,3},{3,4},{4,5},{5,6},{6,7},{7,8},{8,9},{9,10},{10,1... | collective-permute-start | bytes 491528 | tf_op jit(solution)/shard_map/ppermute | solution.py:306
  10.0 8.1 %collective-permute-start.1 = (f32[5,16,512]{2,1,0:T(8,128)S(1)}, f32[5,16,512]{2,1,0:T(8,128)S(1)}, u32[]{:S(2)}, u32[]{:S(2)}) collective-permute-start(f32[5,16,512]{2,1,0:T(8,128)S(1)} %get-tuple-element.48), channel_id=1, source_target_pairs={{1,0},{2,1},{3,2},{4,3},{5,4},{6,5},{7,6},{8,7},{9,8},{10,9},{11,1... | collective-permute-start | bytes 491528 | tf_op jit(solution)/shard_map/ppermute | solution.py:307
  24.9 1.0 copy-start
  25.9 0.7 copy-start.2
  26.6 0.9 copy-start.5
  27.5 0.9 copy-start.7
  28.4 16.1 %copy-start.13 = (f32[6,8,512]{2,1,0:T(8,128)S(1)}, f32[6,8,512]{2,1,0:T(8,128)}, u32[]{:S(2)}) copy-start(f32[6,8,512]{2,1,0:T(8,128)} %observed.1) | copy-start | bytes 294916
  28.4 16.0 %all-to-all-start = ((f32[8,64,512]{2,1,0:T(8,128)}), f32[8,64,512]{2,1,0:T(8,128)S(1)}, u32[]{:S(2)}, u32[]{:S(2)}) async-start(f32[8,64,512]{2,1,0:T(8,128)} %get-tuple-element.20), calls=%async_computation | async-start | bytes 2097152 | tf_op jit(solution)/shard_map/all_to_all | solution.py:323
  44.5 0.9 copy-start.3
  46.2 0.6 copy-start.9
  46.9 0.6 copy-start.11
  47.5 25.3 %all-to-all-start.1 = ((f32[32,8,128]{2,1,0:T(8,128)}), f32[32,8,128]{2,1,0:T(8,128)S(1)}, u32[]{:S(2)}, u32[]{:S(2)}) async-start(f32[32,8,128]{2,1,0:T(8,128)} %copy-done.9), calls=%async_computation.1 | async-start | bytes 262144 | tf_op jit(solution)/shard_map/all_to_all | solution.py:327
  72.8 1.2 copy-start.1
  74.0 0.9 copy-start.4
  74.9 1.2 copy-start.6
  76.1 1.2 copy-start.8
  77.3 0.9 copy-start.10
  78.2 0.7 copy-start.12
  78.9 0.8 copy-start.14
  85.6 1.4 %collective-permute-start.2 = (f32[192,128]{1,0:T(8,128)S(1)}, f32[192,128]{1,0:T(8,128)S(1)}, u32[]{:S(2)}, u32[]{:S(2)}) collective-permute-start(f32[192,128]{1,0:T(8,128)S(1)} %get-tuple-element.28), channel_id=1, source_target_pairs={{0,1},{1,0},{2,3},{3,2},{4,5},{5,4},{6,7},{7,6},{8,9},{9,8},{10,11... | collective-permute-start | bytes 294920 | tf_op jit(solution)/shard_map/ppermute | solution.py:345
  117.1 5.3 %collective-permute-start.3 = (f32[192,128]{1,0:T(8,128)S(1)}, f32[192,128]{1,0:T(8,128)S(1)}, u32[]{:S(2)}, u32[]{:S(2)}) collective-permute-start(f32[192,128]{1,0:T(8,128)S(1)} %bitcast.36), channel_id=1, source_target_pairs={{0,1},{1,0},{2,3},{3,2},{4,5},{5,4},{6,7},{7,6},{8,9},{9,8},{10,11... | collective-permute-start | bytes 294920 | tf_op jit(solution)/shard_map/ppermute | solution.py:349

commit v3 on v2

v3 whole, which is shorter than its diff:
```python
import functools
import math

import jax
import jax.numpy as jnp
import numpy as np
from jax import lax
from jax.experimental import pallas as pl
from jax.experimental.pallas import tpu as pltpu
from jax.sharding import Mesh, PartitionSpec as P

EPSILON = 1e-06
MEMBERS, NLAT, LON, ROWS = 8, 256, 512, 8
VARS, HALF, COND, CH = 6, 3, 6, 64
TILES, RING = 32, 16
ENTRIES = VARS * NLAT * LON
HALO = 5
FIELDS = 16
INPUTS = HALF + COND
WIDE = (ROWS + 4) * HALF
FIXED_AT = 40
CHUNK = 24
TILE = ("ring", "core")
F32, BF16 = jnp.float32, jnp.bfloat16


def spread(value, axes, count):
    copies = jnp.broadcast_to(value[None], (count,) + value.shape)
    return lax.all_to_all(copies, axes, 0, 0)


def lat_table():
    rows = np.arange(NLAT)
    cosine = np.cos((-90.0 + 180.0 * (rows + 0.5) / NLAT) * (np.pi / 180.0))
    lat = (cosine / cosine.mean()).astype(np.float32)
    padded = np.pad(lat, (2, 2))
    table = np.zeros((TILES, FIXED_AT + ROWS), np.float32)
    for tile in range(TILES):
        wide = padded[tile * ROWS : tile * ROWS + ROWS + 4]
        table[tile, :WIDE] = np.repeat(wide, HALF)
        table[tile, FIXED_AT:] = lat[tile * ROWS : (tile + 1) * ROWS]
    return table


def turned(value, step):
    return value if step == 0 else pltpu.roll(value, step % LON, 1)


def dot(left, right):
    return jnp.dot(left, right, preferred_element_type=F32)


def dot_cells(left, right):
    return lax.dot_general(left, right, (((1,), (1,)), ((), ())), preferred_element_type=F32)


def inside(base, row):
    row = base + row
    return jnp.where((row >= 0) & (row < NLAT), 1.0, 0.0).astype(F32)


def sigmoid(value):
    return 0.5 * jnp.tanh(0.5 * value) + 0.5


def loop(start, stop, body):
    lax.fori_loop(start, stop, lambda row, carry: (body(row), carry)[1], 0, unroll=2)


def pack_kernel(place, members, condition, observed, own, edge_far, edge_near):
    for row in range(ROWS):
        own[row, :HALF, :] = members[:HALF, row, :]
        own[row, HALF:INPUTS, :] = condition[:, row, :]
        own[row, INPUTS : INPUTS + HALF, :] = members[HALF:, row, :]
        own[row, INPUTS + HALF : INPUTS + 2 * HALF, :] = observed[HALF:, row, :]
        own[row, FIELDS - 1 :, :] = jnp.zeros((1, LON), F32)
    odd = place[2] == 1
    for row in range(HALO):
        initial, last = own[row], own[ROWS - HALO + row]
        edge_far[row] = jnp.where(odd, last, initial)
        edge_near[row] = jnp.where(odd, initial, last)


def weights_kernel(
    place, kernel_in, kernel_mid, kernel_out, w_in, w_mid, w_out, w_back_2, w_back_1,
    flat_in, square, flat_out, back_2, back_1, held_2, held_1, sems,
):
    flat_in[...] = jnp.zeros_like(flat_in)
    flat_out[...] = jnp.zeros_like(flat_out)
    back_2[...] = jnp.zeros_like(back_2)
    for tap in range(9):
        a, b = tap // 3, tap % 3
        back = 3 * (2 - a) + b
        flat_in[:, tap * FIELDS : tap * FIELDS + INPUTS] = kernel_in[tap].astype(F32)
        mid = kernel_mid[tap].astype(F32)
        square[b * CH : (b + 1) * CH, a * CH : (a + 1) * CH] = mid
        back_1[:, back * CH : (back + 1) * CH] = mid.T
        out = kernel_out[tap].astype(F32)
        across = slice(a * CH, (a + 1) * CH)
        flat_out[b * 16 : b * 16 + HALF, across] = out[:HALF]
        flat_out[b * 16 + 8 : b * 16 + 8 + HALF, across] = out[HALF:]
        out = jnp.concatenate([out, jnp.zeros((8 - VARS, CH), F32)], 0).T
        back_2[:, back * 16 : back * 16 + HALF] = out[:, :HALF]
        back_2[:, back * 16 + 8 : back * 16 + 8 + HALF] = out[:, HALF:VARS]
    held_2[...] = back_2[...].astype(BF16)
    held_1[...] = back_1[...].astype(BF16)
    copies = [
        pltpu.make_async_copy(held_2, w_back_2, sems.at[0]),
        pltpu.make_async_copy(held_1, w_back_1, sems.at[1]),
    ]
    for copy in copies:
        copy.start()
    w_in[...] = flat_in[...].astype(BF16)
    w_mid[...] = square[...].astype(BF16)
    w_out[...] = flat_out[...].astype(BF16)
    for copy in copies:
        copy.wait()


def forward_kernel(
    place, far, near, own, members, w_in, w_mid, w_out,
    send_out, pushed, kept_out, stack_out, hidden_1_out, slope_1_out, hidden_2_out, slope_2_out,
    send, kept, stack, hidden_1, slope_1, hidden_2, slope_2, edges, sems,
):
    base = place[1]
    odd = place[2] == 1
    copies = []

    def keep(source, target):
        copy = pltpu.make_async_copy(source, target, sems.at[len(copies)])
        copy.start()
        copies.append(copy)

    for row in range(HALO):
        edges[row] = jnp.where(odd, near[row], far[row])
        edges[HALO + row] = jnp.where(odd, far[row], near[row])

    def wide(row):
        if row < HALO:
            return edges[row]
        return own[row - HALO] if row < HALO + ROWS else edges[row - ROWS]

    for row in range(ROWS + 2 * HALO):
        field = wide(row)
        for shift in range(3):
            part = turned(field, 1 - shift).astype(BF16)
            stack[row, shift * FIELDS : (shift + 1) * FIELDS, :] = part
    keep(stack, stack_out)

    def first(row, kept_row):
        pre = dot(w_in[...], stack[pl.ds(row, 3)].reshape(9 * FIELDS, LON))
        gate = sigmoid(pre)
        hidden_1[row] = (pre * gate * inside(base, row - 4)).astype(BF16)
        if kept_row:
            slope_1[row - 4] = gate * (1.0 + pre * (1.0 - gate))

    loop(0, 4, functools.partial(first, kept_row=False))
    loop(4, 12, functools.partial(first, kept_row=True))
    loop(12, 16, functools.partial(first, kept_row=False))
    keep(hidden_1, hidden_1_out)
    keep(slope_1, slope_1_out)

    def second(row, kept_row):
        part = dot(w_mid[...], hidden_1[pl.ds(row, 3)].reshape(3 * CH, LON))
        pre = turned(part[:CH], 1) + part[CH : 2 * CH] + turned(part[2 * CH :], -1)
        gate = sigmoid(pre)
        hidden_2[row] = (pre * gate * inside(base, row - 3)).astype(BF16)
        if kept_row:
            slope_2[row - 2] = gate * (1.0 + pre * (1.0 - gate))

    loop(0, 2, functools.partial(second, kept_row=False))
    loop(2, 12, functools.partial(second, kept_row=True))
    loop(12, 14, functools.partial(second, kept_row=False))
    keep(hidden_2, hidden_2_out)
    keep(slope_2, slope_2_out)

    send[WIDE:FIXED_AT, :] = jnp.zeros((FIXED_AT - WIDE, LON), F32)
    send[FIXED_AT:, :] = members[:HALF].reshape(HALF * ROWS, LON)
    for row in range(ROWS + 4):
        part = dot(w_out[...], hidden_2[row : row + 3].reshape(3 * CH, LON))
        both = turned(part[:16], 1) + part[16:32] + turned(part[32:], -1)
        log_scale = jnp.tanh(both[:HALF])
        field = wide(row + 3)
        moving = field[INPUTS : INPUTS + HALF]
        moved = moving * jnp.exp(log_scale) + both[8 : 8 + HALF]
        here = slice(row * HALF, (row + 1) * HALF)
        kept[0, here, :] = log_scale
        kept[1, here, :] = moving
        kept[2, here, :] = field[INPUTS + HALF : INPUTS + 2 * HALF]
        kept[3, here, :] = moved
        send[here, :] = moved
        if 2 <= row < 2 + ROWS:
            for var in range(HALF):
                pushed[HALF + var, row - 2 : row - 1, :] = moved[var : var + 1]
    for member in range(MEMBERS):
        keep(send, send_out.at[member])
    keep(kept, kept_out)
    pushed[:HALF] = members[:HALF]
    for copy in copies:
        copy.wait()


def folded(value):
    return sum(value[..., at : at + 128] for at in range(0, LON, 128))


def distance_kernel(
    place, lat, members, observed, fields_in, kept_in, partials_out, fields, kept, partials, sems
):
    copies = [pltpu.make_async_copy(kept_in.at[2:4], kept, sems.at[MEMBERS])]
    for n in range(MEMBERS):
        copies.append(pltpu.make_async_copy(fields_in.at[n], fields.at[n], sems.at[n]))
    for copy in copies:
        copy.start()
    me = place[0]
    spot = lax.broadcasted_iota(jnp.int32, (WIDE, 1), 0)
    wide = jnp.where((spot >= 2 * HALF) & (spot < WIDE - 2 * HALF), lat[:WIDE, :1], 0.0)
    low = jnp.concatenate([lat[FIXED_AT:, :1]] * HALF, 0)
    fixed_mine = members[:HALF].reshape(HALF * ROWS, LON)
    copies[0].wait()
    mine = kept[1]

    def weighed(moved, fixed):
        upper = jnp.sum(folded(wide * (mine - moved) ** 2), 0, keepdims=True)
        lower = jnp.sum(folded(low * (fixed_mine - fixed) ** 2), 0, keepdims=True)
        return upper + lower

    rows = [weighed(kept[0], observed[:HALF].reshape(HALF * ROWS, LON))]
    for n in range(MEMBERS):
        copies[1 + n].wait()
        rows.append(weighed(fields[n, :WIDE], fields[n, FIXED_AT:]))
    all_rows = jnp.concatenate(rows[1:], 0)
    spot = lax.broadcasted_iota(jnp.int32, (MEMBERS, 128), 0)
    all_rows = jnp.where(spot == me, rows[0], all_rows)
    for tile in range(TILES):
        partials[tile] = all_rows
    copy = pltpu.make_async_copy(partials, partials_out, sems.at[0])
    copy.start()
    copy.wait()


def backward_kernel(
    place, lat, totals, fields_in, kept_in, stack_in, hidden_1_in, slope_1_in, hidden_2_in,
    slope_2_in, w_back_2_in, w_back_1_in,
    mine, theirs,
    fields, kept, stack, hidden_1, slope_1, hidden_2, slope_2, w_back_2, w_back_1,
    coupled, turned_2, sum_out, sum_mid, sum_in, packed, sems,
):
    sources = [kept_in, fields_in, w_back_2_in, slope_2_in, hidden_2_in, hidden_1_in]
    sources += [w_back_1_in, slope_1_in, stack_in]
    targets = [kept, fields, w_back_2, slope_2, hidden_2, hidden_1, w_back_1, slope_1, stack]
    copies = []
    for source, target in zip(sources, targets):
        copies.append(pltpu.make_async_copy(source, target, sems.at[len(copies)]))
        copies[-1].start()
    me, base, core = place[0], place[1], place[2]
    total = totals[0]
    for tile in range(1, TILES):
        total = total + totals[tile]
    distances = jnp.sqrt(jnp.sum(total, 1, keepdims=True) / ENTRIES + EPSILON)
    is_me = lax.broadcasted_iota(jnp.int32, (MEMBERS, 1), 0) == me
    shares = jnp.where(is_me, distances / MEMBERS, -distances / (2.0 * MEMBERS * MEMBERS))
    share = jnp.sum(shares, 0, keepdims=True) / TILES
    weights = 1.0 / (jnp.where(is_me, MEMBERS, MEMBERS * MEMBERS) * distances)
    own_weight = jnp.sum(jnp.where(is_me, weights, 0.0), 0, keepdims=True)
    weights = jnp.where(is_me, 0.0, weights)
    sum_out[...] = jnp.zeros_like(sum_out)
    sum_mid[...] = jnp.zeros_like(sum_mid)
    sum_in[...] = jnp.zeros_like(sum_in)
    copies[0].wait()
    log_scale, moving, observed, moved = kept[0], kept[1], kept[2], kept[3]
    inner = (moved - observed) * own_weight
    copies[1].wait()
    for n in range(MEMBERS):
        inner = inner - weights[n : n + 1] * (moved - fields[n, :WIDE])
    upper = lat[:WIDE, :1] * inner / math.sqrt(ENTRIES)
    scaled = upper * moving * jnp.exp(log_scale) * (1.0 - log_scale * log_scale)
    blank = jnp.zeros((8 - HALF, LON), F32)
    for row in range(ROWS + 4):
        here = slice(row * HALF, (row + 1) * HALF)
        field = jnp.concatenate([scaled[here], blank, upper[here], blank], 0)
        for shift in range(3):
            part = turned(field, shift - 1).astype(BF16)
            coupled[row, shift * 16 : (shift + 1) * 16, :] = part
    copies[2].wait()
    copies[3].wait()

    def second(row):
        back = dot(w_back_2[...], coupled[pl.ds(row, 3)].reshape(144, LON))
        grad = back * slope_2[row] * inside(base, row - 1)
        for shift in range(3):
            part = turned(grad, shift - 1).astype(BF16)
            turned_2[row, shift * CH : (shift + 1) * CH, :] = part

    loop(0, ROWS + 2, second)
    for copy in copies[4:]:
        copy.wait()

    def last(row):
        near_2 = hidden_2[pl.ds(row + 2, 3)].reshape(3 * CH, LON)
        sum_out[...] += dot_cells(coupled[row + 2], near_2)
        near_1 = hidden_1[pl.ds(row + 3, 3)].reshape(3 * CH, LON)
        sum_mid[...] += dot_cells(turned_2[row + 1], near_1)
        back = dot(w_back_1[...], turned_2[pl.ds(row, 3)].reshape(9 * CH, LON))
        grad = (back * slope_1[row]).astype(BF16)
        near_0 = stack[pl.ds(row + 4, 3)].reshape(9 * FIELDS, LON)
        sum_in[...] += dot_cells(near_0, grad)

    loop(0, ROWS, last)
    packed[5 * CH :, :] = jnp.zeros((CH, 128), F32)
    packed[4 * CH : 5 * CH, CH:] = jnp.zeros((CH, CH), F32)
    for tap in range(9):
        a, b = tap // 3, tap % 3
        at, side = place_mid(tap)
        packed[at : at + CH, side] = sum_mid[b * CH : (b + 1) * CH, a * CH : (a + 1) * CH]
        at = 5 * CH + tap * VARS
        across = slice(a * CH, (a + 1) * CH)
        packed[at : at + HALF, :CH] = sum_out[b * 16 : b * 16 + HALF, across]
        packed[at + HALF : at + VARS, :CH] = sum_out[b * 16 + 8 : b * 16 + 8 + HALF, across]
        at = 4 * CH + tap * INPUTS
        packed[at : at + INPUTS, CH:] = sum_in[tap * FIELDS : tap * FIELDS + INPUTS]
    packed[6 * CH - 1 :, 127:] = share
    half = MEMBERS * CHUNK
    for copy in range(2):

        @pl.when(core == copy)
        def _():
            mine[...] = packed[copy * half : (copy + 1) * half, :]
            theirs[...] = packed[(1 - copy) * half : (2 - copy) * half, :]


def place_mid(tap):
    return (tap * CH, slice(0, CH)) if tap < 5 else ((tap - 5) * CH, slice(CH, 2 * CH))


def unpack_kernel(place, mine, theirs, grad_in, grad_mid, grad_out, energy, packed):
    half = MEMBERS * CHUNK
    for copy in range(2):

        @pl.when(place[2] == copy)
        def _():
            packed[copy * half : (copy + 1) * half, :] = mine[...]
            packed[(1 - copy) * half : (2 - copy) * half, :] = theirs[...]

    for tap in range(9):
        at, side = place_mid(tap)
        grad_mid[tap] = packed[at : at + CH, side]
        at = 5 * CH + tap * VARS
        grad_out[tap] = packed[at : at + VARS, :CH]
        at = 4 * CH + tap * INPUTS
        grad_in[tap] = packed[at : at + INPUTS, CH:]
    energy[...] = packed[6 * CH - 1 :, 127:]


VMEM_LIMIT = 32 * 2**20
VMEM = pl.BlockSpec(memory_space=pltpu.VMEM)
HBM = pl.BlockSpec(memory_space=pltpu.HBM)


def call(kernel, ins, outs, scratch=(), copies=0, flops=10**6):
    held = [pltpu.VMEM(shape, dtype) for shape, dtype in scratch]
    if copies > 0:
        held.append(pltpu.SemaphoreType.DMA((copies,)))
    return pl.pallas_call(
        kernel,
        out_shape=[jax.ShapeDtypeStruct(shape, dtype) for shape, dtype, spec in outs],
        in_specs=[pl.BlockSpec(memory_space=pltpu.SMEM)] + ins,
        out_specs=[spec for shape, dtype, spec in outs],
        scratch_shapes=held,
        compiler_params=pltpu.CompilerParams(vmem_limit_bytes=VMEM_LIMIT),
        cost_estimate=pl.CostEstimate(flops=flops, bytes_accessed=10**6, transcendentals=0),
    )


def per_device(members, condition, observed, kernel_in, kernel_mid, kernel_out):
    members = members[0]
    core = lax.axis_index("core")
    tile = lax.axis_index(TILE)
    place = jnp.stack([lax.axis_index("member"), tile * ROWS, core]).astype(jnp.int32)
    table = jnp.asarray(lat_table())
    lat = lax.dynamic_slice_in_dim(table, tile, 1, 0)[0]
    lat = jnp.broadcast_to(lat[:, None], (FIXED_AT + ROWS, 128))
    edge = ((HALO, FIELDS, LON), F32, VMEM)
    own, edge_far, edge_near = call(
        pack_kernel, [VMEM] * 3, [((ROWS, FIELDS, LON), F32, VMEM), edge, edge]
    )(place, members, condition, observed)
    across = [(i, i + 1) for i in range(1, TILES - 1, 2)]
    far = lax.ppermute(edge_far, TILE, across + [(j, i) for i, j in across])
    near = lax.ppermute(edge_near, "core", [(0, 1), (1, 0)])
    w_shapes = [(CH, 9 * FIELDS), (3 * CH, 3 * CH), (48, 3 * CH), (CH, 144), (CH, 9 * CH)]
    w_in, w_mid, w_out, w_back_2, w_back_1 = call(
        weights_kernel,
        [VMEM] * 3,
        [(shape, BF16, VMEM) for shape in w_shapes[:3]]
        + [(shape, BF16, HBM) for shape in w_shapes[3:]],
        [(shape, F32) for shape in w_shapes] + [(shape, BF16) for shape in w_shapes[3:]],
        copies=2,
    )(place, kernel_in, kernel_mid, kernel_out)
    saved = [
        ((ROWS + 10, 3 * FIELDS, LON), BF16),
        ((ROWS + 8, CH, LON), BF16),
        ((ROWS, CH, LON), F32),
        ((ROWS + 6, CH, LON), BF16),
        ((ROWS + 2, CH, LON), F32),
    ]
    rows = FIXED_AT + HALF * ROWS
    fields_shape = ((MEMBERS, rows, LON), F32)
    kept_shape = ((4, WIDE, LON), F32)
    send, pushed, kept, stack, hidden_1, slope_1, hidden_2, slope_2 = call(
        forward_kernel,
        [VMEM] * 7,
        [fields_shape + (HBM,), ((VARS, ROWS, LON), F32, VMEM), kept_shape + (HBM,)]
        + [shape + (HBM,) for shape in saved],
        [((rows, LON), F32), kept_shape] + saved + [((2 * HALO, FIELDS, LON), F32)],
        copies=MEMBERS + 6,
        flops=10**9,
    )(place, far, near, own, members, w_in, w_mid, w_out)
    fields = lax.all_to_all(send, "member", 0, 0)
    partials_shape = ((TILES, MEMBERS, 128), F32)
    (partials,) = call(
        distance_kernel,
        [VMEM] * 3 + [HBM] * 2,
        [partials_shape + (HBM,)],
        [fields_shape, ((2, WIDE, LON), F32), partials_shape],
        copies=MEMBERS + 1,
    )(place, lat, members, observed, fields, kept)
    totals = lax.all_to_all(partials, TILE, 0, 0)
    mine, theirs = call(
        backward_kernel,
        [VMEM] * 2 + [HBM] * 9,
        [((MEMBERS * CHUNK, 128), F32, VMEM)] * 2,
        [fields_shape, kept_shape]
        + saved
        + [(shape, BF16) for shape in w_shapes[3:]]
        + [
            ((ROWS + 4, 48, LON), BF16),
            ((ROWS + 2, 3 * CH, LON), BF16),
            ((48, 3 * CH), F32),
            ((3 * CH, 3 * CH), F32),
            ((9 * FIELDS, CH), F32),
            ((6 * CH, 128), F32),
        ],
        copies=9,
        flops=10**9,
    )(
        place, lat, totals, fields, kept, stack, hidden_1, slope_1, hidden_2, slope_2,
        w_back_2, w_back_1,
    )
    swap = [(0, 1), (1, 0)]
    mine = mine + lax.ppermute(theirs, "core", swap)
    chunk = jnp.sum(lax.all_to_all(mine.reshape(MEMBERS, CHUNK, 128), "member", 0, 0), 0)
    chunk = jnp.sum(spread(chunk, "ring", RING), 0)
    half = spread(chunk, "member", MEMBERS).reshape(MEMBERS * CHUNK, 128)
    other = lax.ppermute(half, "core", swap)
    grad_in, grad_mid, grad_out, energy = call(
        unpack_kernel,
        [VMEM] * 2,
        [
            ((9, INPUTS, CH), F32, VMEM),
            ((9, CH, CH), F32, VMEM),
            ((9, VARS, CH), F32, VMEM),
            ((1, 1), F32, VMEM),
        ],
        [((6 * CH, 128), F32)],
    )(place, half, other)
    return (pushed[None], energy[0, 0], grad_in.transpose(0, 2, 1), grad_mid, grad_out)


def solution(mesh):
    fine = Mesh(mesh.devices.reshape(MEMBERS, -1, 2), ("member",) + TILE)
    in_specs = (
        P("member", None, TILE, None),
        P(None, TILE, None),
        P(None, TILE, None),
        P(),
        P(),
        P(),
    )
    out_specs = (P("member", None, TILE, None), P(), P(), P(), P())
    return jax.shard_map(
        per_device, mesh=fine, in_specs=in_specs, out_specs=out_specs, check_vma=False
    )
```

time: 126 us -> 122 us (0.968)
  blocking collectives: 30 us -> 51.3 us
  starting transfers between devices: 31.6 us -> 15.4 us
  local copies, waits for them, and re-layouts: 24.6 us -> 14.1 us
  Pallas kernels: 14.9 us -> 21.7 us
  waiting for transfers between devices: 22.7 us -> 17.5 us
    all_to_all x0 -> x1, blocking collectives: none -> 22.8 us  [per_device(): totals = lax.all_to_all(partials, TILE, 0, 0)]
    all_to_all x1 -> x0, starting transfers between devices: 14.5 us -> none  [per_device(): totals = lax.all_to_all(partials, TILE, 0, 0)]
    pallas_call x4 -> x6, Pallas kernels: 14.9 us -> 21.7 us  [the longest x1 8.84 us: per_device(): call(forward_kernel, [VMEM] * 7, [fields_shape + (HBM,), ((VARS, ROWS, LO...]
    all_to_all x1 -> x0, waiting for transfers between devices: 4.68 us -> none  [per_device(): totals = lax.all_to_all(partials, TILE, 0, 0)]
    ppermute x2, waiting for transfers between devices: 4.91 us -> 0.26 us  [the longest x1 0.26 us: per_device(): far = lax.ppermute(edge_far, TILE, across + [(j, i) for i, j in across])]
    all_to_all x1, waiting for transfers between devices: 11.1 us -> 15.2 us  [per_device(): fields = lax.all_to_all(send, 'member', 0, 0)]
    reshape x7 -> x0, local copies, waits for them, and re-layouts: 4.14 us -> none  [the longest x1 1.66 us: weights_of(): w_back_1 = taps_mid[::-1].transpose(3, 0, 1, 2).reshape(CH, 9 * CH)]
    rev x2 -> x0, local copies, waits for them, and re-layouts: 2.95 us -> none  [the longest x1 1.56 us: weights_of(): w_back_1 = taps_mid[::-1].transpose(3, 0, 1, 2).reshape(CH, 9 * CH)]
  transfers between devices with their start and end apart: 6 -> 5, of which waited for: 5 -> 4; matrix products, arithmetic and copies ran while one was open for 6% -> 1% of each run, Pallas kernels for 0% -> 1%
where the time goes in v3:
time: 122 us; the launch traced here: 121 us
  blocking collectives  51.3 us (42%)
  Pallas kernels  21.7 us (18%)
  waiting for transfers between devices  17.5 us (14%)
  starting transfers between devices  15.4 us (13%)
  local copies, waits for them, and re-layouts  14.1 us (12%)
    all_to_all x1, blocking collectives, per_device(): totals = lax.all_to_all(partials, TILE, 0, 0)  22.8 us
    all_to_all x2, blocking collectives, spread(): return lax.all_to_all(copies, axes, 0, 0)  20.9 us
    all_to_all x1, waiting for transfers between devices, per_device(): fields = lax.all_to_all(send, 'member', 0, 0)  15.2 us
    unnamed x35, local copies, waits for them, and re-layouts  13.3 us
    pallas_call x1, Pallas kernels, per_device(): call(forward_kernel, [VMEM] * 7, [fields_shape + (HBM,), ((VARS, ROWS, LO...  8.84 us
    all_to_all x1, blocking collectives, per_device(): lax.all_to_all(mine.reshape(MEMBERS, CHUNK, 128), 'member', 0, 0)  7.54 us
    pallas_call x1, Pallas kernels, per_device(): call(backward_kernel, [VMEM] * 2 + [HBM] * 9, [((MEMBERS * CHUNK, 128), F...  7.03 us
    ppermute x1, starting transfers between devices, per_device(): far = lax.ppermute(edge_far, TILE, across + [(j, i) for i, j in across])  6.21 us
  transfers between devices with their start and end apart: 5, of which 4 were waited for; matrix products, arithmetic and copies ran while one was open for 1% of the time, Pallas kernels for 1%

profile of v3, /device:TPU:1, one launch (start us, length us, event | category | flops | bytes accessed | tf_op | source)
XLA Modules:
  0.0 120.9 jit_solution(3068241588446289839)
XLA Ops:
  0.7 0.9 copy-done.9
  1.6 0.9 copy-done.12
  2.5 0.9 copy-done.15
  3.4 0.6 shard_map.110
  4.0 6.2 %collective-permute-start = (f32[5,16,512]{2,1,0:T(8,128)S(1)}, f32[5,16,512]{2,1,0:T(8,128)S(1)}, u32[]{:S(2)}, u32[]{:S(2)}) collective-permute-start(f32[5,16,512]{2,1,0:T(8,128)S(1)} %get-tuple-element.27), channel_id=1, source_target_pairs={{1,2},{3,4},{5,6},{7,8},{9,10},{11,12},{13,14},{15,16},{17,18},{19... | collective-permute-start | bytes 491528 | tf_op jit(solution)/shard_map/ppermute | solution.py:388
  10.4 0.9 copy.13.kernel_in
  11.3 0.9 copy-done.14
  12.2 0.7 copy-done.16
  12.9 1.1 shard_map.111
  14.3 0.9 copy-done.10
  15.2 8.8 %shard_map.112 = (f32[8,64,512]{2,1,0:T(8,128)S(1)}, f32[6,8,512]{2,1,0:T(8,128)}, f32[4,36,512]{2,1,0:T(8,128)S(1)}, bf16[18,48,512]{2,1,0:T(8,128)(2,1)S(1)}, ...) custom-call(s32[3]{0:T(128)S(1)} %pad_add_fusion.place, ...), custom_call_target="tpu_custom_call" | custom-call | flops 1000000000 | bytes 1000000 | tf_op jit(solution)/shard_map/pallas_call | solution.py:409
  24.0 1.0 copy-done
  25.0 1.0 copy-done.1
  26.0 1.0 copy-done.3
  27.0 0.9 copy-done.5
  27.9 0.9 copy-done.7
  28.8 4.3 %all-to-all-start = ((f32[8,64,512]{2,1,0:T(8,128)}), f32[8,64,512]{2,1,0:T(8,128)S(1)}, u32[]{:S(2)}, u32[]{:S(2)}) async-start(f32[8,64,512]{2,1,0:T(8,128)} %copy-done), calls=%async_computation | async-start | bytes 2097152 | tf_op jit(solution)/shard_map/all_to_all | solution.py:418
  33.1 0.7 dynamic-slice_bitcast_fusion
  33.8 15.2 %all-to-all-done.fields_in = f32[8,64,512]{2,1,0:T(8,128)S(1)} async-done(((f32[8,64,512]{2,1,0:T(8,128)}), f32[8,64,512]{2,1,0:T(8,128)S(1)}, u32[]{:S(2)}, u32[]{:S(2)}) %all-to-all-start) | async-done | bytes 1048608 | tf_op jit(solution)/shard_map/all_to_all | solution.py:418
  49.1 2.7 %shard_map.113 = f32[32,8,128]{2,1,0:T(8,128)S(1)} custom-call(s32[3]{0:T(128)S(1)} %pad_add_fusion.place, f32[48,128]{1,0:T(8,128)S(1)} %broadcast_in_dim.24.lat, f32[6,8,512]{2,1,0:T(8,128)S(1)} %bitcast.13, f32[6,8,512]{2,1,0:T(8,128)S(1)} %copy-done.13, f32[8,64,512]{2,1,0:T(8,128)S(1)} %all-to-all-done.fields_in, ...), custom_call_target="tpu_custom_call" | custom-call | flops 1000000 | bytes 1000000 | tf_op jit(solution)/shard_map/pallas_call | solution.py:420
  51.8 22.8 %all_to_all.25.totals = f32[32,8,128]{2,1,0:T(8,128)S(1)} all-to-all(f32[32,8,128]{2,1,0:T(8,128)S(1)} %shard_map.113), channel_id=1, replica_groups=mesh['member'=8,'ring'=16,'core'=2] {'ring','core'}, dimensions={0} | all-to-all | bytes 262144 | tf_op jit(solution)/shard_map/all_to_all | solution.py:427
  74.6 1.2 %copy-done.4 = f32[8,64,512]{2,1,0:T(8,128)S(1)} copy-done((f32[8,64,512]{2,1,0:T(8,128)S(1)}, f32[8,64,512]{2,1,0:T(8,128)}, u32[]{:S(2)}) %copy-start.4) | copy-done | bytes 1048600
  75.8 1.2 copy-done.8
  77.0 7.0 %shard_map.114 = (f32[192,128]{1,0:T(8,128)S(1)}, f32[192,128]{1,0:T(8,128)S(1)}) custom-call(s32[3]{0:T(128)S(1)} %pad_add_fusion.place, f32[48,128]{1,0:T(8,128)S(1)} %broadcast_in_dim.24.lat, f32[32,8,128]{2,1,0:T(8,128)S(1)} %all_to_all.25.totals, f32[8,64,512]{2,1,0:T(8,128)S(1)} %all-to-all-done.fields_in, ...), custom_call_target="tpu_custom_call" | custom-call | flops 1000000000 | bytes 1000000 | tf_op jit(solution)/shard_map/pallas_call | solution.py:428
  84.0 0.3 collective-permute-start.2
  84.4 1.1 collective-permute-done.2
  85.4 7.5 %all_to_all.26 = f32[8,24,128]{2,1,0:T(8,128)S(1)} all-to-all(f32[8,24,128]{2,1,0:T(8,128)S(1)} %bitcast.16), channel_id=1, replica_groups=mesh['member'=8,'ring'=16,'core'=2] {'member'}, dimensions={0} | all-to-all | bytes 196608 | tf_op jit(solution)/shard_map/all_to_all | solution.py:451
  93.0 13.3 %all_to_all.27 = f32[16,24,128]{2,1,0:T(8,128)S(1)} all-to-all(f32[16,24,128]{2,1,0:T(8,128)S(1)} %broadcast_in_dim.25), channel_id=1, replica_groups=mesh['member'=8,'ring'=16,'core'=2] {'ring'}, dimensions={0} | all-to-all | bytes 393216 | tf_op jit(solution)/shard_map/all_to_all | solution.py:29
  106.4 7.6 %all_to_all.28 = f32[8,24,128]{2,1,0:T(8,128)S(1)} all-to-all(f32[8,24,128]{2,1,0:T(8,128)S(1)} %broadcast_in_dim.26), channel_id=1, replica_groups=mesh['member'=8,'ring'=16,'core'=2] {'member'}, dimensions={0} | all-to-all | bytes 196608 | tf_op jit(solution)/shard_map/all_to_all | solution.py:29
  114.0 4.6 %collective-permute-start.3 = (f32[192,128]{1,0:T(8,128)S(1)}, f32[192,128]{1,0:T(8,128)S(1)}, u32[]{:S(2)}, u32[]{:S(2)}) collective-permute-start(f32[192,128]{1,0:T(8,128)S(1)} %bitcast.14), channel_id=1, source_target_pairs={{0,1},{1,0},{2,3},{3,2},{4,5},{5,4},{6,7},{7,6},{8,9},{9,8},{10,11... | collective-permute-start | bytes 294920 | tf_op jit(solution)/shard_map/ppermute | solution.py:454
  118.5 0.9 collective-permute-done.3.theirs
  119.5 1.4 %shard_map.115 = (f32[9,9,64]{2,1,0:T(8,128)}, f32[9,64,64]{2,1,0:T(8,128)}, f32[9,6,64]{2,1,0:T(8,128)}, f32[1,1]{1,0:T(1,128)}) custom-call(s32[3]{0:T(128)S(1)} %pad_add_fusion.place, f32[192,128]{1,0:T(8,128)S(1)} %bitcast.15, f32[192,128]{1,0:T(8,128)S(1)} %collective-permute-done.3.theirs), custom_call_target="tpu_custom_call" | custom-call | flops 1000000 | bytes 1000000 | tf_op jit(solution)/shard_map/pallas_call | solution.py:455
  (31 shorter events, 0.6 us)
Async XLA Ops:
  0.7 0.9 copy-start.9
  1.6 0.9 copy-start.12
  2.5 0.9 copy-start.15
  4.0 10.2 %collective-permute-start = (f32[5,16,512]{2,1,0:T(8,128)S(1)}, f32[5,16,512]{2,1,0:T(8,128)S(1)}, u32[]{:S(2)}, u32[]{:S(2)}) collective-permute-start(f32[5,16,512]{2,1,0:T(8,128)S(1)} %get-tuple-element.27), channel_id=1, source_target_pairs={{1,2},{3,4},{5,6},{7,8},{9,10},{11,12},{13,14},{15,16},{17,18},{19... | collective-permute-start | bytes 491528 | tf_op jit(solution)/shard_map/ppermute | solution.py:388
  10.3 4.0 %collective-permute-start.1 = (f32[5,16,512]{2,1,0:T(8,128)S(1)}, f32[5,16,512]{2,1,0:T(8,128)S(1)}, u32[]{:S(2)}, u32[]{:S(2)}) collective-permute-start(f32[5,16,512]{2,1,0:T(8,128)S(1)} %get-tuple-element.28), channel_id=1, source_target_pairs={{0,1},{1,0},{2,3},{3,2},{4,5},{5,4},{6,7},{7,6},{8,9},{9,8},{10,11... | collective-permute-start | bytes 491528 | tf_op jit(solution)/shard_map/ppermute | solution.py:389
  11.3 0.9 copy-start.14
  12.2 0.7 copy-start.16
  14.3 0.9 copy-start.10
  24.0 1.0 copy-start
  25.0 1.0 copy-start.1
  26.0 1.0 copy-start.3
  27.0 0.9 copy-start.5
  27.9 0.9 copy-start.7
  28.8 20.3 %copy-start.11 = (f32[1,6,8,512]{3,2,1,0:T(8,128)S(1)}, f32[1,6,8,512]{3,2,1,0:T(8,128)}, u32[]{:S(2)}) copy-start(f32[1,6,8,512]{3,2,1,0:T(8,128)} %param.7) | copy-start | bytes 294916
  28.8 20.3 %copy-start.13 = (f32[6,8,512]{2,1,0:T(8,128)S(1)}, f32[6,8,512]{2,1,0:T(8,128)}, u32[]{:S(2)}) copy-start(f32[6,8,512]{2,1,0:T(8,128)} %observed.3) | copy-start | bytes 294916
  28.8 20.2 %all-to-all-start = ((f32[8,64,512]{2,1,0:T(8,128)}), f32[8,64,512]{2,1,0:T(8,128)S(1)}, u32[]{:S(2)}, u32[]{:S(2)}) async-start(f32[8,64,512]{2,1,0:T(8,128)} %copy-done), calls=%async_computation | async-start | bytes 2097152 | tf_op jit(solution)/shard_map/all_to_all | solution.py:418
  49.0 25.6 %copy-start.2 = (bf16[16,64,512]{2,1,0:T(8,128)(2,1)S(1)}, bf16[16,64,512]{2,1,0:T(8,128)(2,1)}, u32[]{:S(2)}) copy-start(bf16[16,64,512]{2,1,0:T(8,128)(2,1)} %copy-done.1) | copy-start | bytes 3145732
  49.0 25.6 %copy-start.6 = (bf16[14,64,512]{2,1,0:T(8,128)(2,1)S(1)}, bf16[14,64,512]{2,1,0:T(8,128)(2,1)}, u32[]{:S(2)}) copy-start(bf16[14,64,512]{2,1,0:T(8,128)(2,1)} %copy-done.5) | copy-start | bytes 2752516
  74.6 1.2 %copy-start.4 = (f32[8,64,512]{2,1,0:T(8,128)S(1)}, f32[8,64,512]{2,1,0:T(8,128)}, u32[]{:S(2)}) copy-start(f32[8,64,512]{2,1,0:T(8,128)} %copy-done.3) | copy-start | bytes 3145732
  75.8 1.2 copy-start.8
  84.0 1.4 %collective-permute-start.2 = (f32[192,128]{1,0:T(8,128)S(1)}, f32[192,128]{1,0:T(8,128)S(1)}, u32[]{:S(2)}, u32[]{:S(2)}) collective-permute-start(f32[192,128]{1,0:T(8,128)S(1)} %get-tuple-element.44), channel_id=1, source_target_pairs={{0,1},{1,0},{2,3},{3,2},{4,5},{5,4},{6,7},{7,6},{8,9},{9,8},{10,11... | collective-permute-start | bytes 294920 | tf_op jit(solution)/shard_map/ppermute | solution.py:450
  114.0 5.5 %collective-permute-start.3 = (f32[192,128]{1,0:T(8,128)S(1)}, f32[192,128]{1,0:T(8,128)S(1)}, u32[]{:S(2)}, u32[]{:S(2)}) collective-permute-start(f32[192,128]{1,0:T(8,128)S(1)} %bitcast.14), channel_id=1, source_target_pairs={{0,1},{1,0},{2,3},{3,2},{4,5},{5,4},{6,7},{7,6},{8,9},{9,8},{10,11... | collective-permute-start | bytes 294920 | tf_op jit(solution)/shard_map/ppermute | solution.py:454

commit v4 on v3

--- a/solution.py
+++ b/solution.py
@@ -85,13 +85,14 @@
     place, kernel_in, kernel_mid, kernel_out, w_in, w_mid, w_out, w_back_2, w_back_1,
     flat_in, square, flat_out, back_2, back_1, held_2, held_1, sems,
 ):
-    flat_in[...] = jnp.zeros_like(flat_in)
     flat_out[...] = jnp.zeros_like(flat_out)
     back_2[...] = jnp.zeros_like(back_2)
     for tap in range(9):
         a, b = tap // 3, tap % 3
         back = 3 * (2 - a) + b
-        flat_in[:, tap * FIELDS : tap * FIELDS + INPUTS] = kernel_in[tap].astype(F32)
+        first = kernel_in[tap].astype(F32)
+        first = jnp.concatenate([first, jnp.zeros((FIELDS - INPUTS, CH), F32)], 0).T
+        flat_in[:, tap * FIELDS : (tap + 1) * FIELDS] = first
         mid = kernel_mid[tap].astype(F32)
         square[b * CH : (b + 1) * CH, a * CH : (a + 1) * CH] = mid
         back_1[:, back * CH : (back + 1) * CH] = mid.T
@@ -352,12 +353,12 @@
     energy[...] = packed[6 * CH - 1 :, 127:]
 
 
-VMEM_LIMIT = 32 * 2**20
+VMEM_LIMIT = 60 * 10**6
 VMEM = pl.BlockSpec(memory_space=pltpu.VMEM)
 HBM = pl.BlockSpec(memory_space=pltpu.HBM)
 
 
-def call(kernel, ins, outs, scratch=(), copies=0, flops=10**6):
+def call(kernel, ins, outs, scratch=(), copies=0, flops=10**6, vmem=VMEM_LIMIT):
     held = [pltpu.VMEM(shape, dtype) for shape, dtype in scratch]
     if copies > 0:
         held.append(pltpu.SemaphoreType.DMA((copies,)))
@@ -367,7 +368,7 @@
         in_specs=[pl.BlockSpec(memory_space=pltpu.SMEM)] + ins,
         out_specs=[spec for shape, dtype, spec in outs],
         scratch_shapes=held,
-        compiler_params=pltpu.CompilerParams(vmem_limit_bytes=VMEM_LIMIT),
+        compiler_params=pltpu.CompilerParams(vmem_limit_bytes=vmem),
         cost_estimate=pl.CostEstimate(flops=flops, bytes_accessed=10**6, transcendentals=0),
     )
 
@@ -395,7 +396,7 @@
         + [(shape, BF16, HBM) for shape in w_shapes[3:]],
         [(shape, F32) for shape in w_shapes] + [(shape, BF16) for shape in w_shapes[3:]],
         copies=2,
-    )(place, kernel_in, kernel_mid, kernel_out)
+    )(place, kernel_in.transpose(0, 2, 1), kernel_mid, kernel_out)
     saved = [
         ((ROWS + 10, 3 * FIELDS, LON), BF16),
         ((ROWS + 8, CH, LON), BF16),
@@ -462,6 +463,7 @@
             ((1, 1), F32, VMEM),
         ],
         [((6 * CH, 128), F32)],
+        vmem=16 * 10**6,
     )(place, half, other)
     return (pushed[None], energy[0, 0], grad_in.transpose(0, 2, 1), grad_mid, grad_out)
 

time: 122 us -> 117 us (0.959)
  local copies, waits for them, and re-layouts: 14.1 us -> 2.43 us
  Pallas kernels: 21.7 us -> 26.3 us
  waiting for transfers between devices: 17.5 us -> 20.1 us
  other arithmetic: 0.12 us -> 1.6 us
    unnamed x35 -> x8, local copies, waits for them, and re-layouts: 13.3 us -> 0.94 us
    pallas_call x1, Pallas kernels: 1.07 us -> 2.61 us  [per_device(): call(weights_kernel, [VMEM] * 3, [(shape, BF16, VMEM) for shape in w_shap...]
    pallas_call x1, Pallas kernels: 7.03 us -> 8.48 us  [per_device(): call(backward_kernel, [VMEM] * 2 + [HBM] * 9, [((MEMBERS * CHUNK, 128), F...]
    ppermute x1, waiting for transfers between devices: 0.26 us -> 1.59 us  [per_device(): far = lax.ppermute(edge_far, TILE, across + [(j, i) for i, j in across])]
    pallas_call x1, Pallas kernels: 0.64 us -> 1.88 us  [per_device(): call(pack_kernel, [VMEM] * 3, [((ROWS, FIELDS, LON), F32, VMEM), edge, ed...]
  transfers between devices with their start and end apart: 5 -> 5, of which waited for: 4 -> 4; matrix products, arithmetic and copies ran while one was open for 1% -> 1% of each run, Pallas kernels for 1% -> 2%
where the time goes in v4:
time: 117 us
  blocking collectives  50.5 us (43%)
  Pallas kernels  26.3 us (22%)
  waiting for transfers between devices  20.1 us (17%)
  starting transfers between devices  15.3 us (13%)
  local copies, waits for them, and re-layouts  2.43 us (2%)
  other arithmetic  1.6 us (1%)
    all_to_all x1, blocking collectives, per_device(): totals = lax.all_to_all(partials, TILE, 0, 0)  22 us
    all_to_all x2, blocking collectives, spread(): return lax.all_to_all(copies, axes, 0, 0)  20.9 us
    all_to_all x1, waiting for transfers between devices, per_device(): fields = lax.all_to_all(send, 'member', 0, 0)  16.2 us
    pallas_call x1, Pallas kernels, per_device(): call(forward_kernel, [VMEM] * 7, [fields_shape + (HBM,), ((VARS, ROWS, LO...  8.85 us
    pallas_call x1, Pallas kernels, per_device(): call(backward_kernel, [VMEM] * 2 + [HBM] * 9, [((MEMBERS * CHUNK, 128), F...  8.48 us
    all_to_all x1, blocking collectives, per_device(): lax.all_to_all(mine.reshape(MEMBERS, CHUNK, 128), 'member', 0, 0)  7.54 us
    ppermute x1, starting transfers between devices, per_device(): far = lax.ppermute(edge_far, TILE, across + [(j, i) for i, j in across])  6.2 us
    ppermute x1, starting transfers between devices, per_device(): other = lax.ppermute(half, 'core', swap)  4.56 us
  transfers between devices with their start and end apart: 5, of which 4 were waited for; matrix products, arithmetic and copies ran while one was open for 1% of the time, Pallas kernels for 2%

profile of v4, /device:TPU:1, one launch (start us, length us, event | category | flops | bytes accessed | tf_op | source)
XLA Modules:
  0.0 116.9 jit_solution(16461510106021127395)
XLA Ops:
  0.6 0.7 pad_add_fusion.place
  1.3 1.9 %shard_map.110 = (f32[8,16,512]{2,1,0:T(8,128)}, f32[5,16,512]{2,1,0:T(8,128)}, f32[5,16,512]{2,1,0:T(8,128)}) custom-call(s32[3]{0:T(128)} %pad_add_fusion.place, f32[6,8,512]{2,1,0:T(8,128)} %bitcast.14, f32[6,8,512]{2,1,0:T(8,128)} %condition.1, f32[6,8,512]{2,1,0:T(8,128)} %observed.3), custom_call_target="tpu_custom_call" | custom-call | flops 1000000 | bytes 1000000 | tf_op jit(solution)/shard_map/pallas_call | solution.py:385
  3.2 6.2 %collective-permute-start = (f32[5,16,512]{2,1,0:T(8,128)}, f32[5,16,512]{2,1,0:T(8,128)S(1)}, u32[]{:S(2)}, u32[]{:S(2)}) collective-permute-start(f32[5,16,512]{2,1,0:T(8,128)} %get-tuple-element.27), channel_id=1, source_target_pairs={{1,2},{3,4},{5,6},{7,8},{9,10},{11,12},{13,14},{15,16},{17,18},{19... | collective-permute-start | bytes 491528 | tf_op jit(solution)/shard_map/ppermute | solution.py:389
  9.4 0.1 collective-permute-start.1
  9.5 2.6 %shard_map.111 = (bf16[64,144]{1,0:T(8,128)(2,1)}, bf16[192,192]{1,0:T(8,128)(2,1)}, bf16[48,192]{1,0:T(8,128)(2,1)}, bf16[64,144]{1,0:T(8,128)(2,1)}, bf16[64,576]{1,0:T(8,128)(2,1)}) custom-call(s32[3]{0:T(128)} %pad_add_fusion.place, bf16[9,9,64]{2,1,0:T(8,128)(2,1)} %bitcast.18, bf16[9,64,64]{2,1,0:T(8,128)(2,1)} %kernel_mid.1, bf16[9,6,64]{2,1,0:T(8,128)(2,1)} %kernel_out.1), custom_call_target="tpu_custom_call" | custom-call | flops 1000000 | bytes 1000000 | tf_op jit(solution)/shard_map/pallas_call | solution.py:392
  12.1 1.6 %collective-permute-done.far = f32[5,16,512]{2,1,0:T(8,128)S(1)} collective-permute-done((f32[5,16,512]{2,1,0:T(8,128)}, f32[5,16,512]{2,1,0:T(8,128)S(1)}, u32[]{:S(2)}, u32[]{:S(2)}) %collective-permute-start) | collective-permute-done | bytes 163872 | tf_op jit(solution)/shard_map/ppermute | solution.py:389
  13.7 0.0 copy-start.2
  13.7 0.0 collective-permute-done.1.near
  13.7 0.0 copy-start.3
  13.7 0.7 copy-done.2
  14.4 0.1 copy-done.3
  14.4 8.8 %shard_map.112 = (f32[8,64,512]{2,1,0:T(8,128)}, f32[6,8,512]{2,1,0:T(8,128)}, f32[4,36,512]{2,1,0:T(8,128)}, bf16[18,48,512]{2,1,0:T(8,128)(2,1)}, bf16[16,64,5...) custom-call(s32[3]{0:T(128)} %pad_add_fusion.place, ...), custom_call_target="tpu_custom_call" | custom-call | flops 1000000000 | bytes 1000000 | tf_op jit(solution)/shard_map/pallas_call | solution.py:410
  23.3 4.1 %all-to-all-start = ((f32[8,64,512]{2,1,0:T(8,128)}), f32[8,64,512]{2,1,0:T(8,128)S(1)}, u32[]{:S(2)}, u32[]{:S(2)}) async-start(f32[8,64,512]{2,1,0:T(8,128)} %get-tuple-element.34), calls=%async_computation | async-start | bytes 2097152 | tf_op jit(solution)/shard_map/all_to_all | solution.py:419
  27.4 0.7 dynamic-slice_bitcast_fusion
  28.1 16.2 %all-to-all-done.fields_in = f32[8,64,512]{2,1,0:T(8,128)S(1)} async-done(((f32[8,64,512]{2,1,0:T(8,128)}), f32[8,64,512]{2,1,0:T(8,128)S(1)}, u32[]{:S(2)}, u32[]{:S(2)}) %all-to-all-start) | async-done | bytes 1048608 | tf_op jit(solution)/shard_map/all_to_all | solution.py:419
  44.4 0.0 copy-start.1
  44.4 0.8 broadcast_in_dim.24.lat
  45.1 0.2 copy-done.1
  45.3 3.1 %shard_map.113 = f32[32,8,128]{2,1,0:T(8,128)} custom-call(s32[3]{0:T(128)} %pad_add_fusion.place, f32[48,128]{1,0:T(8,128)} %broadcast_in_dim.24.lat, f32[6,8,512]{2,1,0:T(8,128)} %bitcast.16, f32[6,8,512]{2,1,0:T(8,128)} %observed.3, f32[8,64,512]{2,1,0:T(8,128)} %copy-done.1, f32[4,36,512]{2,1,0:T(8,128)} %get-tuple-element.35.kept_in), custom_call_target="tpu_custom_call" | custom-call | flops 1000000 | bytes 1000000 | tf_op jit(solution)/shard_map/pallas_call | solution.py:421
  48.4 22.0 %all_to_all.25.totals = f32[32,8,128]{2,1,0:T(8,128)} all-to-all(f32[32,8,128]{2,1,0:T(8,128)} %shard_map.113), channel_id=1, replica_groups=mesh['member'=8,'ring'=16,'core'=2] {'ring','core'}, dimensions={0} | all-to-all | bytes 262144 | tf_op jit(solution)/shard_map/all_to_all | solution.py:428
  70.4 8.5 %shard_map.114 = (f32[192,128]{1,0:T(8,128)}, f32[192,128]{1,0:T(8,128)}) custom-call(s32[3]{0:T(128)} %pad_add_fusion.place, f32[48,128]{1,0:T(8,128)} %broadcast_in_dim.24.lat, f32[32,8,128]{2,1,0:T(8,128)} %all_to_all.25.totals, f32[8,64,512]{2,1,0:T(8,128)} %copy-done.1, f32[4,36,512]{2,1,0:T(8,128)} %get-tuple-element.35.kept_in, ...), custom_call_target="tpu_custom_call" | custom-call | flops 1000000000 | bytes 1000000 | tf_op jit(solution)/shard_map/pallas_call | solution.py:429
  78.9 0.0 copy-start
  78.9 0.3 collective-permute-start.2
  79.2 1.3 %collective-permute-done.2 = f32[192,128]{1,0:T(8,128)S(1)} collective-permute-done((f32[192,128]{1,0:T(8,128)}, f32[192,128]{1,0:T(8,128)S(1)}, u32[]{:S(2)}, u32[]{:S(2)}) %collective-permute-start.2) | collective-permute-done | bytes 98336 | tf_op jit(solution)/shard_map/ppermute | solution.py:451
  80.5 0.9 add.11
  81.4 7.5 %all_to_all.26 = f32[8,24,128]{2,1,0:T(8,128)S(1)} all-to-all(f32[8,24,128]{2,1,0:T(8,128)S(1)} %bitcast.17), channel_id=1, replica_groups=mesh['member'=8,'ring'=16,'core'=2] {'member'}, dimensions={0} | all-to-all | bytes 196608 | tf_op jit(solution)/shard_map/all_to_all | solution.py:452
  89.0 13.3 %all_to_all.27 = f32[16,24,128]{2,1,0:T(8,128)S(1)} all-to-all(f32[16,24,128]{2,1,0:T(8,128)S(1)} %broadcast_in_dim.25), channel_id=1, replica_groups=mesh['member'=8,'ring'=16,'core'=2] {'ring'}, dimensions={0} | all-to-all | bytes 393216 | tf_op jit(solution)/shard_map/all_to_all | solution.py:29
  102.4 7.6 %all_to_all.28 = f32[8,24,128]{2,1,0:T(8,128)S(1)} all-to-all(f32[8,24,128]{2,1,0:T(8,128)S(1)} %broadcast_in_dim.26), channel_id=1, replica_groups=mesh['member'=8,'ring'=16,'core'=2] {'member'}, dimensions={0} | all-to-all | bytes 196608 | tf_op jit(solution)/shard_map/all_to_all | solution.py:29
  110.0 4.6 %collective-permute-start.3 = (f32[192,128]{1,0:T(8,128)S(1)}, f32[192,128]{1,0:T(8,128)S(1)}, u32[]{:S(2)}, u32[]{:S(2)}) collective-permute-start(f32[192,128]{1,0:T(8,128)S(1)} %bitcast.12), channel_id=1, source_target_pairs={{0,1},{1,0},{2,3},{3,2},{4,5},{5,4},{6,7},{7,6},{8,9},{9,8},{10,11... | collective-permute-start | bytes 294920 | tf_op jit(solution)/shard_map/ppermute | solution.py:455
  114.5 0.9 collective-permute-done.3.theirs
  115.5 0.0 copy-done
  115.5 1.4 %shard_map.115 = (f32[9,9,64]{2,1,0:T(8,128)}, f32[9,64,64]{2,1,0:T(8,128)}, f32[9,6,64]{2,1,0:T(8,128)}, f32[1,1]{1,0:T(1,128)}) custom-call(s32[3]{0:T(128)S(1)} %copy-done, f32[192,128]{1,0:T(8,128)S(1)} %bitcast.13, f32[192,128]{1,0:T(8,128)S(1)} %collective-permute-done.3.theirs), custom_call_target="tpu_custom_call" | custom-call | flops 1000000 | bytes 1000000 | tf_op jit(solution)/shard_map/pallas_call | solution.py:456
  (4 shorter events, 0.1 us)
Async XLA Ops:
  3.2 10.5 %collective-permute-start = (f32[5,16,512]{2,1,0:T(8,128)}, f32[5,16,512]{2,1,0:T(8,128)S(1)}, u32[]{:S(2)}, u32[]{:S(2)}) collective-permute-start(f32[5,16,512]{2,1,0:T(8,128)} %get-tuple-element.27), channel_id=1, source_target_pairs={{1,2},{3,4},{5,6},{7,8},{9,10},{11,12},{13,14},{15,16},{17,18},{19... | collective-permute-start | bytes 491528 | tf_op jit(solution)/shard_map/ppermute | solution.py:389
  9.4 4.3 %collective-permute-start.1 = (f32[5,16,512]{2,1,0:T(8,128)}, f32[5,16,512]{2,1,0:T(8,128)S(1)}, u32[]{:S(2)}, u32[]{:S(2)}) collective-permute-start(f32[5,16,512]{2,1,0:T(8,128)} %get-tuple-element.28), channel_id=1, source_target_pairs={{0,1},{1,0},{2,3},{3,2},{4,5},{5,4},{6,7},{7,6},{8,9},{9,8},{10,11... | collective-permute-start | bytes 491528 | tf_op jit(solution)/shard_map/ppermute | solution.py:390
  13.7 0.7 copy-start.2
  13.7 0.7 copy-start.3
  23.3 21.1 %all-to-all-start = ((f32[8,64,512]{2,1,0:T(8,128)}), f32[8,64,512]{2,1,0:T(8,128)S(1)}, u32[]{:S(2)}, u32[]{:S(2)}) async-start(f32[8,64,512]{2,1,0:T(8,128)} %get-tuple-element.34), calls=%async_computation | async-start | bytes 2097152 | tf_op jit(solution)/shard_map/all_to_all | solution.py:419
  44.4 1.0 copy-start.1
  78.9 36.6 %copy-start = (s32[3]{0:T(128)S(1)}, s32[3]{0:T(128)}, u32[]{:S(2)}) copy-start(s32[3]{0:T(128)} %pad_add_fusion.place) | copy-start | bytes 40
  78.9 1.6 %collective-permute-start.2 = (f32[192,128]{1,0:T(8,128)}, f32[192,128]{1,0:T(8,128)S(1)}, u32[]{:S(2)}, u32[]{:S(2)}) collective-permute-start(f32[192,128]{1,0:T(8,128)} %get-tuple-element.44), channel_id=1, source_target_pairs={{0,1},{1,0},{2,3},{3,2},{4,5},{5,4},{6,7},{7,6},{8,9},{9,8},{10,11... | collective-permute-start | bytes 294920 | tf_op jit(solution)/shard_map/ppermute | solution.py:451
  110.0 5.5 %collective-permute-start.3 = (f32[192,128]{1,0:T(8,128)S(1)}, f32[192,128]{1,0:T(8,128)S(1)}, u32[]{:S(2)}, u32[]{:S(2)}) collective-permute-start(f32[192,128]{1,0:T(8,128)S(1)} %bitcast.12), channel_id=1, source_target_pairs={{0,1},{1,0},{2,3},{3,2},{4,5},{5,4},{6,7},{7,6},{8,9},{9,8},{10,11... | collective-permute-start | bytes 294920 | tf_op jit(solution)/shard_map/ppermute | solution.py:455

commit v5 on v4

--- a/solution.py
+++ b/solution.py
@@ -64,17 +64,17 @@
 
 
 def loop(start, stop, body):
-    lax.fori_loop(start, stop, lambda row, carry: (body(row), carry)[1], 0, unroll=2)
-
-
-def pack_kernel(place, members, condition, observed, own, edge_far, edge_near):
+    lax.fori_loop(start, stop, lambda row, carry: (body(row), carry)[1], 0, unroll=True)
+
+
+def pack_kernel(members, condition, observed, own, edge_far, edge_near):
     for row in range(ROWS):
         own[row, :HALF, :] = members[:HALF, row, :]
         own[row, HALF:INPUTS, :] = condition[:, row, :]
         own[row, INPUTS : INPUTS + HALF, :] = members[HALF:, row, :]
         own[row, INPUTS + HALF : INPUTS + 2 * HALF, :] = observed[HALF:, row, :]
         own[row, FIELDS - 1 :, :] = jnp.zeros((1, LON), F32)
-    odd = place[2] == 1
+    odd = lax.axis_index("core") == 1
     for row in range(HALO):
         initial, last = own[row], own[ROWS - HALO + row]
         edge_far[row] = jnp.where(odd, last, initial)
@@ -82,7 +82,7 @@
 
 
 def weights_kernel(
-    place, kernel_in, kernel_mid, kernel_out, w_in, w_mid, w_out, w_back_2, w_back_1,
+    kernel_in, kernel_mid, kernel_out, w_in, w_mid, w_out, w_back_2, w_back_1,
     flat_in, square, flat_out, back_2, back_1, held_2, held_1, sems,
 ):
     flat_out[...] = jnp.zeros_like(flat_out)
@@ -95,7 +95,7 @@
         flat_in[:, tap * FIELDS : (tap + 1) * FIELDS] = first
         mid = kernel_mid[tap].astype(F32)
         square[b * CH : (b + 1) * CH, a * CH : (a + 1) * CH] = mid
-        back_1[:, back * CH : (back + 1) * CH] = mid.T
+        back_1[a * CH : (a + 1) * CH, b * CH : (b + 1) * CH] = mid.T
         out = kernel_out[tap].astype(F32)
         across = slice(a * CH, (a + 1) * CH)
         flat_out[b * 16 : b * 16 + HALF, across] = out[:HALF]
@@ -146,7 +146,7 @@
         for shift in range(3):
             part = turned(field, 1 - shift).astype(BF16)
             stack[row, shift * FIELDS : (shift + 1) * FIELDS, :] = part
-    keep(stack, stack_out)
+    keep(stack.at[4:14], stack_out)
 
     def first(row, kept_row):
         pre = dot(w_in[...], stack[pl.ds(row, 3)].reshape(9 * FIELDS, LON))
@@ -158,7 +158,7 @@
     loop(0, 4, functools.partial(first, kept_row=False))
     loop(4, 12, functools.partial(first, kept_row=True))
     loop(12, 16, functools.partial(first, kept_row=False))
-    keep(hidden_1, hidden_1_out)
+    keep(hidden_1.at[3:13], hidden_1_out)
     keep(slope_1, slope_1_out)
 
     def second(row, kept_row):
@@ -172,7 +172,7 @@
     loop(0, 2, functools.partial(second, kept_row=False))
     loop(2, 12, functools.partial(second, kept_row=True))
     loop(12, 14, functools.partial(second, kept_row=False))
-    keep(hidden_2, hidden_2_out)
+    keep(hidden_2.at[2:12], hidden_2_out)
     keep(slope_2, slope_2_out)
 
     send[WIDE:FIXED_AT, :] = jnp.zeros((FIXED_AT - WIDE, LON), F32)
@@ -205,58 +205,55 @@
     return sum(value[..., at : at + 128] for at in range(0, LON, 128))
 
 
-def distance_kernel(
-    place, lat, members, observed, fields_in, kept_in, partials_out, fields, kept, partials, sems
-):
-    copies = [pltpu.make_async_copy(kept_in.at[2:4], kept, sems.at[MEMBERS])]
-    for n in range(MEMBERS):
-        copies.append(pltpu.make_async_copy(fields_in.at[n], fields.at[n], sems.at[n]))
-    for copy in copies:
-        copy.start()
+def distance_kernel(place, lat, members, observed, fields, kept, partials):
     me = place[0]
     spot = lax.broadcasted_iota(jnp.int32, (WIDE, 1), 0)
     wide = jnp.where((spot >= 2 * HALF) & (spot < WIDE - 2 * HALF), lat[:WIDE, :1], 0.0)
     low = jnp.concatenate([lat[FIXED_AT:, :1]] * HALF, 0)
     fixed_mine = members[:HALF].reshape(HALF * ROWS, LON)
-    copies[0].wait()
-    mine = kept[1]
+    mine = kept[3]
 
     def weighed(moved, fixed):
         upper = jnp.sum(folded(wide * (mine - moved) ** 2), 0, keepdims=True)
         lower = jnp.sum(folded(low * (fixed_mine - fixed) ** 2), 0, keepdims=True)
         return upper + lower
 
-    rows = [weighed(kept[0], observed[:HALF].reshape(HALF * ROWS, LON))]
-    for n in range(MEMBERS):
-        copies[1 + n].wait()
-        rows.append(weighed(fields[n, :WIDE], fields[n, FIXED_AT:]))
-    all_rows = jnp.concatenate(rows[1:], 0)
+    to_observed = weighed(kept[2], observed[:HALF].reshape(HALF * ROWS, LON))
+    rows = [weighed(fields[n, :WIDE], fields[n, FIXED_AT:]) for n in range(MEMBERS)]
+    all_rows = jnp.concatenate(rows, 0)
     spot = lax.broadcasted_iota(jnp.int32, (MEMBERS, 128), 0)
-    all_rows = jnp.where(spot == me, rows[0], all_rows)
-    for tile in range(TILES):
-        partials[tile] = all_rows
-    copy = pltpu.make_async_copy(partials, partials_out, sems.at[0])
-    copy.start()
-    copy.wait()
+    partials[...] = jnp.where(spot == me, to_observed, all_rows)
+
+
+def started(pairs, sems):
+    copies = [
+        pltpu.make_async_copy(source, target, sems.at[at])
+        for at, (source, target) in enumerate(pairs)
+    ]
+    for copy in copies:
+        copy.start()
+    return copies
 
 
 def backward_kernel(
-    place, lat, totals, fields_in, kept_in, stack_in, hidden_1_in, slope_1_in, hidden_2_in,
+    place, lat_in, totals_in, fields_in, kept_in, stack_in, hidden_1_in, slope_1_in, hidden_2_in,
     slope_2_in, w_back_2_in, w_back_1_in,
     mine, theirs,
-    fields, kept, stack, hidden_1, slope_1, hidden_2, slope_2, w_back_2, w_back_1,
-    coupled, turned_2, sum_out, sum_mid, sum_in, packed, sems,
+    lat, totals, fields, kept, stack, hidden_1, slope_1, hidden_2, slope_2, w_back_2, w_back_1,
+    coupled, turned_2, by_row, sum_out, sum_mid, sum_in, packed, sems,
 ):
-    sources = [kept_in, fields_in, w_back_2_in, slope_2_in, hidden_2_in, hidden_1_in]
-    sources += [w_back_1_in, slope_1_in, stack_in]
-    targets = [kept, fields, w_back_2, slope_2, hidden_2, hidden_1, w_back_1, slope_1, stack]
-    copies = []
-    for source, target in zip(sources, targets):
-        copies.append(pltpu.make_async_copy(source, target, sems.at[len(copies)]))
-        copies[-1].start()
+    sources = [totals_in, lat_in, kept_in, fields_in.at[:, :FIXED_AT], w_back_2_in, slope_2_in]
+    sources += [w_back_1_in, hidden_1_in, hidden_2_in, slope_1_in, stack_in]
+    targets = [totals, lat, kept, fields, w_back_2, slope_2]
+    targets += [w_back_1, hidden_1, hidden_2, slope_1, stack]
+    copies = started(list(zip(sources, targets)), sems)
     me, base, core = place[0], place[1], place[2]
+    sum_out[...] = jnp.zeros_like(sum_out)
+    sum_mid[...] = jnp.zeros_like(sum_mid)
+    sum_in[...] = jnp.zeros_like(sum_in)
+    copies[0].wait()
     total = totals[0]
-    for tile in range(1, TILES):
+    for tile in range(1, RING):
         total = total + totals[tile]
     distances = jnp.sqrt(jnp.sum(total, 1, keepdims=True) / ENTRIES + EPSILON)
     is_me = lax.broadcasted_iota(jnp.int32, (MEMBERS, 1), 0) == me
@@ -265,13 +262,11 @@
     weights = 1.0 / (jnp.where(is_me, MEMBERS, MEMBERS * MEMBERS) * distances)
     own_weight = jnp.sum(jnp.where(is_me, weights, 0.0), 0, keepdims=True)
     weights = jnp.where(is_me, 0.0, weights)
-    sum_out[...] = jnp.zeros_like(sum_out)
-    sum_mid[...] = jnp.zeros_like(sum_mid)
-    sum_in[...] = jnp.zeros_like(sum_in)
-    copies[0].wait()
+    copies[1].wait()
+    copies[2].wait()
     log_scale, moving, observed, moved = kept[0], kept[1], kept[2], kept[3]
     inner = (moved - observed) * own_weight
-    copies[1].wait()
+    copies[3].wait()
     for n in range(MEMBERS):
         inner = inner - weights[n : n + 1] * (moved - fields[n, :WIDE])
     upper = lat[:WIDE, :1] * inner / math.sqrt(ENTRIES)
@@ -283,8 +278,8 @@
         for shift in range(3):
             part = turned(field, shift - 1).astype(BF16)
             coupled[row, shift * 16 : (shift + 1) * 16, :] = part
-    copies[2].wait()
-    copies[3].wait()
+    copies[4].wait()
+    copies[5].wait()
 
     def second(row):
         back = dot(w_back_2[...], coupled[pl.ds(row, 3)].reshape(144, LON))
@@ -294,18 +289,34 @@
             turned_2[row, shift * CH : (shift + 1) * CH, :] = part
 
     loop(0, ROWS + 2, second)
-    for copy in copies[4:]:
-        copy.wait()
+    copies[6].wait()
+
+    def across_rows(row):
+        by_row[row] = dot(w_back_1[...], turned_2[row])
+
+    loop(0, ROWS + 2, across_rows)
+    copies[7].wait()
+
+    def middle(row):
+        near = hidden_1[pl.ds(row, 3)].reshape(3 * CH, LON)
+        sum_mid[...] += dot_cells(turned_2[row + 1], near)
+
+    loop(0, ROWS, middle)
+    copies[8].wait()
+
+    def outer(row):
+        near = hidden_2[pl.ds(row, 3)].reshape(3 * CH, LON)
+        sum_out[...] += dot_cells(coupled[row + 2], near)
+
+    loop(0, ROWS, outer)
+    copies[9].wait()
+    copies[10].wait()
 
     def last(row):
-        near_2 = hidden_2[pl.ds(row + 2, 3)].reshape(3 * CH, LON)
-        sum_out[...] += dot_cells(coupled[row + 2], near_2)
-        near_1 = hidden_1[pl.ds(row + 3, 3)].reshape(3 * CH, LON)
-        sum_mid[...] += dot_cells(turned_2[row + 1], near_1)
-        back = dot(w_back_1[...], turned_2[pl.ds(row, 3)].reshape(9 * CH, LON))
+        back = by_row[row + 2, :CH] + by_row[row + 1, CH : 2 * CH] + by_row[row, 2 * CH :]
         grad = (back * slope_1[row]).astype(BF16)
-        near_0 = stack[pl.ds(row + 4, 3)].reshape(9 * FIELDS, LON)
-        sum_in[...] += dot_cells(near_0, grad)
+        near = stack[pl.ds(row, 3)].reshape(9 * FIELDS, LON)
+        sum_in[...] += dot_cells(near, grad)
 
     loop(0, ROWS, last)
     packed[5 * CH :, :] = jnp.zeros((CH, 128), F32)
@@ -334,15 +345,14 @@
     return (tap * CH, slice(0, CH)) if tap < 5 else ((tap - 5) * CH, slice(CH, 2 * CH))
 
 
-def unpack_kernel(place, mine, theirs, grad_in, grad_mid, grad_out, energy, packed):
-    half = MEMBERS * CHUNK
-    for copy in range(2):
-
-        @pl.when(place[2] == copy)
-        def _():
-            packed[copy * half : (copy + 1) * half, :] = mine[...]
-            packed[(1 - copy) * half : (2 - copy) * half, :] = theirs[...]
-
+def unpack_kernel(place, chunks, grad_in, grad_mid, grad_out, energy, packed):
+    core = place[2]
+    for member in range(MEMBERS):
+        first, second = chunks[member, 0], chunks[member, 1]
+        at = member * CHUNK
+        packed[at : at + CHUNK, :] = jnp.where(core == 0, first, second)
+        at += MEMBERS * CHUNK
+        packed[at : at + CHUNK, :] = jnp.where(core == 0, second, first)
     for tap in range(9):
         at, side = place_mid(tap)
         grad_mid[tap] = packed[at : at + CH, side]
@@ -356,6 +366,7 @@
 VMEM_LIMIT = 60 * 10**6
 VMEM = pl.BlockSpec(memory_space=pltpu.VMEM)
 HBM = pl.BlockSpec(memory_space=pltpu.HBM)
+SMEM = pl.BlockSpec(memory_space=pltpu.SMEM)
 
 
 def call(kernel, ins, outs, scratch=(), copies=0, flops=10**6, vmem=VMEM_LIMIT):
@@ -365,7 +376,7 @@
     return pl.pallas_call(
         kernel,
         out_shape=[jax.ShapeDtypeStruct(shape, dtype) for shape, dtype, spec in outs],
-        in_specs=[pl.BlockSpec(memory_space=pltpu.SMEM)] + ins,
+        in_specs=ins,
         out_specs=[spec for shape, dtype, spec in outs],
         scratch_shapes=held,
         compiler_params=pltpu.CompilerParams(vmem_limit_bytes=vmem),
@@ -384,11 +395,12 @@
     edge = ((HALO, FIELDS, LON), F32, VMEM)
     own, edge_far, edge_near = call(
         pack_kernel, [VMEM] * 3, [((ROWS, FIELDS, LON), F32, VMEM), edge, edge]
-    )(place, members, condition, observed)
+    )(members, condition, observed)
     across = [(i, i + 1) for i in range(1, TILES - 1, 2)]
     far = lax.ppermute(edge_far, TILE, across + [(j, i) for i, j in across])
     near = lax.ppermute(edge_near, "core", [(0, 1), (1, 0)])
-    w_shapes = [(CH, 9 * FIELDS), (3 * CH, 3 * CH), (48, 3 * CH), (CH, 144), (CH, 9 * CH)]
+    near, place, lat = lax.optimization_barrier((near, place, lat))
+    w_shapes = [(CH, 9 * FIELDS), (3 * CH, 3 * CH), (48, 3 * CH), (CH, 144), (3 * CH, 3 * CH)]
     w_in, w_mid, w_out, w_back_2, w_back_1 = call(
         weights_kernel,
         [VMEM] * 3,
@@ -396,8 +408,15 @@
         + [(shape, BF16, HBM) for shape in w_shapes[3:]],
         [(shape, F32) for shape in w_shapes] + [(shape, BF16) for shape in w_shapes[3:]],
         copies=2,
-    )(place, kernel_in.transpose(0, 2, 1), kernel_mid, kernel_out)
+    )(kernel_in.transpose(0, 2, 1), kernel_mid, kernel_out)
     saved = [
+        ((ROWS + 2, 3 * FIELDS, LON), BF16),
+        ((ROWS + 2, CH, LON), BF16),
+        ((ROWS, CH, LON), F32),
+        ((ROWS + 2, CH, LON), BF16),
+        ((ROWS + 2, CH, LON), F32),
+    ]
+    worked = [
         ((ROWS + 10, 3 * FIELDS, LON), BF16),
         ((ROWS + 8, CH, LON), BF16),
         ((ROWS, CH, LON), F32),
@@ -409,53 +428,55 @@
     kept_shape = ((4, WIDE, LON), F32)
     send, pushed, kept, stack, hidden_1, slope_1, hidden_2, slope_2 = call(
         forward_kernel,
-        [VMEM] * 7,
+        [SMEM] + [VMEM] * 7,
         [fields_shape + (HBM,), ((VARS, ROWS, LON), F32, VMEM), kept_shape + (HBM,)]
         + [shape + (HBM,) for shape in saved],
-        [((rows, LON), F32), kept_shape] + saved + [((2 * HALO, FIELDS, LON), F32)],
+        [((rows, LON), F32), kept_shape] + worked + [((2 * HALO, FIELDS, LON), F32)],
         copies=MEMBERS + 6,
         flops=10**9,
     )(place, far, near, own, members, w_in, w_mid, w_out)
     fields = lax.all_to_all(send, "member", 0, 0)
-    partials_shape = ((TILES, MEMBERS, 128), F32)
+    near_fields = ((MEMBERS, FIXED_AT, LON), F32)
+    lat_shape = ((FIXED_AT + ROWS, 128), F32)
     (partials,) = call(
         distance_kernel,
-        [VMEM] * 3 + [HBM] * 2,
-        [partials_shape + (HBM,)],
-        [fields_shape, ((2, WIDE, LON), F32), partials_shape],
-        copies=MEMBERS + 1,
+        [SMEM] + [VMEM] * 5,
+        [((MEMBERS, 128), F32, VMEM)],
+        vmem=8 * 10**6,
     )(place, lat, members, observed, fields, kept)
-    totals = lax.all_to_all(partials, TILE, 0, 0)
+    swap = [(0, 1), (1, 0)]
+    partials = partials + lax.ppermute(partials, "core", swap)
+    totals = spread(partials, "ring", RING)
     mine, theirs = call(
         backward_kernel,
-        [VMEM] * 2 + [HBM] * 9,
+        [SMEM] + [HBM] * 11,
         [((MEMBERS * CHUNK, 128), F32, VMEM)] * 2,
-        [fields_shape, kept_shape]
+        [lat_shape, ((RING, MEMBERS, 128), F32), near_fields, kept_shape]
         + saved
         + [(shape, BF16) for shape in w_shapes[3:]]
         + [
             ((ROWS + 4, 48, LON), BF16),
             ((ROWS + 2, 3 * CH, LON), BF16),
+            ((ROWS + 2, 3 * CH, LON), F32),
             ((48, 3 * CH), F32),
             ((3 * CH, 3 * CH), F32),
             ((9 * FIELDS, CH), F32),
             ((6 * CH, 128), F32),
         ],
-        copies=9,
+        copies=11,
         flops=10**9,
     )(
         place, lat, totals, fields, kept, stack, hidden_1, slope_1, hidden_2, slope_2,
         w_back_2, w_back_1,
     )
-    swap = [(0, 1), (1, 0)]
     mine = mine + lax.ppermute(theirs, "core", swap)
     chunk = jnp.sum(lax.all_to_all(mine.reshape(MEMBERS, CHUNK, 128), "member", 0, 0), 0)
     chunk = jnp.sum(spread(chunk, "ring", RING), 0)
-    half = spread(chunk, "member", MEMBERS).reshape(MEMBERS * CHUNK, 128)
-    other = lax.ppermute(half, "core", swap)
+    other = lax.ppermute(chunk, "core", swap)
+    chunks = spread(jnp.stack([chunk, other]), "member", MEMBERS)
     grad_in, grad_mid, grad_out, energy = call(
         unpack_kernel,
-        [VMEM] * 2,
+        [SMEM, VMEM],
         [
             ((9, INPUTS, CH), F32, VMEM),
             ((9, CH, CH), F32, VMEM),
@@ -464,7 +485,7 @@
         ],
         [((6 * CH, 128), F32)],
         vmem=16 * 10**6,
-    )(place, half, other)
+    )(place, chunks)
     return (pushed[None], energy[0, 0], grad_in.transpose(0, 2, 1), grad_mid, grad_out)
 
 

time: 117 us -> 109 us (0.932)
  blocking collectives: 50.5 us -> 69.4 us
  waiting for transfers between devices: 20.1 us -> 4.54 us
  Pallas kernels: 26.3 us -> 19.6 us
  starting transfers between devices: 15.3 us -> 11.2 us
    all_to_all x2 -> x3, blocking collectives: 20.9 us -> 45.6 us  [spread(): return lax.all_to_all(copies, axes, 0, 0)]
    all_to_all x1 -> x0, waiting for transfers between devices: 16.2 us -> none  [per_device(): fields = lax.all_to_all(send, 'member', 0, 0)]
    pallas_call x4, Pallas kernels: 21.8 us -> 15.1 us  [the longest x1 6.69 us: per_device(): call(forward_kernel, [SMEM] + [VMEM] * 7, [fields_shape + (HBM,), ((VARS,...]
    all_to_all x1, blocking collectives: 22 us -> 16.1 us  [per_device(): fields = lax.all_to_all(send, 'member', 0, 0)]
    all_to_all x1 -> x0, starting transfers between devices: 4.14 us -> none  [per_device(): fields = lax.all_to_all(send, 'member', 0, 0)]
    ppermute x1, starting transfers between devices: 6.2 us -> 2.96 us  [per_device(): far = lax.ppermute(edge_far, TILE, across + [(j, i) for i, j in across])]
    ppermute x1, starting transfers between devices: 0.09 us -> 3.24 us  [per_device(): near = lax.ppermute(edge_near, 'core', [(0, 1), (1, 0)])]
    ppermute x1, starting transfers between devices: 0.31 us -> 1.85 us  [per_device(): mine = mine + lax.ppermute(theirs, 'core', swap)]
where the time goes in v5:
time: 109 us; the launch traced here: 108 us
  blocking collectives  69.4 us (64%)
  Pallas kernels  19.6 us (18%)
  starting transfers between devices  11.2 us (10%)
  waiting for transfers between devices  4.54 us (4%)
  other arithmetic  1.53 us (1%)
  local copies, waits for them, and re-layouts  1.51 us (1%)
    all_to_all x3, blocking collectives, spread(): return lax.all_to_all(copies, axes, 0, 0)  45.6 us
    all_to_all x1, blocking collectives, per_device(): fields = lax.all_to_all(send, 'member', 0, 0)  16.1 us
    all_to_all x1, blocking collectives, per_device(): lax.all_to_all(mine.reshape(MEMBERS, CHUNK, 128), 'member', 0, 0)  7.63 us
    pallas_call x1, Pallas kernels, per_device(): call(forward_kernel, [SMEM] + [VMEM] * 7, [fields_shape + (HBM,), ((VARS,...  6.69 us
    pallas_call x1, Pallas kernels, per_device(): call(backward_kernel, [SMEM] + [HBM] * 11, [((MEMBERS * CHUNK, 128), F32,...  6.25 us
    ppermute x1, starting transfers between devices, per_device(): near = lax.ppermute(edge_near, 'core', [(0, 1), (1, 0)])  3.24 us
    ppermute x1, starting transfers between devices, per_device(): other = lax.ppermute(chunk, 'core', swap)  3.06 us
    ppermute x1, starting transfers between devices, per_device(): far = lax.ppermute(edge_far, TILE, across + [(j, i) for i, j in across])  2.96 us
  transfers between devices with their start and end apart: 5, of which 4 were waited for; matrix products, arithmetic and copies ran while one was open for 1% of the time, Pallas kernels for 2%

profile of v5, /device:TPU:1, one launch (start us, length us, event | category | flops | bytes accessed | tf_op | source)
XLA Modules:
  0.0 108.5 jit_solution(5958398443195085434)
XLA Ops:
  0.6 1.9 %shard_map.110 = (f32[8,16,512]{2,1,0:T(8,128)}, f32[5,16,512]{2,1,0:T(8,128)}, f32[5,16,512]{2,1,0:T(8,128)}) custom-call(f32[6,8,512]{2,1,0:T(8,128)} %bitcast.13, f32[6,8,512]{2,1,0:T(8,128)} %condition.1, f32[6,8,512]{2,1,0:T(8,128)} %observed.3), custom_call_target="tpu_custom_call" | custom-call | flops 1000000 | bytes 1000000 | tf_op jit(solution)/shard_map/pallas_call | solution.py:396
  2.5 3.2 %collective-permute-start = (f32[5,16,512]{2,1,0:T(8,128)}, f32[5,16,512]{2,1,0:T(8,128)S(1)}, u32[]{:S(2)}, u32[]{:S(2)}) collective-permute-start(f32[5,16,512]{2,1,0:T(8,128)} %get-tuple-element.30), channel_id=1, source_target_pairs={{0,1},{1,0},{2,3},{3,2},{4,5},{5,4},{6,7},{7,6},{8,9},{9,8},{10,11... | collective-permute-start | bytes 491528 | tf_op jit(solution)/shard_map/ppermute | solution.py:401
  5.7 3.0 %collective-permute-start.1 = (f32[5,16,512]{2,1,0:T(8,128)}, f32[5,16,512]{2,1,0:T(8,128)S(1)}, u32[]{:S(2)}, u32[]{:S(2)}) collective-permute-start(f32[5,16,512]{2,1,0:T(8,128)} %get-tuple-element.32), channel_id=1, source_target_pairs={{1,2},{3,4},{5,6},{7,8},{9,10},{11,12},{13,14},{15,16},{17,18},{19... | collective-permute-start | bytes 491528 | tf_op jit(solution)/shard_map/ppermute | solution.py:400
  8.7 0.7 dynamic-slice_bitcast_fusion
  9.4 2.6 %shard_map.111 = (bf16[64,144]{1,0:T(8,128)(2,1)}, bf16[192,192]{1,0:T(8,128)(2,1)}, bf16[48,192]{1,0:T(8,128)(2,1)}, bf16[64,144]{1,0:T(8,128)(2,1)}, bf16[192,192]{1,0:T(8,128)(2,1)}) custom-call(bf16[9,9,64]{2,1,0:T(8,128)(2,1)} %bitcast.18, bf16[9,64,64]{2,1,0:T(8,128)(2,1)} %kernel_mid.1, bf16[9,6,64]{2,1,0:T(8,128)(2,1)} %kernel_out.1), custom_call_target="tpu_custom_call" | custom-call | flops 1000000 | bytes 1000000 | tf_op jit(solution)/shard_map/pallas_call | solution.py:404
  12.0 0.6 pad_add_fusion.place
  12.6 0.0 collective-permute-done.near
  12.6 0.1 broadcast_in_dim.13.lat.lat_in
  12.7 1.4 %collective-permute-done.1.far = f32[5,16,512]{2,1,0:T(8,128)S(1)} collective-permute-done((f32[5,16,512]{2,1,0:T(8,128)}, f32[5,16,512]{2,1,0:T(8,128)S(1)}, u32[]{:S(2)}, u32[]{:S(2)}) %collective-permute-start.1) | collective-permute-done | bytes 163872 | tf_op jit(solution)/shard_map/ppermute | solution.py:400
  14.1 0.0 copy-done.7
  14.1 0.7 copy-done.8
  14.8 6.7 %shard_map.112 = (f32[8,64,512]{2,1,0:T(8,128)}, f32[6,8,512]{2,1,0:T(8,128)}, f32[4,36,512]{2,1,0:T(8,128)}, bf16[10,48,512]{2,1,0:T(8,128)(2,1)}, bf16[10,64,5...) custom-call(s32[3]{0:T(128)} %pad_add_fusion.place, ...), custom_call_target="tpu_custom_call" | custom-call | flops 1000000000 | bytes 1000000 | tf_op jit(solution)/shard_map/pallas_call | solution.py:429
  21.4 0.0 copy-start.1
  21.5 0.0 copy-start.2
  21.5 0.0 copy-start.3
  21.5 16.1 %all_to_all.25.fields.fields_in = f32[8,64,512]{2,1,0:T(8,128)S(1)} all-to-all(f32[8,64,512]{2,1,0:T(8,128)} %get-tuple-element.40), channel_id=1, replica_groups=mesh['member'=8,'ring'=16,'core'=2] {'member'}, dimensions={0} | all-to-all | bytes 2097152 | tf_op jit(solution)/shard_map/all_to_all | solution.py:438
  37.6 0.0 copy-done.4
  37.6 0.7 shard_map.113
  38.4 0.1 collective-permute-start.2
  38.5 1.2 %collective-permute-done.2 = f32[8,128]{1,0:T(8,128)S(1)} collective-permute-done((f32[8,128]{1,0:T(8,128)S(1)}, f32[8,128]{1,0:T(8,128)S(1)}, u32[]{:S(2)}, u32[]{:S(2)}) %collective-permute-start.2) | collective-permute-done | bytes 4128 | tf_op jit(solution)/shard_map/ppermute | solution.py:448
  39.6 24.2 %all_to_all.26.totals_in = f32[16,8,128]{2,1,0:T(8,128)} all-to-all(f32[16,8,128]{2,1,0:T(8,128)S(1)} %broadcast_in_dim.15), channel_id=1, replica_groups=mesh['member'=8,'ring'=16,'core'=2] {'ring'}, dimensions={0} | all-to-all | bytes 131072 | tf_op jit(solution)/shard_map/all_to_all | solution.py:29
  63.9 6.2 %shard_map.114 = (f32[192,128]{1,0:T(8,128)}, f32[192,128]{1,0:T(8,128)}) custom-call(s32[3]{0:T(128)} %pad_add_fusion.place, f32[48,128]{1,0:T(8,128)} %copy-done.4, f32[16,8,128]{2,1,0:T(8,128)} %all_to_all.26.totals_in, f32[8,64,512]{2,1,0:T(8,128)} %copy-done, f32[4,36,512]{2,1,0:T(8,128)} %get-tuple-element.41.kept.kept_in, ...), custom_call_target="tpu_custom_call" | custom-call | flops 1000000000 | bytes 1000000 | tf_op jit(solution)/shard_map/pallas_call | solution.py:450
  70.1 1.8 %collective-permute-start.3 = (f32[192,128]{1,0:T(8,128)}, f32[192,128]{1,0:T(8,128)S(1)}, u32[]{:S(2)}, u32[]{:S(2)}) collective-permute-start(f32[192,128]{1,0:T(8,128)} %get-tuple-element.50), channel_id=1, source_target_pairs={{0,1},{1,0},{2,3},{3,2},{4,5},{5,4},{6,7},{7,6},{8,9},{9,8},{10,11... | collective-permute-start | bytes 294920 | tf_op jit(solution)/shard_map/ppermute | solution.py:472
  72.0 1.2 %collective-permute-done.3 = f32[192,128]{1,0:T(8,128)S(1)} collective-permute-done((f32[192,128]{1,0:T(8,128)}, f32[192,128]{1,0:T(8,128)S(1)}, u32[]{:S(2)}, u32[]{:S(2)}) %collective-permute-start.3) | collective-permute-done | bytes 98336 | tf_op jit(solution)/shard_map/ppermute | solution.py:472
  73.1 0.9 add.15
  74.0 7.6 %all_to_all.27 = f32[8,24,128]{2,1,0:T(8,128)S(1)} all-to-all(f32[8,24,128]{2,1,0:T(8,128)S(1)} %bitcast.16), channel_id=1, replica_groups=mesh['member'=8,'ring'=16,'core'=2] {'member'}, dimensions={0} | all-to-all | bytes 196608 | tf_op jit(solution)/shard_map/all_to_all | solution.py:473
  81.7 13.2 %all_to_all.28 = f32[16,24,128]{2,1,0:T(8,128)S(1)} all-to-all(f32[16,24,128]{2,1,0:T(8,128)S(1)} %broadcast_in_dim.32), channel_id=1, replica_groups=mesh['member'=8,'ring'=16,'core'=2] {'ring'}, dimensions={0} | all-to-all | bytes 393216 | tf_op jit(solution)/shard_map/all_to_all | solution.py:29
  95.0 3.1 %collective-permute-start.4 = (f32[24,128]{1,0:T(8,128)S(1)}, f32[24,128]{1,0:T(8,128)S(1)}, u32[]{:S(2)}, u32[]{:S(2)}) collective-permute-start(f32[24,128]{1,0:T(8,128)S(1)} %reduce_sum.19), channel_id=1, source_target_pairs={{0,1},{1,0},{2,3},{3,2},{4,5},{5,4},{6,7},{7,6},{8,9},{9,8},{10,11... | collective-permute-start | bytes 36872 | tf_op jit(solution)/shard_map/ppermute | solution.py:475
  98.0 0.8 collective-permute-done.4
  98.9 8.2 %all_to_all.29.chunks = f32[8,2,24,128]{3,2,1,0:T(8,128)S(1)} all-to-all(f32[8,2,24,128]{3,2,1,0:T(8,128)S(1)} %broadcast_in_dim.33), channel_id=1, replica_groups=mesh['member'=8,'ring'=16,'core'=2] {'member'}, dimensions={0} | all-to-all | bytes 393216 | tf_op jit(solution)/shard_map/all_to_all | solution.py:29
  107.1 0.0 copy-done.6
  107.1 1.4 %shard_map.115 = (f32[9,9,64]{2,1,0:T(8,128)}, f32[9,64,64]{2,1,0:T(8,128)}, f32[9,6,64]{2,1,0:T(8,128)}, f32[1,1]{1,0:T(1,128)}) custom-call(s32[3]{0:T(128)S(1)} %copy-done.6, f32[8,2,24,128]{3,2,1,0:T(8,128)S(1)} %all_to_all.29.chunks), custom_call_target="tpu_custom_call" | custom-call | flops 1000000 | bytes 1000000 | tf_op jit(solution)/shard_map/pallas_call | solution.py:477
  (18 shorter events, 0.1 us)
Async XLA Ops:
  2.5 10.1 %collective-permute-start = (f32[5,16,512]{2,1,0:T(8,128)}, f32[5,16,512]{2,1,0:T(8,128)S(1)}, u32[]{:S(2)}, u32[]{:S(2)}) collective-permute-start(f32[5,16,512]{2,1,0:T(8,128)} %get-tuple-element.30), channel_id=1, source_target_pairs={{0,1},{1,0},{2,3},{3,2},{4,5},{5,4},{6,7},{7,6},{8,9},{9,8},{10,11... | collective-permute-start | bytes 491528 | tf_op jit(solution)/shard_map/ppermute | solution.py:401
  5.7 8.3 %collective-permute-start.1 = (f32[5,16,512]{2,1,0:T(8,128)}, f32[5,16,512]{2,1,0:T(8,128)S(1)}, u32[]{:S(2)}, u32[]{:S(2)}) collective-permute-start(f32[5,16,512]{2,1,0:T(8,128)} %get-tuple-element.32), channel_id=1, source_target_pairs={{1,2},{3,4},{5,6},{7,8},{9,10},{11,12},{13,14},{15,16},{17,18},{19... | collective-permute-start | bytes 491528 | tf_op jit(solution)/shard_map/ppermute | solution.py:400
  12.6 1.5 %copy-start.7 = (f32[5,16,512]{2,1,0:T(8,128)}, f32[5,16,512]{2,1,0:T(8,128)S(1)}, u32[]{:S(2)}) copy-start(f32[5,16,512]{2,1,0:T(8,128)S(1)} %collective-permute-done.near) | copy-start | bytes 491524
  12.7 24.9 %copy-start.4 = (f32[48,128]{1,0:T(8,128)}, f32[48,128]{1,0:T(8,128)S(1)}, u32[]{:S(2)}) copy-start(f32[48,128]{1,0:T(8,128)S(1)} %broadcast_in_dim.13.lat.lat_in) | copy-start | bytes 73732
  14.1 0.7 copy-start.8
  21.4 16.2 %copy-start.1 = (f32[4,36,512]{2,1,0:T(8,128)S(1)}, f32[4,36,512]{2,1,0:T(8,128)}, u32[]{:S(2)}) copy-start(f32[4,36,512]{2,1,0:T(8,128)} %get-tuple-element.41.kept.kept_in) | copy-start | bytes 884740
  21.5 16.1 %copy-start.2 = (f32[1,6,8,512]{3,2,1,0:T(8,128)S(1)}, f32[1,6,8,512]{3,2,1,0:T(8,128)}, u32[]{:S(2)}) copy-start(f32[1,6,8,512]{3,2,1,0:T(8,128)} %param.7) | copy-start | bytes 294916
  21.5 16.1 %copy-start.3 = (f32[6,8,512]{2,1,0:T(8,128)S(1)}, f32[6,8,512]{2,1,0:T(8,128)}, u32[]{:S(2)}) copy-start(f32[6,8,512]{2,1,0:T(8,128)} %observed.3) | copy-start | bytes 294916
  21.5 16.1 %copy-start.5 = (s32[3]{0:T(128)S(1)}, s32[3]{0:T(128)}, u32[]{:S(2)}) copy-start(s32[3]{0:T(128)} %pad_add_fusion.place) | copy-start | bytes 40
  37.6 26.3 %copy-start = (f32[8,64,512]{2,1,0:T(8,128)}, f32[8,64,512]{2,1,0:T(8,128)S(1)}, u32[]{:S(2)}) copy-start(f32[8,64,512]{2,1,0:T(8,128)S(1)} %all_to_all.25.fields.fields_in) | copy-start | bytes 3145732
  38.4 1.3 %collective-permute-start.2 = (f32[8,128]{1,0:T(8,128)S(1)}, f32[8,128]{1,0:T(8,128)S(1)}, u32[]{:S(2)}, u32[]{:S(2)}) collective-permute-start(f32[8,128]{1,0:T(8,128)S(1)} %shard_map.113), channel_id=1, source_target_pairs={{0,1},{1,0},{2,3},{3,2},{4,5},{5,4},{6,7},{7,6},{8,9},{9,8},{10,11... | collective-permute-start | bytes 12296 | tf_op jit(solution)/shard_map/ppermute | solution.py:448
  70.1 36.9 %copy-start.6 = (s32[3]{0:T(128)S(1)}, s32[3]{0:T(128)}, u32[]{:S(2)}) copy-start(s32[3]{0:T(128)} %pad_add_fusion.place) | copy-start | bytes 40
  70.1 3.0 %collective-permute-start.3 = (f32[192,128]{1,0:T(8,128)}, f32[192,128]{1,0:T(8,128)S(1)}, u32[]{:S(2)}, u32[]{:S(2)}) collective-permute-start(f32[192,128]{1,0:T(8,128)} %get-tuple-element.50), channel_id=1, source_target_pairs={{0,1},{1,0},{2,3},{3,2},{4,5},{5,4},{6,7},{7,6},{8,9},{9,8},{10,11... | collective-permute-start | bytes 294920 | tf_op jit(solution)/shard_map/ppermute | solution.py:472
  95.0 3.9 %collective-permute-start.4 = (f32[24,128]{1,0:T(8,128)S(1)}, f32[24,128]{1,0:T(8,128)S(1)}, u32[]{:S(2)}, u32[]{:S(2)}) collective-permute-start(f32[24,128]{1,0:T(8,128)S(1)} %reduce_sum.19), channel_id=1, source_target_pairs={{0,1},{1,0},{2,3},{3,2},{4,5},{5,4},{6,7},{7,6},{8,9},{9,8},{10,11... | collective-permute-start | bytes 36872 | tf_op jit(solution)/shard_map/ppermute | solution.py:475

commit v6 on v5

--- a/solution.py
+++ b/solution.py
@@ -67,12 +67,19 @@
     lax.fori_loop(start, stop, lambda row, carry: (body(row), carry)[1], 0, unroll=True)
 
 
-def pack_kernel(members, condition, observed, own, edge_far, edge_near):
+def pack_kernel(
+    members_in, condition_in, observed_in, own, edge_far, edge_near,
+    members, condition, observed, sems,
+):
+    pairs = [(members_in, members), (condition_in, condition)]
+    pairs.append((observed_in.at[HALF:], observed))
+    for copy in started(pairs, sems):
+        copy.wait()
     for row in range(ROWS):
         own[row, :HALF, :] = members[:HALF, row, :]
         own[row, HALF:INPUTS, :] = condition[:, row, :]
         own[row, INPUTS : INPUTS + HALF, :] = members[HALF:, row, :]
-        own[row, INPUTS + HALF : INPUTS + 2 * HALF, :] = observed[HALF:, row, :]
+        own[row, INPUTS + HALF : INPUTS + 2 * HALF, :] = observed[:, row, :]
         own[row, FIELDS - 1 :, :] = jnp.zeros((1, LON), F32)
     odd = lax.axis_index("core") == 1
     for row in range(HALO):
@@ -82,11 +89,20 @@
 
 
 def weights_kernel(
-    kernel_in, kernel_mid, kernel_out, w_in, w_mid, w_out, w_back_2, w_back_1,
-    flat_in, square, flat_out, back_2, back_1, held_2, held_1, sems,
+    kernel_in_in, kernel_mid_in, kernel_out_in, w_in, w_mid, w_out, w_back_2, w_back_1,
+    kernel_in, kernel_mid, kernel_out, flat_in, square, flat_out, back_2, back_1, held_2, held_1, sems,
 ):
+    pairs = [(kernel_in_in, kernel_in), (kernel_mid_in, kernel_mid), (kernel_out_in, kernel_out)]
+    copies = [
+        pltpu.make_async_copy(source, target, sems.at[2 + at])
+        for at, (source, target) in enumerate(pairs)
+    ]
+    for copy in copies:
+        copy.start()
     flat_out[...] = jnp.zeros_like(flat_out)
     back_2[...] = jnp.zeros_like(back_2)
+    for copy in copies:
+        copy.wait()
     for tap in range(9):
         a, b = tap // 3, tap % 3
         back = 3 * (2 - a) + b
@@ -119,10 +135,12 @@
 
 
 def forward_kernel(
-    place, far, near, own, members, w_in, w_mid, w_out,
+    place, far, near, own, members_in, w_in, w_mid, w_out,
     send_out, pushed, kept_out, stack_out, hidden_1_out, slope_1_out, hidden_2_out, slope_2_out,
-    send, kept, stack, hidden_1, slope_1, hidden_2, slope_2, edges, sems,
+    send, kept, stack, hidden_1, slope_1, hidden_2, slope_2, edges, members, sems,
 ):
+    brought = pltpu.make_async_copy(members_in.at[:HALF], members, sems.at[MEMBERS + 6])
+    brought.start()
     base = place[1]
     odd = place[2] == 1
     copies = []
@@ -175,8 +193,9 @@
     keep(hidden_2.at[2:12], hidden_2_out)
     keep(slope_2, slope_2_out)
 
+    brought.wait()
     send[WIDE:FIXED_AT, :] = jnp.zeros((FIXED_AT - WIDE, LON), F32)
-    send[FIXED_AT:, :] = members[:HALF].reshape(HALF * ROWS, LON)
+    send[FIXED_AT:, :] = members[...].reshape(HALF * ROWS, LON)
     for row in range(ROWS + 4):
         part = dot(w_out[...], hidden_2[row : row + 3].reshape(3 * CH, LON))
         both = turned(part[:16], 1) + part[16:32] + turned(part[32:], -1)
@@ -196,7 +215,7 @@
     for member in range(MEMBERS):
         keep(send, send_out.at[member])
     keep(kept, kept_out)
-    pushed[:HALF] = members[:HALF]
+    pushed[:HALF] = members[...]
     for copy in copies:
         copy.wait()
 
@@ -236,22 +255,21 @@
 
 
 def backward_kernel(
-    place, lat_in, totals_in, fields_in, kept_in, stack_in, hidden_1_in, slope_1_in, hidden_2_in,
+    place, lat, totals, fields_in, kept_in, stack_in, hidden_1_in, slope_1_in, hidden_2_in,
     slope_2_in, w_back_2_in, w_back_1_in,
     mine, theirs,
-    lat, totals, fields, kept, stack, hidden_1, slope_1, hidden_2, slope_2, w_back_2, w_back_1,
+    fields, kept, stack, hidden_1, slope_1, hidden_2, slope_2, w_back_2, w_back_1,
     coupled, turned_2, by_row, sum_out, sum_mid, sum_in, packed, sems,
 ):
-    sources = [totals_in, lat_in, kept_in, fields_in.at[:, :FIXED_AT], w_back_2_in, slope_2_in]
+    sources = [kept_in, fields_in.at[:, :FIXED_AT], w_back_2_in, slope_2_in]
     sources += [w_back_1_in, hidden_1_in, hidden_2_in, slope_1_in, stack_in]
-    targets = [totals, lat, kept, fields, w_back_2, slope_2]
+    targets = [kept, fields, w_back_2, slope_2]
     targets += [w_back_1, hidden_1, hidden_2, slope_1, stack]
     copies = started(list(zip(sources, targets)), sems)
     me, base, core = place[0], place[1], place[2]
     sum_out[...] = jnp.zeros_like(sum_out)
     sum_mid[...] = jnp.zeros_like(sum_mid)
     sum_in[...] = jnp.zeros_like(sum_in)
-    copies[0].wait()
     total = totals[0]
     for tile in range(1, RING):
         total = total + totals[tile]
@@ -262,11 +280,10 @@
     weights = 1.0 / (jnp.where(is_me, MEMBERS, MEMBERS * MEMBERS) * distances)
     own_weight = jnp.sum(jnp.where(is_me, weights, 0.0), 0, keepdims=True)
     weights = jnp.where(is_me, 0.0, weights)
-    copies[1].wait()
-    copies[2].wait()
+    copies[0].wait()
     log_scale, moving, observed, moved = kept[0], kept[1], kept[2], kept[3]
     inner = (moved - observed) * own_weight
-    copies[3].wait()
+    copies[1].wait()
     for n in range(MEMBERS):
         inner = inner - weights[n : n + 1] * (moved - fields[n, :WIDE])
     upper = lat[:WIDE, :1] * inner / math.sqrt(ENTRIES)
@@ -278,8 +295,8 @@
         for shift in range(3):
             part = turned(field, shift - 1).astype(BF16)
             coupled[row, shift * 16 : (shift + 1) * 16, :] = part
-    copies[4].wait()
-    copies[5].wait()
+    copies[2].wait()
+    copies[3].wait()
 
     def second(row):
         back = dot(w_back_2[...], coupled[pl.ds(row, 3)].reshape(144, LON))
@@ -289,28 +306,28 @@
             turned_2[row, shift * CH : (shift + 1) * CH, :] = part
 
     loop(0, ROWS + 2, second)
-    copies[6].wait()
+    copies[4].wait()
 
     def across_rows(row):
         by_row[row] = dot(w_back_1[...], turned_2[row])
 
     loop(0, ROWS + 2, across_rows)
-    copies[7].wait()
+    copies[5].wait()
 
     def middle(row):
         near = hidden_1[pl.ds(row, 3)].reshape(3 * CH, LON)
         sum_mid[...] += dot_cells(turned_2[row + 1], near)
 
     loop(0, ROWS, middle)
-    copies[8].wait()
+    copies[6].wait()
 
     def outer(row):
         near = hidden_2[pl.ds(row, 3)].reshape(3 * CH, LON)
         sum_out[...] += dot_cells(coupled[row + 2], near)
 
     loop(0, ROWS, outer)
-    copies[9].wait()
-    copies[10].wait()
+    copies[7].wait()
+    copies[8].wait()
 
     def last(row):
         back = by_row[row + 2, :CH] + by_row[row + 1, CH : 2 * CH] + by_row[row, 2 * CH :]
@@ -363,7 +380,7 @@
     energy[...] = packed[6 * CH - 1 :, 127:]
 
 
-VMEM_LIMIT = 60 * 10**6
+VMEM_LIMIT = 28 * 10**6
 VMEM = pl.BlockSpec(memory_space=pltpu.VMEM)
 HBM = pl.BlockSpec(memory_space=pltpu.HBM)
 SMEM = pl.BlockSpec(memory_space=pltpu.SMEM)
@@ -373,15 +390,29 @@
     held = [pltpu.VMEM(shape, dtype) for shape, dtype in scratch]
     if copies > 0:
         held.append(pltpu.SemaphoreType.DMA((copies,)))
-    return pl.pallas_call(
+    shapes = [
+        pltpu.HBM(shape, dtype) if spec is HBM else jax.ShapeDtypeStruct(shape, dtype)
+        for shape, dtype, spec in outs
+    ]
+    run = pl.pallas_call(
         kernel,
-        out_shape=[jax.ShapeDtypeStruct(shape, dtype) for shape, dtype, spec in outs],
+        out_shape=shapes,
         in_specs=ins,
         out_specs=[spec for shape, dtype, spec in outs],
         scratch_shapes=held,
         compiler_params=pltpu.CompilerParams(vmem_limit_bytes=vmem),
         cost_estimate=pl.CostEstimate(flops=flops, bytes_accessed=10**6, transcendentals=0),
     )
+
+    def placed(*arrays):
+        return run(
+            *[
+                pltpu.with_memory_space_constraint(array, pltpu.HBM) if spec is HBM else array
+                for array, spec in zip(arrays, ins)
+            ]
+        )
+
+    return placed
 
 
 def per_device(members, condition, observed, kernel_in, kernel_mid, kernel_out):
@@ -394,7 +425,11 @@
     lat = jnp.broadcast_to(lat[:, None], (FIXED_AT + ROWS, 128))
     edge = ((HALO, FIELDS, LON), F32, VMEM)
     own, edge_far, edge_near = call(
-        pack_kernel, [VMEM] * 3, [((ROWS, FIELDS, LON), F32, VMEM), edge, edge]
+        pack_kernel,
+        [HBM] * 3,
+        [((ROWS, FIELDS, LON), F32, VMEM), edge, edge],
+        [((VARS, ROWS, LON), F32), ((COND, ROWS, LON), F32), ((HALF, ROWS, LON), F32)],
+        copies=3,
     )(members, condition, observed)
     across = [(i, i + 1) for i in range(1, TILES - 1, 2)]
     far = lax.ppermute(edge_far, TILE, across + [(j, i) for i, j in across])
@@ -403,11 +438,13 @@
     w_shapes = [(CH, 9 * FIELDS), (3 * CH, 3 * CH), (48, 3 * CH), (CH, 144), (3 * CH, 3 * CH)]
     w_in, w_mid, w_out, w_back_2, w_back_1 = call(
         weights_kernel,
-        [VMEM] * 3,
+        [HBM] * 3,
         [(shape, BF16, VMEM) for shape in w_shapes[:3]]
         + [(shape, BF16, HBM) for shape in w_shapes[3:]],
-        [(shape, F32) for shape in w_shapes] + [(shape, BF16) for shape in w_shapes[3:]],
-        copies=2,
+        [((9, INPUTS, CH), BF16), ((9, CH, CH), BF16), ((9, VARS, CH), BF16)]
+        + [(shape, F32) for shape in w_shapes]
+        + [(shape, BF16) for shape in w_shapes[3:]],
+        copies=5,
     )(kernel_in.transpose(0, 2, 1), kernel_mid, kernel_out)
     saved = [
         ((ROWS + 2, 3 * FIELDS, LON), BF16),
@@ -428,16 +465,16 @@
     kept_shape = ((4, WIDE, LON), F32)
     send, pushed, kept, stack, hidden_1, slope_1, hidden_2, slope_2 = call(
         forward_kernel,
-        [SMEM] + [VMEM] * 7,
+        [SMEM] + [VMEM] * 3 + [HBM] + [VMEM] * 3,
         [fields_shape + (HBM,), ((VARS, ROWS, LON), F32, VMEM), kept_shape + (HBM,)]
         + [shape + (HBM,) for shape in saved],
-        [((rows, LON), F32), kept_shape] + worked + [((2 * HALO, FIELDS, LON), F32)],
-        copies=MEMBERS + 6,
+        [((rows, LON), F32), kept_shape] + worked
+        + [((2 * HALO, FIELDS, LON), F32), ((HALF, ROWS, LON), F32)],
+        copies=MEMBERS + 7,
         flops=10**9,
     )(place, far, near, own, members, w_in, w_mid, w_out)
     fields = lax.all_to_all(send, "member", 0, 0)
     near_fields = ((MEMBERS, FIXED_AT, LON), F32)
-    lat_shape = ((FIXED_AT + ROWS, 128), F32)
     (partials,) = call(
         distance_kernel,
         [SMEM] + [VMEM] * 5,
@@ -449,9 +486,9 @@
     totals = spread(partials, "ring", RING)
     mine, theirs = call(
         backward_kernel,
-        [SMEM] + [HBM] * 11,
+        [SMEM] + [VMEM] * 2 + [HBM] * 9,
         [((MEMBERS * CHUNK, 128), F32, VMEM)] * 2,
-        [lat_shape, ((RING, MEMBERS, 128), F32), near_fields, kept_shape]
+        [near_fields, kept_shape]
         + saved
         + [(shape, BF16) for shape in w_shapes[3:]]
         + [
@@ -463,7 +500,7 @@
             ((9 * FIELDS, CH), F32),
             ((6 * CH, 128), F32),
         ],
-        copies=11,
+        copies=9,
         flops=10**9,
     )(
         place, lat, totals, fields, kept, stack, hidden_1, slope_1, hidden_2, slope_2,

time: 109 us -> 104 us (0.954)
  Pallas kernels: 19.6 us -> 16.3 us
  other arithmetic: 1.53 us -> 0.13 us
    pallas_call x6, Pallas kernels: 19.6 us -> 16.3 us  [placed(): run(*[pltpu.with_memory_space_constraint(array, pltpu.HBM) if spec is HBM...]
where the time goes in v6:
time: 104 us
  blocking collectives  69.3 us (67%)
  Pallas kernels  16.3 us (16%)
  starting transfers between devices  11.3 us (11%)
  waiting for transfers between devices  5.2 us (5%)
    all_to_all x3, blocking collectives, spread(): return lax.all_to_all(copies, axes, 0, 0)  46.4 us
    pallas_call x6, Pallas kernels, placed(): run(*[pltpu.with_memory_space_constraint(array, pltpu.HBM) if spec is HBM...  16.3 us
    all_to_all x1, blocking collectives, per_device(): fields = lax.all_to_all(send, 'member', 0, 0)  15.2 us
    all_to_all x1, blocking collectives, per_device(): lax.all_to_all(mine.reshape(MEMBERS, CHUNK, 128), 'member', 0, 0)  7.63 us
    ppermute x1, starting transfers between devices, per_device(): near = lax.ppermute(edge_near, 'core', [(0, 1), (1, 0)])  3.33 us
    ppermute x1, starting transfers between devices, per_device(): other = lax.ppermute(chunk, 'core', swap)  3.06 us
    ppermute x1, starting transfers between devices, per_device(): far = lax.ppermute(edge_far, TILE, across + [(j, i) for i, j in across])  2.99 us
    ppermute x1, waiting for transfers between devices, per_device(): far = lax.ppermute(edge_far, TILE, across + [(j, i) for i, j in across])  2.27 us
  transfers between devices with their start and end apart: 5, of which 4 were waited for; matrix products, arithmetic and copies ran while one was open for 1% of the time, Pallas kernels for 2%

profile of v6, /device:TPU:1, one launch (start us, length us, event | category | flops | bytes accessed | tf_op | source)
XLA Modules:
  0.0 103.8 jit_solution(11356663164939006889)
XLA Ops:
  0.6 1.1 %shard_map.110 = (f32[8,16,512]{2,1,0:T(8,128)S(1)}, f32[5,16,512]{2,1,0:T(8,128)S(1)}, f32[5,16,512]{2,1,0:T(8,128)S(1)}) custom-call(f32[6,8,512]{2,1,0:T(8,128)} %bitcast.13, f32[6,8,512]{2,1,0:T(8,128)} %condition_in.1, f32[6,8,512]{2,1,0:T(8,128)} %observed.1), custom_call_target="tpu_custom_call" | custom-call | flops 1000000 | bytes 1000000 | tf_op jit(solution)/shard_map/pallas_call | solution.py:408
  1.7 3.3 %collective-permute-start = (f32[5,16,512]{2,1,0:T(8,128)S(1)}, f32[5,16,512]{2,1,0:T(8,128)S(1)}, u32[]{:S(2)}, u32[]{:S(2)}) collective-permute-start(f32[5,16,512]{2,1,0:T(8,128)S(1)} %get-tuple-element.30), channel_id=1, source_target_pairs={{0,1},{1,0},{2,3},{3,2},{4,5},{5,4},{6,7},{7,6},{8,9},{9,8},{10,11... | collective-permute-start | bytes 491528 | tf_op jit(solution)/shard_map/ppermute | solution.py:436
  5.0 3.0 %collective-permute-start.1 = (f32[5,16,512]{2,1,0:T(8,128)S(1)}, f32[5,16,512]{2,1,0:T(8,128)S(1)}, u32[]{:S(2)}, u32[]{:S(2)}) collective-permute-start(f32[5,16,512]{2,1,0:T(8,128)S(1)} %get-tuple-element.32), channel_id=1, source_target_pairs={{1,2},{3,4},{5,6},{7,8},{9,10},{11,12},{13,14},{15,16},{17,18},{19... | collective-permute-start | bytes 491528 | tf_op jit(solution)/shard_map/ppermute | solution.py:435
  8.0 0.7 dynamic-slice_bitcast_fusion
  8.7 2.0 %shard_map.111 = (bf16[64,144]{1,0:T(8,128)(2,1)S(1)}, bf16[192,192]{1,0:T(8,128)(2,1)S(1)}, bf16[48,192]{1,0:T(8,128)(2,1)S(1)}, bf16[64,144]{1,0:T(8,128)(2,1)}, bf16[192,192]{1,0:T(8,128)(2,1)}) custom-call(bf16[9,9,64]{2,1,0:T(8,128)(2,1)} %bitcast.18, bf16[9,64,64]{2,1,0:T(8,128)(2,1)} %kernel_mid_in.1, bf16[9,6,64]{2,1,0:T(8,128)(2,1)} %kernel_out_in.1), custom_call_target="tpu_custom_call" | custom-call | flops 1000000 | bytes 1000000 | tf_op jit(solution)/shard_map/pallas_call | solution.py:408
  10.7 0.1 pad_add_fusion.place
  10.8 0.0 collective-permute-done.near
  10.8 0.1 broadcast_in_dim.13.lat
  10.9 2.3 %collective-permute-done.1.far = f32[5,16,512]{2,1,0:T(8,128)S(1)} collective-permute-done((f32[5,16,512]{2,1,0:T(8,128)S(1)}, f32[5,16,512]{2,1,0:T(8,128)S(1)}, u32[]{:S(2)}, u32[]{:S(2)}) %collective-permute-start.1) | collective-permute-done | bytes 163872 | tf_op jit(solution)/shard_map/ppermute | solution.py:435
  13.2 5.7 %shard_map.112 = (f32[8,64,512]{2,1,0:T(8,128)}, f32[6,8,512]{2,1,0:T(8,128)}, f32[4,36,512]{2,1,0:T(8,128)}, bf16[10,48,512]{2,1,0:T(8,128)(2,1)}, bf16[10,64,5...) custom-call(s32[3]{0:T(128)S(1)} %pad_add_fusion.place, ...), custom_call_target="tpu_custom_call" | custom-call | flops 1000000000 | bytes 1000000 | tf_op jit(solution)/shard_map/pallas_call | solution.py:408
  18.9 0.0 copy-start.1
  18.9 0.0 copy-start.2
  18.9 0.0 copy-start.3
  18.9 15.2 %all_to_all.25.fields.fields_in = f32[8,64,512]{2,1,0:T(8,128)S(1)} all-to-all(f32[8,64,512]{2,1,0:T(8,128)} %get-tuple-element.40), channel_id=1, replica_groups=mesh['member'=8,'ring'=16,'core'=2] {'member'}, dimensions={0} | all-to-all | bytes 2097152 | tf_op jit(solution)/shard_map/all_to_all | solution.py:476
  34.1 0.0 copy-start
  34.1 0.0 copy-done.1
  34.1 0.0 copy-done.2
  34.1 0.0 copy-done.3
  34.2 0.7 shard_map.113
  34.9 0.1 collective-permute-start.2
  35.0 1.2 %collective-permute-done.2 = f32[8,128]{1,0:T(8,128)S(1)} collective-permute-done((f32[8,128]{1,0:T(8,128)S(1)}, f32[8,128]{1,0:T(8,128)S(1)}, u32[]{:S(2)}, u32[]{:S(2)}) %collective-permute-start.2) | collective-permute-done | bytes 4128 | tf_op jit(solution)/shard_map/ppermute | solution.py:485
  36.2 25.0 %all_to_all.26.totals = f32[16,8,128]{2,1,0:T(8,128)S(1)} all-to-all(f32[16,8,128]{2,1,0:T(8,128)S(1)} %broadcast_in_dim.15), channel_id=1, replica_groups=mesh['member'=8,'ring'=16,'core'=2] {'ring'}, dimensions={0} | all-to-all | bytes 131072 | tf_op jit(solution)/shard_map/all_to_all | solution.py:29
  61.2 0.0 copy-done
  61.2 5.4 %shard_map.114 = (f32[192,128]{1,0:T(8,128)S(1)}, f32[192,128]{1,0:T(8,128)S(1)}) custom-call(s32[3]{0:T(128)S(1)} %pad_add_fusion.place, f32[48,128]{1,0:T(8,128)S(1)} %broadcast_in_dim.13.lat, f32[16,8,128]{2,1,0:T(8,128)S(1)} %all_to_all.26.totals, f32[8,64,512]{2,1,0:T(8,128)} %copy-done, f32[4,36,512]{2,1,0:T(8,128)} %get-tuple-element.41.kept.kept_in, ...), custom_call_target="tpu_custom_call" | custom-call | flops 1000000000 | bytes 1000000 | tf_op jit(solution)/shard_map/pallas_call | solution.py:408
  66.6 1.8 %collective-permute-start.3 = (f32[192,128]{1,0:T(8,128)S(1)}, f32[192,128]{1,0:T(8,128)S(1)}, u32[]{:S(2)}, u32[]{:S(2)}) collective-permute-start(f32[192,128]{1,0:T(8,128)S(1)} %get-tuple-element.50), channel_id=1, source_target_pairs={{0,1},{1,0},{2,3},{3,2},{4,5},{5,4},{6,7},{7,6},{8,9},{9,8},{10,11... | collective-permute-start | bytes 294920 | tf_op jit(solution)/shard_map/ppermute | solution.py:509
  68.4 0.9 collective-permute-done.3
  69.4 7.6 %all_to_all.27 = f32[8,24,128]{2,1,0:T(8,128)S(1)} all-to-all(f32[8,24,128]{2,1,0:T(8,128)S(1)} %bitcast.16), channel_id=1, replica_groups=mesh['member'=8,'ring'=16,'core'=2] {'member'}, dimensions={0} | all-to-all | bytes 196608 | tf_op jit(solution)/shard_map/all_to_all | solution.py:510
  77.0 13.2 %all_to_all.28 = f32[16,24,128]{2,1,0:T(8,128)S(1)} all-to-all(f32[16,24,128]{2,1,0:T(8,128)S(1)} %broadcast_in_dim.32), channel_id=1, replica_groups=mesh['member'=8,'ring'=16,'core'=2] {'ring'}, dimensions={0} | all-to-all | bytes 393216 | tf_op jit(solution)/shard_map/all_to_all | solution.py:29
  90.3 3.1 %collective-permute-start.4 = (f32[24,128]{1,0:T(8,128)S(1)}, f32[24,128]{1,0:T(8,128)S(1)}, u32[]{:S(2)}, u32[]{:S(2)}) collective-permute-start(f32[24,128]{1,0:T(8,128)S(1)} %reduce_sum.19), channel_id=1, source_target_pairs={{0,1},{1,0},{2,3},{3,2},{4,5},{5,4},{6,7},{7,6},{8,9},{9,8},{10,11... | collective-permute-start | bytes 36872 | tf_op jit(solution)/shard_map/ppermute | solution.py:512
  93.3 0.8 collective-permute-done.4
  94.2 8.2 %all_to_all.29.chunks = f32[8,2,24,128]{3,2,1,0:T(8,128)S(1)} all-to-all(f32[8,2,24,128]{3,2,1,0:T(8,128)S(1)} %broadcast_in_dim.33), channel_id=1, replica_groups=mesh['member'=8,'ring'=16,'core'=2] {'member'}, dimensions={0} | all-to-all | bytes 393216 | tf_op jit(solution)/shard_map/all_to_all | solution.py:29
  102.4 1.4 %shard_map.115 = (f32[9,9,64]{2,1,0:T(8,128)}, f32[9,64,64]{2,1,0:T(8,128)}, f32[9,6,64]{2,1,0:T(8,128)}, f32[1,1]{1,0:T(1,128)}) custom-call(s32[3]{0:T(128)S(1)} %pad_add_fusion.place, f32[8,2,24,128]{3,2,1,0:T(8,128)S(1)} %all_to_all.29.chunks), custom_call_target="tpu_custom_call" | custom-call | flops 1000000 | bytes 1000000 | tf_op jit(solution)/shard_map/pallas_call | solution.py:408
  (8 shorter events, 0.1 us)
Async XLA Ops:
  1.7 9.1 %collective-permute-start = (f32[5,16,512]{2,1,0:T(8,128)S(1)}, f32[5,16,512]{2,1,0:T(8,128)S(1)}, u32[]{:S(2)}, u32[]{:S(2)}) collective-permute-start(f32[5,16,512]{2,1,0:T(8,128)S(1)} %get-tuple-element.30), channel_id=1, source_target_pairs={{0,1},{1,0},{2,3},{3,2},{4,5},{5,4},{6,7},{7,6},{8,9},{9,8},{10,11... | collective-permute-start | bytes 491528 | tf_op jit(solution)/shard_map/ppermute | solution.py:436
  5.0 8.1 %collective-permute-start.1 = (f32[5,16,512]{2,1,0:T(8,128)S(1)}, f32[5,16,512]{2,1,0:T(8,128)S(1)}, u32[]{:S(2)}, u32[]{:S(2)}) collective-permute-start(f32[5,16,512]{2,1,0:T(8,128)S(1)} %get-tuple-element.32), channel_id=1, source_target_pairs={{1,2},{3,4},{5,6},{7,8},{9,10},{11,12},{13,14},{15,16},{17,18},{19... | collective-permute-start | bytes 491528 | tf_op jit(solution)/shard_map/ppermute | solution.py:435
  18.9 15.3 %copy-start.1 = (f32[4,36,512]{2,1,0:T(8,128)S(1)}, f32[4,36,512]{2,1,0:T(8,128)}, u32[]{:S(2)}) copy-start(f32[4,36,512]{2,1,0:T(8,128)} %get-tuple-element.41.kept.kept_in) | copy-start | bytes 884740
  18.9 15.3 %copy-start.2 = (f32[1,6,8,512]{3,2,1,0:T(8,128)S(1)}, f32[1,6,8,512]{3,2,1,0:T(8,128)}, u32[]{:S(2)}) copy-start(f32[1,6,8,512]{3,2,1,0:T(8,128)} %param.7) | copy-start | bytes 294916
  18.9 15.2 %copy-start.3 = (f32[6,8,512]{2,1,0:T(8,128)S(1)}, f32[6,8,512]{2,1,0:T(8,128)}, u32[]{:S(2)}) copy-start(f32[6,8,512]{2,1,0:T(8,128)} %observed.1) | copy-start | bytes 294916
  34.1 27.0 %copy-start = (f32[8,64,512]{2,1,0:T(8,128)}, f32[8,64,512]{2,1,0:T(8,128)S(1)}, u32[]{:S(2)}) copy-start(f32[8,64,512]{2,1,0:T(8,128)S(1)} %all_to_all.25.fields.fields_in) | copy-start | bytes 3145732
  34.9 1.3 %collective-permute-start.2 = (f32[8,128]{1,0:T(8,128)S(1)}, f32[8,128]{1,0:T(8,128)S(1)}, u32[]{:S(2)}, u32[]{:S(2)}) collective-permute-start(f32[8,128]{1,0:T(8,128)S(1)} %shard_map.113), channel_id=1, source_target_pairs={{0,1},{1,0},{2,3},{3,2},{4,5},{5,4},{6,7},{7,6},{8,9},{9,8},{10,11... | collective-permute-start | bytes 12296 | tf_op jit(solution)/shard_map/ppermute | solution.py:485
  66.6 2.8 %collective-permute-start.3 = (f32[192,128]{1,0:T(8,128)S(1)}, f32[192,128]{1,0:T(8,128)S(1)}, u32[]{:S(2)}, u32[]{:S(2)}) collective-permute-start(f32[192,128]{1,0:T(8,128)S(1)} %get-tuple-element.50), channel_id=1, source_target_pairs={{0,1},{1,0},{2,3},{3,2},{4,5},{5,4},{6,7},{7,6},{8,9},{9,8},{10,11... | collective-permute-start | bytes 294920 | tf_op jit(solution)/shard_map/ppermute | solution.py:509
  90.3 3.9 %collective-permute-start.4 = (f32[24,128]{1,0:T(8,128)S(1)}, f32[24,128]{1,0:T(8,128)S(1)}, u32[]{:S(2)}, u32[]{:S(2)}) collective-permute-start(f32[24,128]{1,0:T(8,128)S(1)} %reduce_sum.19), channel_id=1, source_target_pairs={{0,1},{1,0},{2,3},{3,2},{4,5},{5,4},{6,7},{7,6},{8,9},{9,8},{10,11... | collective-permute-start | bytes 36872 | tf_op jit(solution)/shard_map/ppermute | solution.py:512

commit v7 on v6

--- a/solution.py
+++ b/solution.py
@@ -136,10 +136,10 @@
 
 def forward_kernel(
     place, far, near, own, members_in, w_in, w_mid, w_out,
-    send_out, pushed, kept_out, stack_out, hidden_1_out, slope_1_out, hidden_2_out, slope_2_out,
-    send, kept, stack, hidden_1, slope_1, hidden_2, slope_2, edges, members, sems,
+    send, pushed, kept_out, stack_out, hidden_1_out, slope_1_out, hidden_2_out, slope_2_out,
+    kept, stack, hidden_1, slope_1, hidden_2, slope_2, edges, members, sems,
 ):
-    brought = pltpu.make_async_copy(members_in.at[:HALF], members, sems.at[MEMBERS + 6])
+    brought = pltpu.make_async_copy(members_in.at[:HALF], members, sems.at[6])
     brought.start()
     base = place[1]
     odd = place[2] == 1
@@ -212,8 +212,6 @@
         if 2 <= row < 2 + ROWS:
             for var in range(HALF):
                 pushed[HALF + var, row - 2 : row - 1, :] = moved[var : var + 1]
-    for member in range(MEMBERS):
-        keep(send, send_out.at[member])
     keep(kept, kept_out)
     pushed[:HALF] = members[...]
     for copy in copies:
@@ -461,19 +459,18 @@
         ((ROWS + 2, CH, LON), F32),
     ]
     rows = FIXED_AT + HALF * ROWS
-    fields_shape = ((MEMBERS, rows, LON), F32)
     kept_shape = ((4, WIDE, LON), F32)
     send, pushed, kept, stack, hidden_1, slope_1, hidden_2, slope_2 = call(
         forward_kernel,
         [SMEM] + [VMEM] * 3 + [HBM] + [VMEM] * 3,
-        [fields_shape + (HBM,), ((VARS, ROWS, LON), F32, VMEM), kept_shape + (HBM,)]
+        [((rows, LON), F32, VMEM), ((VARS, ROWS, LON), F32, VMEM), kept_shape + (HBM,)]
         + [shape + (HBM,) for shape in saved],
-        [((rows, LON), F32), kept_shape] + worked
+        [kept_shape] + worked
         + [((2 * HALO, FIELDS, LON), F32), ((HALF, ROWS, LON), F32)],
-        copies=MEMBERS + 7,
+        copies=7,
         flops=10**9,
     )(place, far, near, own, members, w_in, w_mid, w_out)
-    fields = lax.all_to_all(send, "member", 0, 0)
+    fields = spread(send, "member", MEMBERS)
     near_fields = ((MEMBERS, FIXED_AT, LON), F32)
     (partials,) = call(
         distance_kernel,

time: 104 us -> 104 us (level)
    all_to_all x1 -> x0, blocking collectives: 15.2 us -> none  [per_device(): fields = lax.all_to_all(send, 'member', 0, 0)]
    all_to_all x3 -> x4, blocking collectives: 46.4 us -> 61.4 us  [spread(): return lax.all_to_all(copies, axes, 0, 0)]
where the time goes in v7:
time: 104 us; the launch traced here: 103 us
  blocking collectives  69 us (66%)
  Pallas kernels  15.9 us (15%)
  starting transfers between devices  11.3 us (11%)
  waiting for transfers between devices  5.2 us (5%)
    all_to_all x4, blocking collectives, spread(): return lax.all_to_all(copies, axes, 0, 0)  61.4 us
    pallas_call x6, Pallas kernels, placed(): run(*[pltpu.with_memory_space_constraint(array, pltpu.HBM) if spec is HBM...  15.9 us
    all_to_all x1, blocking collectives, per_device(): lax.all_to_all(mine.reshape(MEMBERS, CHUNK, 128), 'member', 0, 0)  7.62 us
    ppermute x1, starting transfers between devices, per_device(): near = lax.ppermute(edge_near, 'core', [(0, 1), (1, 0)])  3.33 us
    ppermute x1, starting transfers between devices, per_device(): other = lax.ppermute(chunk, 'core', swap)  3.06 us
    ppermute x1, starting transfers between devices, per_device(): far = lax.ppermute(edge_far, TILE, across + [(j, i) for i, j in across])  2.99 us
    ppermute x1, waiting for transfers between devices, per_device(): far = lax.ppermute(edge_far, TILE, across + [(j, i) for i, j in across])  2.27 us
  transfers between devices with their start and end apart: 5, of which 4 were waited for; matrix products, arithmetic and copies ran while one was open for 1% of the time, Pallas kernels for 2%

profile of v7, /device:TPU:1, one launch (start us, length us, event | category | flops | bytes accessed | tf_op | source)
XLA Modules:
  0.0 103.3 jit_solution(16942376209785929145)
XLA Ops:
  0.6 1.1 %shard_map.110 = (f32[8,16,512]{2,1,0:T(8,128)S(1)}, f32[5,16,512]{2,1,0:T(8,128)S(1)}, f32[5,16,512]{2,1,0:T(8,128)S(1)}) custom-call(f32[6,8,512]{2,1,0:T(8,128)} %bitcast.13, f32[6,8,512]{2,1,0:T(8,128)} %condition_in.1, f32[6,8,512]{2,1,0:T(8,128)} %observed.1), custom_call_target="tpu_custom_call" | custom-call | flops 1000000 | bytes 1000000 | tf_op jit(solution)/shard_map/pallas_call | solution.py:406
  1.7 3.3 %collective-permute-start = (f32[5,16,512]{2,1,0:T(8,128)S(1)}, f32[5,16,512]{2,1,0:T(8,128)S(1)}, u32[]{:S(2)}, u32[]{:S(2)}) collective-permute-start(f32[5,16,512]{2,1,0:T(8,128)S(1)} %get-tuple-element.30), channel_id=1, source_target_pairs={{0,1},{1,0},{2,3},{3,2},{4,5},{5,4},{6,7},{7,6},{8,9},{9,8},{10,11... | collective-permute-start | bytes 491528 | tf_op jit(solution)/shard_map/ppermute | solution.py:434
  5.0 3.0 %collective-permute-start.1 = (f32[5,16,512]{2,1,0:T(8,128)S(1)}, f32[5,16,512]{2,1,0:T(8,128)S(1)}, u32[]{:S(2)}, u32[]{:S(2)}) collective-permute-start(f32[5,16,512]{2,1,0:T(8,128)S(1)} %get-tuple-element.32), channel_id=1, source_target_pairs={{1,2},{3,4},{5,6},{7,8},{9,10},{11,12},{13,14},{15,16},{17,18},{19... | collective-permute-start | bytes 491528 | tf_op jit(solution)/shard_map/ppermute | solution.py:433
  8.0 0.7 dynamic-slice_bitcast_fusion
  8.7 2.0 %shard_map.111 = (bf16[64,144]{1,0:T(8,128)(2,1)S(1)}, bf16[192,192]{1,0:T(8,128)(2,1)S(1)}, bf16[48,192]{1,0:T(8,128)(2,1)S(1)}, bf16[64,144]{1,0:T(8,128)(2,1)}, bf16[192,192]{1,0:T(8,128)(2,1)}) custom-call(bf16[9,9,64]{2,1,0:T(8,128)(2,1)} %bitcast.18, bf16[9,64,64]{2,1,0:T(8,128)(2,1)} %kernel_mid_in.1, bf16[9,6,64]{2,1,0:T(8,128)(2,1)} %kernel_out_in.1), custom_call_target="tpu_custom_call" | custom-call | flops 1000000 | bytes 1000000 | tf_op jit(solution)/shard_map/pallas_call | solution.py:406
  10.7 0.1 pad_add_fusion.place
  10.8 0.0 collective-permute-done.near
  10.8 0.1 broadcast_in_dim.15.lat
  10.9 2.3 %collective-permute-done.1.far = f32[5,16,512]{2,1,0:T(8,128)S(1)} collective-permute-done((f32[5,16,512]{2,1,0:T(8,128)S(1)}, f32[5,16,512]{2,1,0:T(8,128)S(1)}, u32[]{:S(2)}, u32[]{:S(2)}) %collective-permute-start.1) | collective-permute-done | bytes 163872 | tf_op jit(solution)/shard_map/ppermute | solution.py:433
  13.2 5.3 %shard_map.112 = (f32[64,512]{1,0:T(8,128)S(1)}, f32[6,8,512]{2,1,0:T(8,128)}, f32[4,36,512]{2,1,0:T(8,128)}, bf16[10,48,512]{2,1,0:T(8,128)(2,1)}, bf16[10,64,5...) custom-call(s32[3]{0:T(128)S(1)} %pad_add_fusion.place, ...), custom_call_target="tpu_custom_call" | custom-call | flops 1000000000 | bytes 1000000 | tf_op jit(solution)/shard_map/pallas_call | solution.py:406
  18.4 0.1 broadcast_in_dim.17
  18.6 0.0 copy-start.1
  18.6 0.0 copy-start.2
  18.6 0.0 copy-start.3
  18.6 15.0 %all_to_all.25.fields.fields_in = f32[8,64,512]{2,1,0:T(8,128)S(1)} all-to-all(f32[8,64,512]{2,1,0:T(8,128)S(1)} %broadcast_in_dim.17), channel_id=1, replica_groups=mesh['member'=8,'ring'=16,'core'=2] {'member'}, dimensions={0} | all-to-all | bytes 2097152 | tf_op jit(solution)/shard_map/all_to_all | solution.py:29
  33.6 0.0 copy-done.1
  33.6 0.0 copy-done.2
  33.6 0.0 copy-done.3
  33.6 0.7 shard_map.113
  34.4 0.1 collective-permute-start.2
  34.5 1.2 %collective-permute-done.2 = f32[8,128]{1,0:T(8,128)S(1)} collective-permute-done((f32[8,128]{1,0:T(8,128)S(1)}, f32[8,128]{1,0:T(8,128)S(1)}, u32[]{:S(2)}, u32[]{:S(2)}) %collective-permute-start.2) | collective-permute-done | bytes 4128 | tf_op jit(solution)/shard_map/ppermute | solution.py:482
  35.6 25.0 %all_to_all.26.totals = f32[16,8,128]{2,1,0:T(8,128)S(1)} all-to-all(f32[16,8,128]{2,1,0:T(8,128)S(1)} %broadcast_in_dim.18), channel_id=1, replica_groups=mesh['member'=8,'ring'=16,'core'=2] {'ring'}, dimensions={0} | all-to-all | bytes 131072 | tf_op jit(solution)/shard_map/all_to_all | solution.py:29
  60.6 0.0 copy-done
  60.6 5.4 %shard_map.114 = (f32[192,128]{1,0:T(8,128)S(1)}, f32[192,128]{1,0:T(8,128)S(1)}) custom-call(s32[3]{0:T(128)S(1)} %pad_add_fusion.place, f32[48,128]{1,0:T(8,128)S(1)} %broadcast_in_dim.15.lat, f32[16,8,128]{2,1,0:T(8,128)S(1)} %all_to_all.26.totals, f32[8,64,512]{2,1,0:T(8,128)} %copy-done, f32[4,36,512]{2,1,0:T(8,128)} %get-tuple-element.41.kept.kept_in, ...), custom_call_target="tpu_custom_call" | custom-call | flops 1000000000 | bytes 1000000 | tf_op jit(solution)/shard_map/pallas_call | solution.py:406
  66.0 1.8 %collective-permute-start.3 = (f32[192,128]{1,0:T(8,128)S(1)}, f32[192,128]{1,0:T(8,128)S(1)}, u32[]{:S(2)}, u32[]{:S(2)}) collective-permute-start(f32[192,128]{1,0:T(8,128)S(1)} %get-tuple-element.50), channel_id=1, source_target_pairs={{0,1},{1,0},{2,3},{3,2},{4,5},{5,4},{6,7},{7,6},{8,9},{9,8},{10,11... | collective-permute-start | bytes 294920 | tf_op jit(solution)/shard_map/ppermute | solution.py:506
  67.9 0.9 collective-permute-done.3
  68.9 7.6 %all_to_all.27 = f32[8,24,128]{2,1,0:T(8,128)S(1)} all-to-all(f32[8,24,128]{2,1,0:T(8,128)S(1)} %bitcast.16), channel_id=1, replica_groups=mesh['member'=8,'ring'=16,'core'=2] {'member'}, dimensions={0} | all-to-all | bytes 196608 | tf_op jit(solution)/shard_map/all_to_all | solution.py:507
  76.5 13.2 %all_to_all.28 = f32[16,24,128]{2,1,0:T(8,128)S(1)} all-to-all(f32[16,24,128]{2,1,0:T(8,128)S(1)} %broadcast_in_dim.19), channel_id=1, replica_groups=mesh['member'=8,'ring'=16,'core'=2] {'ring'}, dimensions={0} | all-to-all | bytes 393216 | tf_op jit(solution)/shard_map/all_to_all | solution.py:29
  89.8 3.1 %collective-permute-start.4 = (f32[24,128]{1,0:T(8,128)S(1)}, f32[24,128]{1,0:T(8,128)S(1)}, u32[]{:S(2)}, u32[]{:S(2)}) collective-permute-start(f32[24,128]{1,0:T(8,128)S(1)} %reduce_sum.19), channel_id=1, source_target_pairs={{0,1},{1,0},{2,3},{3,2},{4,5},{5,4},{6,7},{7,6},{8,9},{9,8},{10,11... | collective-permute-start | bytes 36872 | tf_op jit(solution)/shard_map/ppermute | solution.py:509
  92.8 0.8 collective-permute-done.4
  93.7 8.2 %all_to_all.29.chunks = f32[8,2,24,128]{3,2,1,0:T(8,128)S(1)} all-to-all(f32[8,2,24,128]{3,2,1,0:T(8,128)S(1)} %broadcast_in_dim.40), channel_id=1, replica_groups=mesh['member'=8,'ring'=16,'core'=2] {'member'}, dimensions={0} | all-to-all | bytes 393216 | tf_op jit(solution)/shard_map/all_to_all | solution.py:29
  101.9 1.4 %shard_map.115 = (f32[9,9,64]{2,1,0:T(8,128)}, f32[9,64,64]{2,1,0:T(8,128)}, f32[9,6,64]{2,1,0:T(8,128)}, f32[1,1]{1,0:T(1,128)}) custom-call(s32[3]{0:T(128)S(1)} %pad_add_fusion.place, f32[8,2,24,128]{3,2,1,0:T(8,128)S(1)} %all_to_all.29.chunks), custom_call_target="tpu_custom_call" | custom-call | flops 1000000 | bytes 1000000 | tf_op jit(solution)/shard_map/pallas_call | solution.py:406
  (9 shorter events, 0.1 us)
Async XLA Ops:
  1.7 9.1 %collective-permute-start = (f32[5,16,512]{2,1,0:T(8,128)S(1)}, f32[5,16,512]{2,1,0:T(8,128)S(1)}, u32[]{:S(2)}, u32[]{:S(2)}) collective-permute-start(f32[5,16,512]{2,1,0:T(8,128)S(1)} %get-tuple-element.30), channel_id=1, source_target_pairs={{0,1},{1,0},{2,3},{3,2},{4,5},{5,4},{6,7},{7,6},{8,9},{9,8},{10,11... | collective-permute-start | bytes 491528 | tf_op jit(solution)/shard_map/ppermute | solution.py:434
  5.0 8.1 %collective-permute-start.1 = (f32[5,16,512]{2,1,0:T(8,128)S(1)}, f32[5,16,512]{2,1,0:T(8,128)S(1)}, u32[]{:S(2)}, u32[]{:S(2)}) collective-permute-start(f32[5,16,512]{2,1,0:T(8,128)S(1)} %get-tuple-element.32), channel_id=1, source_target_pairs={{1,2},{3,4},{5,6},{7,8},{9,10},{11,12},{13,14},{15,16},{17,18},{19... | collective-permute-start | bytes 491528 | tf_op jit(solution)/shard_map/ppermute | solution.py:433
  18.6 15.1 %copy-start.1 = (f32[4,36,512]{2,1,0:T(8,128)S(1)}, f32[4,36,512]{2,1,0:T(8,128)}, u32[]{:S(2)}) copy-start(f32[4,36,512]{2,1,0:T(8,128)} %get-tuple-element.41.kept.kept_in) | copy-start | bytes 884740
  18.6 15.0 %copy-start.2 = (f32[1,6,8,512]{3,2,1,0:T(8,128)S(1)}, f32[1,6,8,512]{3,2,1,0:T(8,128)}, u32[]{:S(2)}) copy-start(f32[1,6,8,512]{3,2,1,0:T(8,128)} %param.7) | copy-start | bytes 294916
  18.6 15.0 %copy-start.3 = (f32[6,8,512]{2,1,0:T(8,128)S(1)}, f32[6,8,512]{2,1,0:T(8,128)}, u32[]{:S(2)}) copy-start(f32[6,8,512]{2,1,0:T(8,128)} %observed.1) | copy-start | bytes 294916
  33.6 27.0 %copy-start = (f32[8,64,512]{2,1,0:T(8,128)}, f32[8,64,512]{2,1,0:T(8,128)S(1)}, u32[]{:S(2)}) copy-start(f32[8,64,512]{2,1,0:T(8,128)S(1)} %all_to_all.25.fields.fields_in) | copy-start | bytes 3145732
  34.4 1.3 %collective-permute-start.2 = (f32[8,128]{1,0:T(8,128)S(1)}, f32[8,128]{1,0:T(8,128)S(1)}, u32[]{:S(2)}, u32[]{:S(2)}) collective-permute-start(f32[8,128]{1,0:T(8,128)S(1)} %shard_map.113), channel_id=1, source_target_pairs={{0,1},{1,0},{2,3},{3,2},{4,5},{5,4},{6,7},{7,6},{8,9},{9,8},{10,11... | collective-permute-start | bytes 12296 | tf_op jit(solution)/shard_map/ppermute | solution.py:482
  66.0 2.8 %collective-permute-start.3 = (f32[192,128]{1,0:T(8,128)S(1)}, f32[192,128]{1,0:T(8,128)S(1)}, u32[]{:S(2)}, u32[]{:S(2)}) collective-permute-start(f32[192,128]{1,0:T(8,128)S(1)} %get-tuple-element.50), channel_id=1, source_target_pairs={{0,1},{1,0},{2,3},{3,2},{4,5},{5,4},{6,7},{7,6},{8,9},{9,8},{10,11... | collective-permute-start | bytes 294920 | tf_op jit(solution)/shard_map/ppermute | solution.py:506
  89.8 3.9 %collective-permute-start.4 = (f32[24,128]{1,0:T(8,128)S(1)}, f32[24,128]{1,0:T(8,128)S(1)}, u32[]{:S(2)}, u32[]{:S(2)}) collective-permute-start(f32[24,128]{1,0:T(8,128)S(1)} %reduce_sum.19), channel_id=1, source_target_pairs={{0,1},{1,0},{2,3},{3,2},{4,5},{5,4},{6,7},{7,6},{8,9},{9,8},{10,11... | collective-permute-start | bytes 36872 | tf_op jit(solution)/shard_map/ppermute | solution.py:509

commit v8 on v7

--- a/solution.py
+++ b/solution.py
@@ -18,7 +18,11 @@
 FIELDS = 16
 INPUTS = HALF + COND
 WIDE = (ROWS + 4) * HALF
-FIXED_AT = 40
+LAT_AT = 40
+OWN = ROWS * HALF
+FAR_AT = 2 * OWN
+NEAR = 2 * HALF
+SENT = 56
 CHUNK = 24
 TILE = ("ring", "core")
 F32, BF16 = jnp.float32, jnp.bfloat16
@@ -34,11 +38,11 @@
     cosine = np.cos((-90.0 + 180.0 * (rows + 0.5) / NLAT) * (np.pi / 180.0))
     lat = (cosine / cosine.mean()).astype(np.float32)
     padded = np.pad(lat, (2, 2))
-    table = np.zeros((TILES, FIXED_AT + ROWS), np.float32)
+    table = np.zeros((TILES, LAT_AT + ROWS), np.float32)
     for tile in range(TILES):
         wide = padded[tile * ROWS : tile * ROWS + ROWS + 4]
         table[tile, :WIDE] = np.repeat(wide, HALF)
-        table[tile, FIXED_AT:] = lat[tile * ROWS : (tile + 1) * ROWS]
+        table[tile, LAT_AT:] = lat[tile * ROWS : (tile + 1) * ROWS]
     return table
 
 
@@ -82,10 +86,25 @@
         own[row, INPUTS + HALF : INPUTS + 2 * HALF, :] = observed[:, row, :]
         own[row, FIELDS - 1 :, :] = jnp.zeros((1, LON), F32)
     odd = lax.axis_index("core") == 1
-    for row in range(HALO):
-        initial, last = own[row], own[ROWS - HALO + row]
-        edge_far[row] = jnp.where(odd, last, initial)
-        edge_near[row] = jnp.where(odd, initial, last)
+    is_input = lax.broadcasted_iota(jnp.int32, (FIELDS, 1), 0) < INPUTS
+    initial = in_parts(own[0], own[1])
+    last = in_parts(own[ROWS - 2], own[ROWS - 1])
+    for row in range(HALO + 1):
+        at = min(row, HALO - 1)
+        first = jnp.where(is_input, own[at], initial[row])
+        final = jnp.where(is_input, own[ROWS - HALO + at], last[row])
+        edge_far[row] = jnp.where(odd, final, first).astype(BF16)
+        edge_near[row] = jnp.where(odd, first, final).astype(BF16)
+
+
+def in_parts(row_a, row_b):
+    parts = []
+    for value in (row_a, row_b):
+        high = value.astype(BF16).astype(F32)
+        middle = (value - high).astype(BF16).astype(F32)
+        parts.append((high, middle, value - high - middle))
+    (high_a, middle_a, low_a), (high_b, middle_b, low_b) = parts
+    return [high_a, high_b, middle_a, middle_b, low_a, low_b]
 
 
 def weights_kernel(
@@ -150,9 +169,19 @@
         copy.start()
         copies.append(copy)
 
-    for row in range(HALO):
-        edges[row] = jnp.where(odd, near[row], far[row])
-        edges[HALO + row] = jnp.where(odd, far[row], near[row])
+    is_input = lax.broadcasted_iota(jnp.int32, (FIELDS, 1), 0) < INPUTS
+    for side in range(2):
+        got = []
+        for row in range(HALO + 1):
+            one, other = far[row].astype(F32), near[row].astype(F32)
+            got.append(jnp.where(odd == (side == 0), other, one))
+        whole = [got[0] + got[2] + got[4], got[1] + got[3] + got[5]]
+        for row in range(HALO):
+            field = got[row]
+            exact = row - (HALO - 2) if side == 0 else row
+            if 0 <= exact < 2:
+                field = jnp.where(is_input, field, whole[exact])
+            edges[side * HALO + row] = field
 
     def wide(row):
         if row < HALO:
@@ -194,8 +223,7 @@
     keep(slope_2, slope_2_out)
 
     brought.wait()
-    send[WIDE:FIXED_AT, :] = jnp.zeros((FIXED_AT - WIDE, LON), F32)
-    send[FIXED_AT:, :] = members[...].reshape(HALF * ROWS, LON)
+    send[OWN:FAR_AT, :] = members[...].reshape(OWN, LON)
     for row in range(ROWS + 4):
         part = dot(w_out[...], hidden_2[row : row + 3].reshape(3 * CH, LON))
         both = turned(part[:16], 1) + part[16:32] + turned(part[32:], -1)
@@ -208,11 +236,13 @@
         kept[1, here, :] = moving
         kept[2, here, :] = field[INPUTS + HALF : INPUTS + 2 * HALF]
         kept[3, here, :] = moved
-        send[here, :] = moved
         if 2 <= row < 2 + ROWS:
+            send[(row - 2) * HALF : (row - 1) * HALF, :] = moved
             for var in range(HALF):
                 pushed[HALF + var, row - 2 : row - 1, :] = moved[var : var + 1]
     keep(kept, kept_out)
+    far_rows = jnp.where(odd, kept[3, WIDE - NEAR :, :], kept[3, :NEAR, :])
+    send[FAR_AT:, :] = jnp.concatenate([far_rows, jnp.zeros((SENT - FAR_AT - NEAR, LON), F32)], 0)
     pushed[:HALF] = members[...]
     for copy in copies:
         copy.wait()
@@ -222,21 +252,26 @@
     return sum(value[..., at : at + 128] for at in range(0, LON, 128))
 
 
-def distance_kernel(place, lat, members, observed, fields, kept, partials):
+def distance_kernel(place, lat, members, observed, fields, kept, partials, swapped):
     me = place[0]
-    spot = lax.broadcasted_iota(jnp.int32, (WIDE, 1), 0)
-    wide = jnp.where((spot >= 2 * HALF) & (spot < WIDE - 2 * HALF), lat[:WIDE, :1], 0.0)
-    low = jnp.concatenate([lat[FIXED_AT:, :1]] * HALF, 0)
-    fixed_mine = members[:HALF].reshape(HALF * ROWS, LON)
-    mine = kept[3]
+    odd = place[2] == 1
+    upper_lat = lat[NEAR : NEAR + OWN, :1]
+    lower_lat = jnp.concatenate([lat[LAT_AT:, :1]] * HALF, 0)
+    fixed_mine = members[:HALF].reshape(OWN, LON)
+    mine = kept[3, NEAR : NEAR + OWN, :]
 
     def weighed(moved, fixed):
-        upper = jnp.sum(folded(wide * (mine - moved) ** 2), 0, keepdims=True)
-        lower = jnp.sum(folded(low * (fixed_mine - fixed) ** 2), 0, keepdims=True)
+        upper = jnp.sum(folded(upper_lat * (mine - moved) ** 2), 0, keepdims=True)
+        lower = jnp.sum(folded(lower_lat * (fixed_mine - fixed) ** 2), 0, keepdims=True)
         return upper + lower
 
-    to_observed = weighed(kept[2], observed[:HALF].reshape(HALF * ROWS, LON))
-    rows = [weighed(fields[n, :WIDE], fields[n, FIXED_AT:]) for n in range(MEMBERS)]
+    seen = kept[2, NEAR : NEAR + OWN, :]
+    to_observed = weighed(seen, observed[:HALF].reshape(OWN, LON))
+    rows = []
+    for n in range(MEMBERS):
+        first, last = fields[n, :NEAR], fields[n, OWN - NEAR : OWN]
+        swapped[n * NEAR : (n + 1) * NEAR, :] = jnp.where(odd, first, last)
+        rows.append(weighed(fields[n, :OWN], fields[n, OWN:FAR_AT]))
     all_rows = jnp.concatenate(rows, 0)
     spot = lax.broadcasted_iota(jnp.int32, (MEMBERS, 128), 0)
     partials[...] = jnp.where(spot == me, to_observed, all_rows)
@@ -253,13 +288,13 @@
 
 
 def backward_kernel(
-    place, lat, totals, fields_in, kept_in, stack_in, hidden_1_in, slope_1_in, hidden_2_in,
+    place, lat, totals, near, fields_in, kept_in, stack_in, hidden_1_in, slope_1_in, hidden_2_in,
     slope_2_in, w_back_2_in, w_back_1_in,
     mine, theirs,
     fields, kept, stack, hidden_1, slope_1, hidden_2, slope_2, w_back_2, w_back_1,
     coupled, turned_2, by_row, sum_out, sum_mid, sum_in, packed, sems,
 ):
-    sources = [kept_in, fields_in.at[:, :FIXED_AT], w_back_2_in, slope_2_in]
+    sources = [kept_in, fields_in, w_back_2_in, slope_2_in]
     sources += [w_back_1_in, hidden_1_in, hidden_2_in, slope_1_in, stack_in]
     targets = [kept, fields, w_back_2, slope_2]
     targets += [w_back_1, hidden_1, hidden_2, slope_1, stack]
@@ -282,8 +317,19 @@
     log_scale, moving, observed, moved = kept[0], kept[1], kept[2], kept[3]
     inner = (moved - observed) * own_weight
     copies[1].wait()
+    odd = core == 1
+    first, last = moved[:NEAR], moved[WIDE - NEAR :]
+    near_mine, far_mine = jnp.where(odd, first, last), jnp.where(odd, last, first)
+    own_sum = jnp.zeros((OWN, LON), F32)
+    near_sum = jnp.zeros((NEAR, LON), F32)
+    far_sum = near_sum
     for n in range(MEMBERS):
-        inner = inner - weights[n : n + 1] * (moved - fields[n, :WIDE])
+        weight = weights[n : n + 1]
+        own_sum += weight * (moved[NEAR : NEAR + OWN] - fields[n, :OWN])
+        near_sum += weight * (near_mine - near[n * NEAR : (n + 1) * NEAR])
+        far_sum += weight * (far_mine - fields[n, FAR_AT : FAR_AT + NEAR])
+    first, last = jnp.where(odd, near_sum, far_sum), jnp.where(odd, far_sum, near_sum)
+    inner = inner - jnp.concatenate([first, own_sum, last], 0)
     upper = lat[:WIDE, :1] * inner / math.sqrt(ENTRIES)
     scaled = upper * moving * jnp.exp(log_scale) * (1.0 - log_scale * log_scale)
     blank = jnp.zeros((8 - HALF, LON), F32)
@@ -420,8 +466,8 @@
     place = jnp.stack([lax.axis_index("member"), tile * ROWS, core]).astype(jnp.int32)
     table = jnp.asarray(lat_table())
     lat = lax.dynamic_slice_in_dim(table, tile, 1, 0)[0]
-    lat = jnp.broadcast_to(lat[:, None], (FIXED_AT + ROWS, 128))
-    edge = ((HALO, FIELDS, LON), F32, VMEM)
+    lat = jnp.broadcast_to(lat[:, None], (LAT_AT + ROWS, 128))
+    edge = ((HALO + 1, FIELDS, LON), BF16, VMEM)
     own, edge_far, edge_near = call(
         pack_kernel,
         [HBM] * 3,
@@ -458,12 +504,11 @@
         ((ROWS + 6, CH, LON), BF16),
         ((ROWS + 2, CH, LON), F32),
     ]
-    rows = FIXED_AT + HALF * ROWS
     kept_shape = ((4, WIDE, LON), F32)
     send, pushed, kept, stack, hidden_1, slope_1, hidden_2, slope_2 = call(
         forward_kernel,
         [SMEM] + [VMEM] * 3 + [HBM] + [VMEM] * 3,
-        [((rows, LON), F32, VMEM), ((VARS, ROWS, LON), F32, VMEM), kept_shape + (HBM,)]
+        [((SENT, LON), F32, VMEM), ((VARS, ROWS, LON), F32, VMEM), kept_shape + (HBM,)]
         + [shape + (HBM,) for shape in saved],
         [kept_shape] + worked
         + [((2 * HALO, FIELDS, LON), F32), ((HALF, ROWS, LON), F32)],
@@ -471,21 +516,22 @@
         flops=10**9,
     )(place, far, near, own, members, w_in, w_mid, w_out)
     fields = spread(send, "member", MEMBERS)
-    near_fields = ((MEMBERS, FIXED_AT, LON), F32)
-    (partials,) = call(
+    fields_shape = ((MEMBERS, SENT, LON), F32)
+    partials, swapped = call(
         distance_kernel,
         [SMEM] + [VMEM] * 5,
-        [((MEMBERS, 128), F32, VMEM)],
+        [((MEMBERS, 128), F32, VMEM), ((MEMBERS * NEAR, LON), F32, VMEM)],
         vmem=8 * 10**6,
     )(place, lat, members, observed, fields, kept)
     swap = [(0, 1), (1, 0)]
+    beside = lax.ppermute(swapped, "core", swap)
     partials = partials + lax.ppermute(partials, "core", swap)
     totals = spread(partials, "ring", RING)
     mine, theirs = call(
         backward_kernel,
-        [SMEM] + [VMEM] * 2 + [HBM] * 9,
+        [SMEM] + [VMEM] * 3 + [HBM] * 9,
         [((MEMBERS * CHUNK, 128), F32, VMEM)] * 2,
-        [near_fields, kept_shape]
+        [fields_shape, kept_shape]
         + saved
         + [(shape, BF16) for shape in w_shapes[3:]]
         + [
@@ -500,7 +546,7 @@
         copies=9,
         flops=10**9,
     )(
-        place, lat, totals, fields, kept, stack, hidden_1, slope_1, hidden_2, slope_2,
+        place, lat, totals, beside, fields, kept, stack, hidden_1, slope_1, hidden_2, slope_2,
         w_back_2, w_back_1,
     )
     mine = mine + lax.ppermute(theirs, "core", swap)

time: 104 us -> 102 us (0.981)
  blocking collectives: 69 us -> 43.5 us
  starting transfers between devices: 11.3 us -> 26.6 us
  waiting for transfers between devices: 5.2 us -> 13.2 us
    all_to_all x4 -> x3, blocking collectives: 61.4 us -> 35.9 us  [spread(): return lax.all_to_all(copies, axes, 0, 0)]
    all_to_all x0 -> x1, starting transfers between devices: none -> 14.6 us  [spread(): return lax.all_to_all(copies, axes, 0, 0)]
    all_to_all x0 -> x1, waiting for transfers between devices: none -> 7.75 us  [spread(): return lax.all_to_all(copies, axes, 0, 0)]
  transfers between devices with their start and end apart: 5 -> 7, of which waited for: 4 -> 6; matrix products, arithmetic and copies ran while one was open for 1% -> 1% of each run, Pallas kernels for 2% -> 2%
where the time goes in v8:
time: 102 us
  blocking collectives  43.5 us (43%)
  starting transfers between devices  26.6 us (26%)
  Pallas kernels  16 us (16%)
  waiting for transfers between devices  13.2 us (13%)
  local copies, waits for them, and re-layouts  1.56 us (2%)
    all_to_all x3, blocking collectives, spread(): return lax.all_to_all(copies, axes, 0, 0)  35.9 us
    pallas_call x6, Pallas kernels, placed(): run(*[pltpu.with_memory_space_constraint(array, pltpu.HBM) if spec is HBM...  16 us
    all_to_all x1, starting transfers between devices, spread(): return lax.all_to_all(copies, axes, 0, 0)  14.6 us
    all_to_all x1, waiting for transfers between devices, spread(): return lax.all_to_all(copies, axes, 0, 0)  7.75 us
    all_to_all x1, blocking collectives, per_device(): lax.all_to_all(mine.reshape(MEMBERS, CHUNK, 128), 'member', 0, 0)  7.62 us
    ppermute x1, starting transfers between devices, per_device(): near = lax.ppermute(edge_near, 'core', [(0, 1), (1, 0)])  3.33 us
    ppermute x1, starting transfers between devices, per_device(): other = lax.ppermute(chunk, 'core', swap)  3.06 us
    ppermute x1, starting transfers between devices, per_device(): far = lax.ppermute(edge_far, TILE, across + [(j, i) for i, j in across])  2.99 us
  transfers between devices with their start and end apart: 7, of which 6 were waited for; matrix products, arithmetic and copies ran while one was open for 1% of the time, Pallas kernels for 2%

profile of v8, /device:TPU:1, one launch (start us, length us, event | category | flops | bytes accessed | tf_op | source)
XLA Modules:
  0.0 101.8 jit_solution(14052411240629352708)
XLA Ops:
  0.6 1.1 %shard_map.110 = (f32[8,16,512]{2,1,0:T(8,128)S(1)}, bf16[6,16,512]{2,1,0:T(8,128)(2,1)S(1)}, bf16[6,16,512]{2,1,0:T(8,128)(2,1)S(1)}) custom-call(f32[6,8,512]{2,1,0:T(8,128)} %bitcast.13, f32[6,8,512]{2,1,0:T(8,128)} %condition_in.1, f32[6,8,512]{2,1,0:T(8,128)} %observed.1), custom_call_target="tpu_custom_call" | custom-call | flops 1000000 | bytes 1000000 | tf_op jit(solution)/shard_map/pallas_call | solution.py:452
  1.7 3.3 %collective-permute-start = (bf16[6,16,512]{2,1,0:T(8,128)(2,1)S(1)}, bf16[6,16,512]{2,1,0:T(8,128)(2,1)S(1)}, u32[]{:S(2)}, u32[]{:S(2)}) collective-permute-start(bf16[6,16,512]{2,1,0:T(8,128)(2,1)S(1)} %get-tuple-element.32), channel_id=1, source_target_pairs={{0,1},{1,0},{2,3},{3,2},{4,5},{5,4},{6,7},{7,6},{8,9},{9,8},{10,11... | collective-permute-start | bytes 294920 | tf_op jit(solution)/shard_map/ppermute | solution.py:480
  5.1 3.0 %collective-permute-start.1 = (bf16[6,16,512]{2,1,0:T(8,128)(2,1)S(1)}, bf16[6,16,512]{2,1,0:T(8,128)(2,1)S(1)}, u32[]{:S(2)}, u32[]{:S(2)}) collective-permute-start(bf16[6,16,512]{2,1,0:T(8,128)(2,1)S(1)} %get-tuple-element.34), channel_id=1, source_target_pairs={{1,2},{3,4},{5,6},{7,8},{9,10},{11,12},{13,14},{15,16},{17,18},{19... | collective-permute-start | bytes 294920 | tf_op jit(solution)/shard_map/ppermute | solution.py:479
  8.1 0.7 dynamic-slice_bitcast_fusion
  8.8 2.0 %shard_map.111 = (bf16[64,144]{1,0:T(8,128)(2,1)S(1)}, bf16[192,192]{1,0:T(8,128)(2,1)S(1)}, bf16[48,192]{1,0:T(8,128)(2,1)S(1)}, bf16[64,144]{1,0:T(8,128)(2,1)}, bf16[192,192]{1,0:T(8,128)(2,1)}) custom-call(bf16[9,9,64]{2,1,0:T(8,128)(2,1)} %bitcast.18, bf16[9,64,64]{2,1,0:T(8,128)(2,1)} %kernel_mid_in.1, bf16[9,6,64]{2,1,0:T(8,128)(2,1)} %kernel_out_in.1), custom_call_target="tpu_custom_call" | custom-call | flops 1000000 | bytes 1000000 | tf_op jit(solution)/shard_map/pallas_call | solution.py:452
  10.8 0.1 pad_add_fusion.place
  10.9 0.0 collective-permute-done.near
  10.9 0.1 broadcast_in_dim.15.lat
  10.9 1.6 %collective-permute-done.1.far = bf16[6,16,512]{2,1,0:T(8,128)(2,1)S(1)} collective-permute-done((bf16[6,16,512]{2,1,0:T(8,128)(2,1)S(1)}, bf16[6,16,512]{2,1,0:T(8,128)(2,1)S(1)}, u32[]{:S(2)}, u32[]{:S(2)}) %collective-permute-start.1) | collective-permute-done | bytes 98336 | tf_op jit(solution)/shard_map/ppermute | solution.py:479
  12.5 5.3 %shard_map.112 = (f32[56,512]{1,0:T(8,128)S(1)}, f32[6,8,512]{2,1,0:T(8,128)}, f32[4,36,512]{2,1,0:T(8,128)}, bf16[10,48,512]{2,1,0:T(8,128)(2,1)}, bf16[10,64,5...) custom-call(s32[3]{0:T(128)S(1)} %pad_add_fusion.place, ...), custom_call_target="tpu_custom_call" | custom-call | flops 1000000000 | bytes 1000000 | tf_op jit(solution)/shard_map/pallas_call | solution.py:452
  17.8 0.0 copy-start.2
  17.8 0.0 copy-start.3
  17.8 0.1 broadcast_in_dim.17
  17.9 14.5 %all_to_all.25.fields.fields_in = f32[8,56,512]{2,1,0:T(8,128)S(1)} all-to-all(f32[8,56,512]{2,1,0:T(8,128)S(1)} %broadcast_in_dim.17), channel_id=1, replica_groups=mesh['member'=8,'ring'=16,'core'=2] {'member'}, dimensions={0} | all-to-all | bytes 1835008 | tf_op jit(solution)/shard_map/all_to_all | solution.py:33
  32.4 0.8 shard_map.113
  33.2 0.1 collective-permute-start.2
  33.3 1.2 %collective-permute-done.2 = f32[8,128]{1,0:T(8,128)S(1)} collective-permute-done((f32[8,128]{1,0:T(8,128)S(1)}, f32[8,128]{1,0:T(8,128)S(1)}, u32[]{:S(2)}, u32[]{:S(2)}) %collective-permute-start.2) | collective-permute-done | bytes 4128 | tf_op jit(solution)/shard_map/ppermute | solution.py:528
  34.4 0.6 broadcast_in_dim.18
  35.1 14.6 %all-to-all-start.1 = ((f32[16,8,128]{2,1,0:T(8,128)}), f32[16,8,128]{2,1,0:T(8,128)S(1)}, u32[]{:S(2)}, u32[]{:S(2)}) async-start(f32[16,8,128]{2,1,0:T(8,128)} %broadcast_in_dim.18), calls=%async_computation.1 | async-start | bytes 131072 | tf_op jit(solution)/shard_map/all_to_all | solution.py:33
  49.6 0.7 collective-permute-start.3
  50.3 0.9 collective-permute-done.3.near
  51.3 7.8 %all-to-all-done.1.totals = f32[16,8,128]{2,1,0:T(8,128)S(1)} async-done(((f32[16,8,128]{2,1,0:T(8,128)}), f32[16,8,128]{2,1,0:T(8,128)S(1)}, u32[]{:S(2)}, u32[]{:S(2)}) %all-to-all-start.1) | async-done | bytes 65568 | tf_op jit(solution)/shard_map/all_to_all | solution.py:33
  59.0 0.0 copy-done
  59.0 5.5 %shard_map.114 = (f32[192,128]{1,0:T(8,128)S(1)}, f32[192,128]{1,0:T(8,128)S(1)}) custom-call(s32[3]{0:T(128)S(1)} %pad_add_fusion.place, f32[48,128]{1,0:T(8,128)S(1)} %broadcast_in_dim.15.lat, f32[16,8,128]{2,1,0:T(8,128)S(1)} %all-to-all-done.1.totals, f32[48,512]{1,0:T(8,128)S(1)} %collective-permute-done.3.near, f32[8,56,512]{2,1,0:T(8,128)} %copy-done, ...), custom_call_target="tpu_custom_call" | custom-call | flops 1000000000 | bytes 1000000 | tf_op jit(solution)/shard_map/pallas_call | solution.py:452
  64.5 1.8 %collective-permute-start.4 = (f32[192,128]{1,0:T(8,128)S(1)}, f32[192,128]{1,0:T(8,128)S(1)}, u32[]{:S(2)}, u32[]{:S(2)}) collective-permute-start(f32[192,128]{1,0:T(8,128)S(1)} %get-tuple-element.54), channel_id=1, source_target_pairs={{0,1},{1,0},{2,3},{3,2},{4,5},{5,4},{6,7},{7,6},{8,9},{9,8},{10,11... | collective-permute-start | bytes 294920 | tf_op jit(solution)/shard_map/ppermute | solution.py:552
  66.4 0.9 collective-permute-done.4
  67.3 7.6 %all_to_all.26 = f32[8,24,128]{2,1,0:T(8,128)S(1)} all-to-all(f32[8,24,128]{2,1,0:T(8,128)S(1)} %bitcast.16), channel_id=1, replica_groups=mesh['member'=8,'ring'=16,'core'=2] {'member'}, dimensions={0} | all-to-all | bytes 196608 | tf_op jit(solution)/shard_map/all_to_all | solution.py:553
  75.0 13.2 %all_to_all.27 = f32[16,24,128]{2,1,0:T(8,128)S(1)} all-to-all(f32[16,24,128]{2,1,0:T(8,128)S(1)} %broadcast_in_dim.19), channel_id=1, replica_groups=mesh['member'=8,'ring'=16,'core'=2] {'ring'}, dimensions={0} | all-to-all | bytes 393216 | tf_op jit(solution)/shard_map/all_to_all | solution.py:33
  88.2 3.1 %collective-permute-start.5 = (f32[24,128]{1,0:T(8,128)S(1)}, f32[24,128]{1,0:T(8,128)S(1)}, u32[]{:S(2)}, u32[]{:S(2)}) collective-permute-start(f32[24,128]{1,0:T(8,128)S(1)} %reduce_sum.19), channel_id=1, source_target_pairs={{0,1},{1,0},{2,3},{3,2},{4,5},{5,4},{6,7},{7,6},{8,9},{9,8},{10,11... | collective-permute-start | bytes 36872 | tf_op jit(solution)/shard_map/ppermute | solution.py:555
  91.3 0.8 collective-permute-done.5
  92.1 8.2 %all_to_all.28.chunks = f32[8,2,24,128]{3,2,1,0:T(8,128)S(1)} all-to-all(f32[8,2,24,128]{3,2,1,0:T(8,128)S(1)} %broadcast_in_dim.40), channel_id=1, replica_groups=mesh['member'=8,'ring'=16,'core'=2] {'member'}, dimensions={0} | all-to-all | bytes 393216 | tf_op jit(solution)/shard_map/all_to_all | solution.py:33
  100.3 1.4 %shard_map.115 = (f32[9,9,64]{2,1,0:T(8,128)}, f32[9,64,64]{2,1,0:T(8,128)}, f32[9,6,64]{2,1,0:T(8,128)}, f32[1,1]{1,0:T(1,128)}) custom-call(s32[3]{0:T(128)S(1)} %pad_add_fusion.place, f32[8,2,24,128]{3,2,1,0:T(8,128)S(1)} %all_to_all.28.chunks), custom_call_target="tpu_custom_call" | custom-call | flops 1000000 | bytes 1000000 | tf_op jit(solution)/shard_map/pallas_call | solution.py:452
  (12 shorter events, 0.1 us)
Async XLA Ops:
  1.7 9.1 %collective-permute-start = (bf16[6,16,512]{2,1,0:T(8,128)(2,1)S(1)}, bf16[6,16,512]{2,1,0:T(8,128)(2,1)S(1)}, u32[]{:S(2)}, u32[]{:S(2)}) collective-permute-start(bf16[6,16,512]{2,1,0:T(8,128)(2,1)S(1)} %get-tuple-element.32), channel_id=1, source_target_pairs={{0,1},{1,0},{2,3},{3,2},{4,5},{5,4},{6,7},{7,6},{8,9},{9,8},{10,11... | collective-permute-start | bytes 294920 | tf_op jit(solution)/shard_map/ppermute | solution.py:480
  5.1 7.4 %collective-permute-start.1 = (bf16[6,16,512]{2,1,0:T(8,128)(2,1)S(1)}, bf16[6,16,512]{2,1,0:T(8,128)(2,1)S(1)}, u32[]{:S(2)}, u32[]{:S(2)}) collective-permute-start(bf16[6,16,512]{2,1,0:T(8,128)(2,1)S(1)} %get-tuple-element.34), channel_id=1, source_target_pairs={{1,2},{3,4},{5,6},{7,8},{9,10},{11,12},{13,14},{15,16},{17,18},{19... | collective-permute-start | bytes 294920 | tf_op jit(solution)/shard_map/ppermute | solution.py:479
  17.8 14.6 %copy-start.1 = (f32[4,36,512]{2,1,0:T(8,128)S(1)}, f32[4,36,512]{2,1,0:T(8,128)}, u32[]{:S(2)}) copy-start(f32[4,36,512]{2,1,0:T(8,128)} %get-tuple-element.43.kept.kept_in) | copy-start | bytes 884740
  17.8 14.6 %copy-start.2 = (f32[1,6,8,512]{3,2,1,0:T(8,128)S(1)}, f32[1,6,8,512]{3,2,1,0:T(8,128)}, u32[]{:S(2)}) copy-start(f32[1,6,8,512]{3,2,1,0:T(8,128)} %param.7) | copy-start | bytes 294916
  17.8 14.6 %copy-start.3 = (f32[6,8,512]{2,1,0:T(8,128)S(1)}, f32[6,8,512]{2,1,0:T(8,128)}, u32[]{:S(2)}) copy-start(f32[6,8,512]{2,1,0:T(8,128)} %observed.1) | copy-start | bytes 294916
  32.4 26.7 %copy-start = (f32[8,56,512]{2,1,0:T(8,128)}, f32[8,56,512]{2,1,0:T(8,128)S(1)}, u32[]{:S(2)}) copy-start(f32[8,56,512]{2,1,0:T(8,128)S(1)} %all_to_all.25.fields.fields_in) | copy-start | bytes 2752516
  33.2 1.3 %collective-permute-start.2 = (f32[8,128]{1,0:T(8,128)S(1)}, f32[8,128]{1,0:T(8,128)S(1)}, u32[]{:S(2)}, u32[]{:S(2)}) collective-permute-start(f32[8,128]{1,0:T(8,128)S(1)} %get-tuple-element.44), channel_id=1, source_target_pairs={{0,1},{1,0},{2,3},{3,2},{4,5},{5,4},{6,7},{7,6},{8,9},{9,8},{10,11... | collective-permute-start | bytes 12296 | tf_op jit(solution)/shard_map/ppermute | solution.py:528
  35.1 24.0 %all-to-all-start.1 = ((f32[16,8,128]{2,1,0:T(8,128)}), f32[16,8,128]{2,1,0:T(8,128)S(1)}, u32[]{:S(2)}, u32[]{:S(2)}) async-start(f32[16,8,128]{2,1,0:T(8,128)} %broadcast_in_dim.18), calls=%async_computation.1 | async-start | bytes 131072 | tf_op jit(solution)/shard_map/all_to_all | solution.py:33
  49.6 1.7 %collective-permute-start.3 = (f32[48,512]{1,0:T(8,128)S(1)}, f32[48,512]{1,0:T(8,128)S(1)}, u32[]{:S(2)}, u32[]{:S(2)}) collective-permute-start(f32[48,512]{1,0:T(8,128)S(1)} %get-tuple-element.45), channel_id=1, source_target_pairs={{0,1},{1,0},{2,3},{3,2},{4,5},{5,4},{6,7},{7,6},{8,9},{9,8},{10,11... | collective-permute-start | bytes 294920 | tf_op jit(solution)/shard_map/ppermute | solution.py:527
  64.5 2.8 %collective-permute-start.4 = (f32[192,128]{1,0:T(8,128)S(1)}, f32[192,128]{1,0:T(8,128)S(1)}, u32[]{:S(2)}, u32[]{:S(2)}) collective-permute-start(f32[192,128]{1,0:T(8,128)S(1)} %get-tuple-element.54), channel_id=1, source_target_pairs={{0,1},{1,0},{2,3},{3,2},{4,5},{5,4},{6,7},{7,6},{8,9},{9,8},{10,11... | collective-permute-start | bytes 294920 | tf_op jit(solution)/shard_map/ppermute | solution.py:552
  88.2 3.9 %collective-permute-start.5 = (f32[24,128]{1,0:T(8,128)S(1)}, f32[24,128]{1,0:T(8,128)S(1)}, u32[]{:S(2)}, u32[]{:S(2)}) collective-permute-start(f32[24,128]{1,0:T(8,128)S(1)} %reduce_sum.19), channel_id=1, source_target_pairs={{0,1},{1,0},{2,3},{3,2},{4,5},{5,4},{6,7},{7,6},{8,9},{9,8},{10,11... | collective-permute-start | bytes 36872 | tf_op jit(solution)/shard_map/ppermute | solution.py:555

commit v9 on v8

--- a/solution.py
+++ b/solution.py
@@ -56,6 +56,10 @@
 
 def dot_cells(left, right):
     return lax.dot_general(left, right, (((1,), (1,)), ((), ())), preferred_element_type=F32)
+
+
+def first_row():
+    return lax.axis_index(TILE) * ROWS
 
 
 def inside(base, row):
@@ -154,14 +158,13 @@
 
 
 def forward_kernel(
-    place, far, near, own, members_in, w_in, w_mid, w_out,
+    far, near, own, members_in, w_in, w_mid, w_out,
     send, pushed, kept_out, stack_out, hidden_1_out, slope_1_out, hidden_2_out, slope_2_out,
     kept, stack, hidden_1, slope_1, hidden_2, slope_2, edges, members, sems,
 ):
     brought = pltpu.make_async_copy(members_in.at[:HALF], members, sems.at[6])
     brought.start()
-    base = place[1]
-    odd = place[2] == 1
+    base, odd = first_row(), lax.axis_index("core") == 1
     copies = []
 
     def keep(source, target):
@@ -252,9 +255,8 @@
     return sum(value[..., at : at + 128] for at in range(0, LON, 128))
 
 
-def distance_kernel(place, lat, members, observed, fields, kept, partials, swapped):
-    me = place[0]
-    odd = place[2] == 1
+def distance_kernel(lat, members, observed, fields, kept, swapped):
+    me, odd = lax.axis_index("member"), lax.axis_index("core") == 1
     upper_lat = lat[NEAR : NEAR + OWN, :1]
     lower_lat = jnp.concatenate([lat[LAT_AT:, :1]] * HALF, 0)
     fixed_mine = members[:HALF].reshape(OWN, LON)
@@ -274,7 +276,8 @@
         rows.append(weighed(fields[n, :OWN], fields[n, OWN:FAR_AT]))
     all_rows = jnp.concatenate(rows, 0)
     spot = lax.broadcasted_iota(jnp.int32, (MEMBERS, 128), 0)
-    partials[...] = jnp.where(spot == me, to_observed, all_rows)
+    swapped[MEMBERS * NEAR :, :128] = jnp.where(spot == me, to_observed, all_rows)
+    swapped[MEMBERS * NEAR :, 128:] = jnp.zeros((MEMBERS, LON - 128), F32)
 
 
 def started(pairs, sems):
@@ -288,7 +291,7 @@
 
 
 def backward_kernel(
-    place, lat, totals, near, fields_in, kept_in, stack_in, hidden_1_in, slope_1_in, hidden_2_in,
+    lat, totals, near, fields_in, kept_in, stack_in, hidden_1_in, slope_1_in, hidden_2_in,
     slope_2_in, w_back_2_in, w_back_1_in,
     mine, theirs,
     fields, kept, stack, hidden_1, slope_1, hidden_2, slope_2, w_back_2, w_back_1,
@@ -299,7 +302,7 @@
     targets = [kept, fields, w_back_2, slope_2]
     targets += [w_back_1, hidden_1, hidden_2, slope_1, stack]
     copies = started(list(zip(sources, targets)), sems)
-    me, base, core = place[0], place[1], place[2]
+    me, base, core = lax.axis_index("member"), first_row(), lax.axis_index("core")
     sum_out[...] = jnp.zeros_like(sum_out)
     sum_mid[...] = jnp.zeros_like(sum_mid)
     sum_in[...] = jnp.zeros_like(sum_in)
@@ -406,8 +409,8 @@
     return (tap * CH, slice(0, CH)) if tap < 5 else ((tap - 5) * CH, slice(CH, 2 * CH))
 
 
-def unpack_kernel(place, chunks, grad_in, grad_mid, grad_out, energy, packed):
-    core = place[2]
+def unpack_kernel(chunks, grad_in, grad_mid, grad_out, energy, packed):
+    core = lax.axis_index("core")
     for member in range(MEMBERS):
         first, second = chunks[member, 0], chunks[member, 1]
         at = member * CHUNK
@@ -427,7 +430,6 @@
 VMEM_LIMIT = 28 * 10**6
 VMEM = pl.BlockSpec(memory_space=pltpu.VMEM)
 HBM = pl.BlockSpec(memory_space=pltpu.HBM)
-SMEM = pl.BlockSpec(memory_space=pltpu.SMEM)
 
 
 def call(kernel, ins, outs, scratch=(), copies=0, flops=10**6, vmem=VMEM_LIMIT):
@@ -461,9 +463,7 @@
 
 def per_device(members, condition, observed, kernel_in, kernel_mid, kernel_out):
     members = members[0]
-    core = lax.axis_index("core")
     tile = lax.axis_index(TILE)
-    place = jnp.stack([lax.axis_index("member"), tile * ROWS, core]).astype(jnp.int32)
     table = jnp.asarray(lat_table())
     lat = lax.dynamic_slice_in_dim(table, tile, 1, 0)[0]
     lat = jnp.broadcast_to(lat[:, None], (LAT_AT + ROWS, 128))
@@ -478,7 +478,7 @@
     across = [(i, i + 1) for i in range(1, TILES - 1, 2)]
     far = lax.ppermute(edge_far, TILE, across + [(j, i) for i, j in across])
     near = lax.ppermute(edge_near, "core", [(0, 1), (1, 0)])
-    near, place, lat = lax.optimization_barrier((near, place, lat))
+    near, lat = lax.optimization_barrier((near, lat))
     w_shapes = [(CH, 9 * FIELDS), (3 * CH, 3 * CH), (48, 3 * CH), (CH, 144), (3 * CH, 3 * CH)]
     w_in, w_mid, w_out, w_back_2, w_back_1 = call(
         weights_kernel,
@@ -507,29 +507,29 @@
     kept_shape = ((4, WIDE, LON), F32)
     send, pushed, kept, stack, hidden_1, slope_1, hidden_2, slope_2 = call(
         forward_kernel,
-        [SMEM] + [VMEM] * 3 + [HBM] + [VMEM] * 3,
+        [VMEM] * 3 + [HBM] + [VMEM] * 3,
         [((SENT, LON), F32, VMEM), ((VARS, ROWS, LON), F32, VMEM), kept_shape + (HBM,)]
         + [shape + (HBM,) for shape in saved],
         [kept_shape] + worked
         + [((2 * HALO, FIELDS, LON), F32), ((HALF, ROWS, LON), F32)],
         copies=7,
         flops=10**9,
-    )(place, far, near, own, members, w_in, w_mid, w_out)
+    )(far, near, own, members, w_in, w_mid, w_out)
     fields = spread(send, "member", MEMBERS)
     fields_shape = ((MEMBERS, SENT, LON), F32)
-    partials, swapped = call(
+    (swapped,) = call(
         distance_kernel,
-        [SMEM] + [VMEM] * 5,
-        [((MEMBERS, 128), F32, VMEM), ((MEMBERS * NEAR, LON), F32, VMEM)],
+        [VMEM] * 5,
+        [((MEMBERS * (NEAR + 1), LON), F32, VMEM)],
         vmem=8 * 10**6,
-    )(place, lat, members, observed, fields, kept)
+    )(lat, members, observed, fields, kept)
     swap = [(0, 1), (1, 0)]
     beside = lax.ppermute(swapped, "core", swap)
-    partials = partials + lax.ppermute(partials, "core", swap)
+    partials = swapped[MEMBERS * NEAR :, :128] + beside[MEMBERS * NEAR :, :128]
     totals = spread(partials, "ring", RING)
     mine, theirs = call(
         backward_kernel,
-        [SMEM] + [VMEM] * 3 + [HBM] * 9,
+        [VMEM] * 3 + [HBM] * 9,
         [((MEMBERS * CHUNK, 128), F32, VMEM)] * 2,
         [fields_shape, kept_shape]
         + saved
@@ -546,7 +546,7 @@
         copies=9,
         flops=10**9,
     )(
-        place, lat, totals, beside, fields, kept, stack, hidden_1, slope_1, hidden_2, slope_2,
+        lat, totals, beside, fields, kept, stack, hidden_1, slope_1, hidden_2, slope_2,
         w_back_2, w_back_1,
     )
     mine = mine + lax.ppermute(theirs, "core", swap)
@@ -556,7 +556,7 @@
     chunks = spread(jnp.stack([chunk, other]), "member", MEMBERS)
     grad_in, grad_mid, grad_out, energy = call(
         unpack_kernel,
-        [SMEM, VMEM],
+        [VMEM],
         [
             ((9, INPUTS, CH), F32, VMEM),
             ((9, CH, CH), F32, VMEM),
@@ -565,7 +565,7 @@
         ],
         [((6 * CH, 128), F32)],
         vmem=16 * 10**6,
-    )(place, chunks)
+    )(chunks)
     return (pushed[None], energy[0, 0], grad_in.transpose(0, 2, 1), grad_mid, grad_out)
 
 

time: 102 us -> 99.1 us (0.972)
  blocking collectives: 43.5 us -> 66.8 us
  starting transfers between devices: 26.6 us -> 13.6 us
  waiting for transfers between devices: 13.2 us -> 2.75 us
  Pallas kernels: 16 us -> 13.9 us
    all_to_all x3 -> x4, blocking collectives: 35.9 us -> 59.2 us  [spread(): return lax.all_to_all(copies, axes, 0, 0)]
    all_to_all x1 -> x0, starting transfers between devices: 14.6 us -> none  [spread(): return lax.all_to_all(copies, axes, 0, 0)]
    all_to_all x1 -> x0, waiting for transfers between devices: 7.75 us -> none  [spread(): return lax.all_to_all(copies, axes, 0, 0)]
    ppermute x1, starting transfers between devices: 3.33 us -> 0.09 us  [per_device(): near = lax.ppermute(edge_near, 'core', [(0, 1), (1, 0)])]
    ppermute x1, starting transfers between devices: 2.99 us -> 6.21 us  [per_device(): far = lax.ppermute(edge_far, TILE, across + [(j, i) for i, j in across])]
    pallas_call x6, Pallas kernels: 16 us -> 13.9 us  [placed(): run(*[pltpu.with_memory_space_constraint(array, pltpu.HBM) if spec is HBM...]
    ppermute x1, starting transfers between devices: 0.71 us -> 2.32 us  [per_device(): beside = lax.ppermute(swapped, 'core', swap)]
    ppermute x1, waiting for transfers between devices: 1.57 us -> 0.01 us  [per_device(): far = lax.ppermute(edge_far, TILE, across + [(j, i) for i, j in across])]
  transfers between devices with their start and end apart: 7 -> 5, of which waited for: 6 -> 3; matrix products, arithmetic and copies ran while one was open for 1% -> 1% of each run, Pallas kernels for 2% -> 2%
where the time goes in v9:
time: 99.1 us; the launch traced here: 98.7 us
  blocking collectives  66.8 us (67%)
  Pallas kernels  13.9 us (14%)
  starting transfers between devices  13.6 us (14%)
  waiting for transfers between devices  2.75 us (3%)
    all_to_all x4, blocking collectives, spread(): return lax.all_to_all(copies, axes, 0, 0)  59.2 us
    pallas_call x6, Pallas kernels, placed(): run(*[pltpu.with_memory_space_constraint(array, pltpu.HBM) if spec is HBM...  13.9 us
    all_to_all x1, blocking collectives, per_device(): lax.all_to_all(mine.reshape(MEMBERS, CHUNK, 128), 'member', 0, 0)  7.59 us
    ppermute x1, starting transfers between devices, per_device(): far = lax.ppermute(edge_far, TILE, across + [(j, i) for i, j in across])  6.21 us
    ppermute x1, starting transfers between devices, per_device(): other = lax.ppermute(chunk, 'core', swap)  3.06 us
    ppermute x1, starting transfers between devices, per_device(): beside = lax.ppermute(swapped, 'core', swap)  2.32 us
  transfers between devices with their start and end apart: 5, of which 3 were waited for; matrix products, arithmetic and copies ran while one was open for 1% of the time, Pallas kernels for 2%

profile of v9, /device:TPU:1, one launch (start us, length us, event | category | flops | bytes accessed | tf_op | source)
XLA Modules:
  0.0 98.7 jit_solution(11646469209923147524)
XLA Ops:
  0.6 1.1 %shard_map.110 = (f32[8,16,512]{2,1,0:T(8,128)S(1)}, bf16[6,16,512]{2,1,0:T(8,128)(2,1)S(1)}, bf16[6,16,512]{2,1,0:T(8,128)(2,1)S(1)}) custom-call(f32[6,8,512]{2,1,0:T(8,128)} %bitcast.10, f32[6,8,512]{2,1,0:T(8,128)} %condition_in.1, f32[6,8,512]{2,1,0:T(8,128)} %observed.1), custom_call_target="tpu_custom_call" | custom-call | flops 1000000 | bytes 1000000 | tf_op jit(solution)/shard_map/pallas_call | solution.py:454
  1.7 6.2 %collective-permute-start = (bf16[6,16,512]{2,1,0:T(8,128)(2,1)S(1)}, bf16[6,16,512]{2,1,0:T(8,128)(2,1)S(1)}, u32[]{:S(2)}, u32[]{:S(2)}) collective-permute-start(bf16[6,16,512]{2,1,0:T(8,128)(2,1)S(1)} %get-tuple-element.29), channel_id=1, source_target_pairs={{1,2},{3,4},{5,6},{7,8},{9,10},{11,12},{13,14},{15,16},{17,18},{19... | collective-permute-start | bytes 294920 | tf_op jit(solution)/shard_map/ppermute | solution.py:479
  8.0 0.1 collective-permute-start.1
  8.1 2.0 %shard_map.111 = (bf16[64,144]{1,0:T(8,128)(2,1)S(1)}, bf16[192,192]{1,0:T(8,128)(2,1)S(1)}, bf16[48,192]{1,0:T(8,128)(2,1)S(1)}, bf16[64,144]{1,0:T(8,128)(2,1)}, bf16[192,192]{1,0:T(8,128)(2,1)}) custom-call(bf16[9,9,64]{2,1,0:T(8,128)(2,1)} %bitcast.15, bf16[9,64,64]{2,1,0:T(8,128)(2,1)} %kernel_mid_in.1, bf16[9,6,64]{2,1,0:T(8,128)(2,1)} %kernel_out_in.1), custom_call_target="tpu_custom_call" | custom-call | flops 1000000 | bytes 1000000 | tf_op jit(solution)/shard_map/pallas_call | solution.py:454
  10.1 0.7 dynamic-slice_bitcast_fusion
  10.8 0.0 collective-permute-done.1.near
  10.8 0.1 broadcast_in_dim.15.lat
  10.8 0.0 collective-permute-done.far
  10.9 4.7 %shard_map.112 = (f32[56,512]{1,0:T(8,128)S(1)}, f32[6,8,512]{2,1,0:T(8,128)}, f32[4,36,512]{2,1,0:T(8,128)}, bf16[10,48,512]{2,1,0:T(8,128)(2,1)}, bf16[10,64,5...) custom-call(bf16[6,16,512]{2,1,0:T(8,128)(2,1)S(1)} %collective-permute-done.fa, ...), custom_call_target="tpu_custom_call" | custom-call | flops 1000000000 | bytes 1000000 | tf_op jit(solution)/shard_map/pallas_call | solution.py:454
  15.6 0.0 copy-start.1
  15.6 0.0 copy-start.2
  15.6 0.0 copy-start.3
  15.6 0.1 broadcast_in_dim.17
  15.7 17.0 %all_to_all.25.fields.fields_in = f32[8,56,512]{2,1,0:T(8,128)S(1)} all-to-all(f32[8,56,512]{2,1,0:T(8,128)S(1)} %broadcast_in_dim.17), channel_id=1, replica_groups=mesh['member'=8,'ring'=16,'core'=2] {'member'}, dimensions={0} | all-to-all | bytes 1835008 | tf_op jit(solution)/shard_map/all_to_all | solution.py:33
  32.7 0.0 copy-start
  32.7 0.0 copy-done.1
  32.7 0.0 copy-done.2
  32.7 0.0 copy-done.3
  32.7 0.2 shard_map.113
  32.9 2.3 %collective-permute-start.2 = (f32[56,512]{1,0:T(8,128)S(1)}, f32[56,512]{1,0:T(8,128)S(1)}, u32[]{:S(2)}, u32[]{:S(2)}) collective-permute-start(f32[56,512]{1,0:T(8,128)S(1)} %shard_map.113), channel_id=1, source_target_pairs={{0,1},{1,0},{2,3},{3,2},{4,5},{5,4},{6,7},{7,6},{8,9},{9,8},{10,11... | collective-permute-start | bytes 344072 | tf_op jit(solution)/shard_map/ppermute | solution.py:527
  35.3 1.0 collective-permute-done.2.near
  36.2 20.8 %all_to_all.26.totals = f32[16,8,128]{2,1,0:T(8,128)S(1)} all-to-all(f32[16,8,128]{2,1,0:T(8,128)S(1)} %broadcast_in_dim.18), channel_id=1, replica_groups=mesh['member'=8,'ring'=16,'core'=2] {'ring'}, dimensions={0} | all-to-all | bytes 131072 | tf_op jit(solution)/shard_map/all_to_all | solution.py:33
  57.1 0.0 copy-done
  57.1 4.9 %shard_map.114 = (f32[192,128]{1,0:T(8,128)S(1)}, f32[192,128]{1,0:T(8,128)S(1)}) custom-call(f32[48,128]{1,0:T(8,128)S(1)} %broadcast_in_dim.15.lat, f32[16,8,128]{2,1,0:T(8,128)S(1)} %all_to_all.26.totals, f32[56,512]{1,0:T(8,128)S(1)} %collective-permute-done.2.near, f32[8,56,512]{2,1,0:T(8,128)} %copy-done, ...), custom_call_target="tpu_custom_call" | custom-call | flops 1000000000 | bytes 1000000 | tf_op jit(solution)/shard_map/pallas_call | solution.py:454
  62.0 1.9 %collective-permute-start.3 = (f32[192,128]{1,0:T(8,128)S(1)}, f32[192,128]{1,0:T(8,128)S(1)}, u32[]{:S(2)}, u32[]{:S(2)}) collective-permute-start(f32[192,128]{1,0:T(8,128)S(1)} %get-tuple-element.48), channel_id=1, source_target_pairs={{0,1},{1,0},{2,3},{3,2},{4,5},{5,4},{6,7},{7,6},{8,9},{9,8},{10,11... | collective-permute-start | bytes 294920 | tf_op jit(solution)/shard_map/ppermute | solution.py:552
  63.9 0.9 collective-permute-done.3
  64.9 7.6 %all_to_all.27 = f32[8,24,128]{2,1,0:T(8,128)S(1)} all-to-all(f32[8,24,128]{2,1,0:T(8,128)S(1)} %bitcast.13), channel_id=1, replica_groups=mesh['member'=8,'ring'=16,'core'=2] {'member'}, dimensions={0} | all-to-all | bytes 196608 | tf_op jit(solution)/shard_map/all_to_all | solution.py:553
  72.5 13.2 %all_to_all.28 = f32[16,24,128]{2,1,0:T(8,128)S(1)} all-to-all(f32[16,24,128]{2,1,0:T(8,128)S(1)} %broadcast_in_dim.19), channel_id=1, replica_groups=mesh['member'=8,'ring'=16,'core'=2] {'ring'}, dimensions={0} | all-to-all | bytes 393216 | tf_op jit(solution)/shard_map/all_to_all | solution.py:33
  85.7 3.1 %collective-permute-start.4 = (f32[24,128]{1,0:T(8,128)S(1)}, f32[24,128]{1,0:T(8,128)S(1)}, u32[]{:S(2)}, u32[]{:S(2)}) collective-permute-start(f32[24,128]{1,0:T(8,128)S(1)} %reduce_sum.19), channel_id=1, source_target_pairs={{0,1},{1,0},{2,3},{3,2},{4,5},{5,4},{6,7},{7,6},{8,9},{9,8},{10,11... | collective-permute-start | bytes 36872 | tf_op jit(solution)/shard_map/ppermute | solution.py:555
  88.8 0.8 collective-permute-done.4
  89.6 8.2 %all_to_all.29.chunks = f32[8,2,24,128]{3,2,1,0:T(8,128)S(1)} all-to-all(f32[8,2,24,128]{3,2,1,0:T(8,128)S(1)} %broadcast_in_dim.40), channel_id=1, replica_groups=mesh['member'=8,'ring'=16,'core'=2] {'member'}, dimensions={0} | all-to-all | bytes 393216 | tf_op jit(solution)/shard_map/all_to_all | solution.py:33
  97.8 0.9 shard_map.115
  (8 shorter events, 0.1 us)
Async XLA Ops:
  1.7 9.1 %collective-permute-start = (bf16[6,16,512]{2,1,0:T(8,128)(2,1)S(1)}, bf16[6,16,512]{2,1,0:T(8,128)(2,1)S(1)}, u32[]{:S(2)}, u32[]{:S(2)}) collective-permute-start(bf16[6,16,512]{2,1,0:T(8,128)(2,1)S(1)} %get-tuple-element.29), channel_id=1, source_target_pairs={{1,2},{3,4},{5,6},{7,8},{9,10},{11,12},{13,14},{15,16},{17,18},{19... | collective-permute-start | bytes 294920 | tf_op jit(solution)/shard_map/ppermute | solution.py:479
  8.0 2.8 %collective-permute-start.1 = (bf16[6,16,512]{2,1,0:T(8,128)(2,1)S(1)}, bf16[6,16,512]{2,1,0:T(8,128)(2,1)S(1)}, u32[]{:S(2)}, u32[]{:S(2)}) collective-permute-start(bf16[6,16,512]{2,1,0:T(8,128)(2,1)S(1)} %get-tuple-element.30), channel_id=1, source_target_pairs={{0,1},{1,0},{2,3},{3,2},{4,5},{5,4},{6,7},{7,6},{8,9},{9,8},{10,11... | collective-permute-start | bytes 294920 | tf_op jit(solution)/shard_map/ppermute | solution.py:480
  15.6 17.1 %copy-start.1 = (f32[4,36,512]{2,1,0:T(8,128)S(1)}, f32[4,36,512]{2,1,0:T(8,128)}, u32[]{:S(2)}) copy-start(f32[4,36,512]{2,1,0:T(8,128)} %get-tuple-element.39.kept.kept_in) | copy-start | bytes 884740
  15.6 17.1 %copy-start.2 = (f32[1,6,8,512]{3,2,1,0:T(8,128)S(1)}, f32[1,6,8,512]{3,2,1,0:T(8,128)}, u32[]{:S(2)}) copy-start(f32[1,6,8,512]{3,2,1,0:T(8,128)} %param.7) | copy-start | bytes 294916
  15.6 17.1 %copy-start.3 = (f32[6,8,512]{2,1,0:T(8,128)S(1)}, f32[6,8,512]{2,1,0:T(8,128)}, u32[]{:S(2)}) copy-start(f32[6,8,512]{2,1,0:T(8,128)} %observed.1) | copy-start | bytes 294916
  32.7 24.4 %copy-start = (f32[8,56,512]{2,1,0:T(8,128)}, f32[8,56,512]{2,1,0:T(8,128)S(1)}, u32[]{:S(2)}) copy-start(f32[8,56,512]{2,1,0:T(8,128)S(1)} %all_to_all.25.fields.fields_in) | copy-start | bytes 2752516
  32.9 3.3 %collective-permute-start.2 = (f32[56,512]{1,0:T(8,128)S(1)}, f32[56,512]{1,0:T(8,128)S(1)}, u32[]{:S(2)}, u32[]{:S(2)}) collective-permute-start(f32[56,512]{1,0:T(8,128)S(1)} %shard_map.113), channel_id=1, source_target_pairs={{0,1},{1,0},{2,3},{3,2},{4,5},{5,4},{6,7},{7,6},{8,9},{9,8},{10,11... | collective-permute-start | bytes 344072 | tf_op jit(solution)/shard_map/ppermute | solution.py:527
  62.0 2.8 %collective-permute-start.3 = (f32[192,128]{1,0:T(8,128)S(1)}, f32[192,128]{1,0:T(8,128)S(1)}, u32[]{:S(2)}, u32[]{:S(2)}) collective-permute-start(f32[192,128]{1,0:T(8,128)S(1)} %get-tuple-element.48), channel_id=1, source_target_pairs={{0,1},{1,0},{2,3},{3,2},{4,5},{5,4},{6,7},{7,6},{8,9},{9,8},{10,11... | collective-permute-start | bytes 294920 | tf_op jit(solution)/shard_map/ppermute | solution.py:552
  85.7 3.9 %collective-permute-start.4 = (f32[24,128]{1,0:T(8,128)S(1)}, f32[24,128]{1,0:T(8,128)S(1)}, u32[]{:S(2)}, u32[]{:S(2)}) collective-permute-start(f32[24,128]{1,0:T(8,128)S(1)} %reduce_sum.19), channel_id=1, source_target_pairs={{0,1},{1,0},{2,3},{3,2},{4,5},{5,4},{6,7},{7,6},{8,9},{9,8},{10,11... | collective-permute-start | bytes 36872 | tf_op jit(solution)/shard_map/ppermute | solution.py:555

commit v10 on v9

--- a/solution.py
+++ b/solution.py
@@ -410,13 +410,10 @@
 
 
 def unpack_kernel(chunks, grad_in, grad_mid, grad_out, energy, packed):
-    core = lax.axis_index("core")
     for member in range(MEMBERS):
-        first, second = chunks[member, 0], chunks[member, 1]
-        at = member * CHUNK
-        packed[at : at + CHUNK, :] = jnp.where(core == 0, first, second)
-        at += MEMBERS * CHUNK
-        packed[at : at + CHUNK, :] = jnp.where(core == 0, second, first)
+        for half in range(2):
+            at = (half * MEMBERS + member) * CHUNK
+            packed[at : at + CHUNK, :] = chunks[member * 2 + half]
     for tap in range(9):
         at, side = place_mid(tap)
         grad_mid[tap] = packed[at : at + CH, side]
@@ -552,8 +549,7 @@
     mine = mine + lax.ppermute(theirs, "core", swap)
     chunk = jnp.sum(lax.all_to_all(mine.reshape(MEMBERS, CHUNK, 128), "member", 0, 0), 0)
     chunk = jnp.sum(spread(chunk, "ring", RING), 0)
-    other = lax.ppermute(chunk, "core", swap)
-    chunks = spread(jnp.stack([chunk, other]), "member", MEMBERS)
+    chunks = spread(chunk, ("member", "core"), 2 * MEMBERS)
     grad_in, grad_mid, grad_out, energy = call(
         unpack_kernel,
         [VMEM],

time: 99.1 us -> 99.4 us (level)
  blocking collectives: 66.8 us -> 71 us
  starting transfers between devices: 13.6 us -> 10.5 us
    all_to_all x4, blocking collectives: 59.2 us -> 63.4 us  [spread(): return lax.all_to_all(copies, axes, 0, 0)]
    ppermute x1 -> x0, starting transfers between devices: 3.06 us -> none  [per_device(): other = lax.ppermute(chunk, 'core', swap)]
  transfers between devices with their start and end apart: 5 -> 4, of which waited for: 3 -> 2; matrix products, arithmetic and copies ran while one was open for 1% -> 1% of each run, Pallas kernels for 2% -> 2%
where the time goes in v10:
time: 99.4 us; the launch traced here: 99 us
  blocking collectives  71 us (71%)
  Pallas kernels  13.9 us (14%)
  starting transfers between devices  10.5 us (11%)
  waiting for transfers between devices  1.91 us (2%)
    all_to_all x4, blocking collectives, spread(): return lax.all_to_all(copies, axes, 0, 0)  63.4 us
    pallas_call x6, Pallas kernels, placed(): run(*[pltpu.with_memory_space_constraint(array, pltpu.HBM) if spec is HBM...  13.9 us
    all_to_all x1, blocking collectives, per_device(): lax.all_to_all(mine.reshape(MEMBERS, CHUNK, 128), 'member', 0, 0)  7.59 us
    ppermute x1, starting transfers between devices, per_device(): far = lax.ppermute(edge_far, TILE, across + [(j, i) for i, j in across])  6.21 us
    ppermute x1, starting transfers between devices, per_device(): beside = lax.ppermute(swapped, 'core', swap)  2.32 us
  transfers between devices with their start and end apart: 4, of which 2 were waited for; matrix products, arithmetic and copies ran while one was open for 1% of the time, Pallas kernels for 2%

profile of v10, /device:TPU:1, one launch (start us, length us, event | category | flops | bytes accessed | tf_op | source)
XLA Modules:
  0.0 99.0 jit_solution(15183987296958012450)
XLA Ops:
  0.6 1.1 %shard_map.110 = (f32[8,16,512]{2,1,0:T(8,128)S(1)}, bf16[6,16,512]{2,1,0:T(8,128)(2,1)S(1)}, bf16[6,16,512]{2,1,0:T(8,128)(2,1)S(1)}) custom-call(f32[6,8,512]{2,1,0:T(8,128)} %bitcast.8, f32[6,8,512]{2,1,0:T(8,128)} %condition_in.1, f32[6,8,512]{2,1,0:T(8,128)} %observed.1), custom_call_target="tpu_custom_call" | custom-call | flops 1000000 | bytes 1000000 | tf_op jit(solution)/shard_map/pallas_call | solution.py:451
  1.7 6.2 %collective-permute-start = (bf16[6,16,512]{2,1,0:T(8,128)(2,1)S(1)}, bf16[6,16,512]{2,1,0:T(8,128)(2,1)S(1)}, u32[]{:S(2)}, u32[]{:S(2)}) collective-permute-start(bf16[6,16,512]{2,1,0:T(8,128)(2,1)S(1)} %get-tuple-element.29), channel_id=1, source_target_pairs={{1,2},{3,4},{5,6},{7,8},{9,10},{11,12},{13,14},{15,16},{17,18},{19... | collective-permute-start | bytes 294920 | tf_op jit(solution)/shard_map/ppermute | solution.py:476
  8.0 0.1 collective-permute-start.1
  8.1 2.0 %shard_map.111 = (bf16[64,144]{1,0:T(8,128)(2,1)S(1)}, bf16[192,192]{1,0:T(8,128)(2,1)S(1)}, bf16[48,192]{1,0:T(8,128)(2,1)S(1)}, bf16[64,144]{1,0:T(8,128)(2,1)}, bf16[192,192]{1,0:T(8,128)(2,1)}) custom-call(bf16[9,9,64]{2,1,0:T(8,128)(2,1)} %bitcast.12, bf16[9,64,64]{2,1,0:T(8,128)(2,1)} %kernel_mid_in.1, bf16[9,6,64]{2,1,0:T(8,128)(2,1)} %kernel_out_in.1), custom_call_target="tpu_custom_call" | custom-call | flops 1000000 | bytes 1000000 | tf_op jit(solution)/shard_map/pallas_call | solution.py:451
  10.1 0.7 dynamic-slice_bitcast_fusion
  10.8 0.0 collective-permute-done.1.near
  10.8 0.1 broadcast_in_dim.15.lat
  10.8 0.0 collective-permute-done.far
  10.9 4.7 %shard_map.112 = (f32[56,512]{1,0:T(8,128)S(1)}, f32[6,8,512]{2,1,0:T(8,128)}, f32[4,36,512]{2,1,0:T(8,128)}, bf16[10,48,512]{2,1,0:T(8,128)(2,1)}, bf16[10,64,5...) custom-call(bf16[6,16,512]{2,1,0:T(8,128)(2,1)S(1)} %collective-permute-done.fa, ...), custom_call_target="tpu_custom_call" | custom-call | flops 1000000000 | bytes 1000000 | tf_op jit(solution)/shard_map/pallas_call | solution.py:451
  15.6 0.0 copy-start.1
  15.6 0.0 copy-start.2
  15.6 0.0 copy-start.3
  15.6 0.1 broadcast_in_dim.17
  15.7 17.0 %all_to_all.25.fields.fields_in = f32[8,56,512]{2,1,0:T(8,128)S(1)} all-to-all(f32[8,56,512]{2,1,0:T(8,128)S(1)} %broadcast_in_dim.17), channel_id=1, replica_groups=mesh['member'=8,'ring'=16,'core'=2] {'member'}, dimensions={0} | all-to-all | bytes 1835008 | tf_op jit(solution)/shard_map/all_to_all | solution.py:33
  32.7 0.0 copy-start
  32.7 0.0 copy-done.1
  32.7 0.0 copy-done.2
  32.7 0.0 copy-done.3
  32.7 0.2 shard_map.113
  32.9 2.3 %collective-permute-start.2 = (f32[56,512]{1,0:T(8,128)S(1)}, f32[56,512]{1,0:T(8,128)S(1)}, u32[]{:S(2)}, u32[]{:S(2)}) collective-permute-start(f32[56,512]{1,0:T(8,128)S(1)} %shard_map.113), channel_id=1, source_target_pairs={{0,1},{1,0},{2,3},{3,2},{4,5},{5,4},{6,7},{7,6},{8,9},{9,8},{10,11... | collective-permute-start | bytes 344072 | tf_op jit(solution)/shard_map/ppermute | solution.py:524
  35.3 1.0 collective-permute-done.2.near
  36.2 20.8 %all_to_all.26.totals = f32[16,8,128]{2,1,0:T(8,128)S(1)} all-to-all(f32[16,8,128]{2,1,0:T(8,128)S(1)} %broadcast_in_dim.18), channel_id=1, replica_groups=mesh['member'=8,'ring'=16,'core'=2] {'ring'}, dimensions={0} | all-to-all | bytes 131072 | tf_op jit(solution)/shard_map/all_to_all | solution.py:33
  57.1 0.0 copy-done
  57.1 4.9 %shard_map.114 = (f32[192,128]{1,0:T(8,128)S(1)}, f32[192,128]{1,0:T(8,128)S(1)}) custom-call(f32[48,128]{1,0:T(8,128)S(1)} %broadcast_in_dim.15.lat, f32[16,8,128]{2,1,0:T(8,128)S(1)} %all_to_all.26.totals, f32[56,512]{1,0:T(8,128)S(1)} %collective-permute-done.2.near, f32[8,56,512]{2,1,0:T(8,128)} %copy-done, ...), custom_call_target="tpu_custom_call" | custom-call | flops 1000000000 | bytes 1000000 | tf_op jit(solution)/shard_map/pallas_call | solution.py:451
  62.0 1.9 %collective-permute-start.3 = (f32[192,128]{1,0:T(8,128)S(1)}, f32[192,128]{1,0:T(8,128)S(1)}, u32[]{:S(2)}, u32[]{:S(2)}) collective-permute-start(f32[192,128]{1,0:T(8,128)S(1)} %get-tuple-element.48), channel_id=1, source_target_pairs={{0,1},{1,0},{2,3},{3,2},{4,5},{5,4},{6,7},{7,6},{8,9},{9,8},{10,11... | collective-permute-start | bytes 294920 | tf_op jit(solution)/shard_map/ppermute | solution.py:549
  63.9 0.9 collective-permute-done.3
  64.9 7.6 %all_to_all.27 = f32[8,24,128]{2,1,0:T(8,128)S(1)} all-to-all(f32[8,24,128]{2,1,0:T(8,128)S(1)} %bitcast.11), channel_id=1, replica_groups=mesh['member'=8,'ring'=16,'core'=2] {'member'}, dimensions={0} | all-to-all | bytes 196608 | tf_op jit(solution)/shard_map/all_to_all | solution.py:550
  72.5 13.2 %all_to_all.28 = f32[16,24,128]{2,1,0:T(8,128)S(1)} all-to-all(f32[16,24,128]{2,1,0:T(8,128)S(1)} %broadcast_in_dim.19), channel_id=1, replica_groups=mesh['member'=8,'ring'=16,'core'=2] {'ring'}, dimensions={0} | all-to-all | bytes 393216 | tf_op jit(solution)/shard_map/all_to_all | solution.py:33
  85.7 12.4 %all_to_all.29.chunks = f32[16,24,128]{2,1,0:T(8,128)S(1)} all-to-all(f32[16,24,128]{2,1,0:T(8,128)S(1)} %broadcast_in_dim.40), channel_id=1, replica_groups=mesh['member'=8,'ring'=16,'core'=2] {'member','core'}, dimensions={0} | all-to-all | bytes 393216 | tf_op jit(solution)/shard_map/all_to_all | solution.py:33
  98.1 0.9 shard_map.115
  (7 shorter events, 0.1 us)
Async XLA Ops:
  1.7 9.1 %collective-permute-start = (bf16[6,16,512]{2,1,0:T(8,128)(2,1)S(1)}, bf16[6,16,512]{2,1,0:T(8,128)(2,1)S(1)}, u32[]{:S(2)}, u32[]{:S(2)}) collective-permute-start(bf16[6,16,512]{2,1,0:T(8,128)(2,1)S(1)} %get-tuple-element.29), channel_id=1, source_target_pairs={{1,2},{3,4},{5,6},{7,8},{9,10},{11,12},{13,14},{15,16},{17,18},{19... | collective-permute-start | bytes 294920 | tf_op jit(solution)/shard_map/ppermute | solution.py:476
  8.0 2.8 %collective-permute-start.1 = (bf16[6,16,512]{2,1,0:T(8,128)(2,1)S(1)}, bf16[6,16,512]{2,1,0:T(8,128)(2,1)S(1)}, u32[]{:S(2)}, u32[]{:S(2)}) collective-permute-start(bf16[6,16,512]{2,1,0:T(8,128)(2,1)S(1)} %get-tuple-element.30), channel_id=1, source_target_pairs={{0,1},{1,0},{2,3},{3,2},{4,5},{5,4},{6,7},{7,6},{8,9},{9,8},{10,11... | collective-permute-start | bytes 294920 | tf_op jit(solution)/shard_map/ppermute | solution.py:477
  15.6 17.1 %copy-start.1 = (f32[4,36,512]{2,1,0:T(8,128)S(1)}, f32[4,36,512]{2,1,0:T(8,128)}, u32[]{:S(2)}) copy-start(f32[4,36,512]{2,1,0:T(8,128)} %get-tuple-element.39.kept.kept_in) | copy-start | bytes 884740
  15.6 17.1 %copy-start.2 = (f32[1,6,8,512]{3,2,1,0:T(8,128)S(1)}, f32[1,6,8,512]{3,2,1,0:T(8,128)}, u32[]{:S(2)}) copy-start(f32[1,6,8,512]{3,2,1,0:T(8,128)} %param.7) | copy-start | bytes 294916
  15.6 17.1 %copy-start.3 = (f32[6,8,512]{2,1,0:T(8,128)S(1)}, f32[6,8,512]{2,1,0:T(8,128)}, u32[]{:S(2)}) copy-start(f32[6,8,512]{2,1,0:T(8,128)} %observed.1) | copy-start | bytes 294916
  32.7 24.4 %copy-start = (f32[8,56,512]{2,1,0:T(8,128)}, f32[8,56,512]{2,1,0:T(8,128)S(1)}, u32[]{:S(2)}) copy-start(f32[8,56,512]{2,1,0:T(8,128)S(1)} %all_to_all.25.fields.fields_in) | copy-start | bytes 2752516
  32.9 3.3 %collective-permute-start.2 = (f32[56,512]{1,0:T(8,128)S(1)}, f32[56,512]{1,0:T(8,128)S(1)}, u32[]{:S(2)}, u32[]{:S(2)}) collective-permute-start(f32[56,512]{1,0:T(8,128)S(1)} %shard_map.113), channel_id=1, source_target_pairs={{0,1},{1,0},{2,3},{3,2},{4,5},{5,4},{6,7},{7,6},{8,9},{9,8},{10,11... | collective-permute-start | bytes 344072 | tf_op jit(solution)/shard_map/ppermute | solution.py:524
  62.0 2.8 %collective-permute-start.3 = (f32[192,128]{1,0:T(8,128)S(1)}, f32[192,128]{1,0:T(8,128)S(1)}, u32[]{:S(2)}, u32[]{:S(2)}) collective-permute-start(f32[192,128]{1,0:T(8,128)S(1)} %get-tuple-element.48), channel_id=1, source_target_pairs={{0,1},{1,0},{2,3},{3,2},{4,5},{5,4},{6,7},{7,6},{8,9},{9,8},{10,11... | collective-permute-start | bytes 294920 | tf_op jit(solution)/shard_map/ppermute | solution.py:549

commit v11 on v9

--- a/solution.py
+++ b/solution.py
@@ -159,19 +159,11 @@
 
 def forward_kernel(
     far, near, own, members_in, w_in, w_mid, w_out,
-    send, pushed, kept_out, stack_out, hidden_1_out, slope_1_out, hidden_2_out, slope_2_out,
-    kept, stack, hidden_1, slope_1, hidden_2, slope_2, edges, members, sems,
+    send, pushed, kept, stack, hidden_1, slope_1, hidden_2, slope_2, edges, members, sems,
 ):
-    brought = pltpu.make_async_copy(members_in.at[:HALF], members, sems.at[6])
+    brought = pltpu.make_async_copy(members_in.at[:HALF], members, sems.at[0])
     brought.start()
     base, odd = first_row(), lax.axis_index("core") == 1
-    copies = []
-
-    def keep(source, target):
-        copy = pltpu.make_async_copy(source, target, sems.at[len(copies)])
-        copy.start()
-        copies.append(copy)
-
     is_input = lax.broadcasted_iota(jnp.int32, (FIELDS, 1), 0) < INPUTS
     for side in range(2):
         got = []
@@ -196,7 +188,6 @@
         for shift in range(3):
             part = turned(field, 1 - shift).astype(BF16)
             stack[row, shift * FIELDS : (shift + 1) * FIELDS, :] = part
-    keep(stack.at[4:14], stack_out)
 
     def first(row, kept_row):
         pre = dot(w_in[...], stack[pl.ds(row, 3)].reshape(9 * FIELDS, LON))
@@ -208,8 +199,6 @@
     loop(0, 4, functools.partial(first, kept_row=False))
     loop(4, 12, functools.partial(first, kept_row=True))
     loop(12, 16, functools.partial(first, kept_row=False))
-    keep(hidden_1.at[3:13], hidden_1_out)
-    keep(slope_1, slope_1_out)
 
     def second(row, kept_row):
         part = dot(w_mid[...], hidden_1[pl.ds(row, 3)].reshape(3 * CH, LON))
@@ -222,8 +211,6 @@
     loop(0, 2, functools.partial(second, kept_row=False))
     loop(2, 12, functools.partial(second, kept_row=True))
     loop(12, 14, functools.partial(second, kept_row=False))
-    keep(hidden_2.at[2:12], hidden_2_out)
-    keep(slope_2, slope_2_out)
 
     brought.wait()
     send[OWN:FAR_AT, :] = members[...].reshape(OWN, LON)
@@ -243,12 +230,9 @@
             send[(row - 2) * HALF : (row - 1) * HALF, :] = moved
             for var in range(HALF):
                 pushed[HALF + var, row - 2 : row - 1, :] = moved[var : var + 1]
-    keep(kept, kept_out)
     far_rows = jnp.where(odd, kept[3, WIDE - NEAR :, :], kept[3, :NEAR, :])
     send[FAR_AT:, :] = jnp.concatenate([far_rows, jnp.zeros((SENT - FAR_AT - NEAR, LON), F32)], 0)
     pushed[:HALF] = members[...]
-    for copy in copies:
-        copy.wait()
 
 
 def folded(value):
@@ -291,17 +275,12 @@
 
 
 def backward_kernel(
-    lat, totals, near, fields_in, kept_in, stack_in, hidden_1_in, slope_1_in, hidden_2_in,
-    slope_2_in, w_back_2_in, w_back_1_in,
+    lat, totals, near, fields, kept, stack, hidden_1, slope_1, hidden_2, slope_2, w_back_2_in, w_back_1_in,
     mine, theirs,
-    fields, kept, stack, hidden_1, slope_1, hidden_2, slope_2, w_back_2, w_back_1,
+    w_back_2, w_back_1,
     coupled, turned_2, by_row, sum_out, sum_mid, sum_in, packed, sems,
 ):
-    sources = [kept_in, fields_in, w_back_2_in, slope_2_in]
-    sources += [w_back_1_in, hidden_1_in, hidden_2_in, slope_1_in, stack_in]
-    targets = [kept, fields, w_back_2, slope_2]
-    targets += [w_back_1, hidden_1, hidden_2, slope_1, stack]
-    copies = started(list(zip(sources, targets)), sems)
+    copies = started([(w_back_2_in, w_back_2), (w_back_1_in, w_back_1)], sems)
     me, base, core = lax.axis_index("member"), first_row(), lax.axis_index("core")
     sum_out[...] = jnp.zeros_like(sum_out)
     sum_mid[...] = jnp.zeros_like(sum_mid)
@@ -316,10 +295,8 @@
     weights = 1.0 / (jnp.where(is_me, MEMBERS, MEMBERS * MEMBERS) * distances)
     own_weight = jnp.sum(jnp.where(is_me, weights, 0.0), 0, keepdims=True)
     weights = jnp.where(is_me, 0.0, weights)
-    copies[0].wait()
     log_scale, moving, observed, moved = kept[0], kept[1], kept[2], kept[3]
     inner = (moved - observed) * own_weight
-    copies[1].wait()
     odd = core == 1
     first, last = moved[:NEAR], moved[WIDE - NEAR :]
     near_mine, far_mine = jnp.where(odd, first, last), jnp.where(odd, last, first)
@@ -342,8 +319,7 @@
         for shift in range(3):
             part = turned(field, shift - 1).astype(BF16)
             coupled[row, shift * 16 : (shift + 1) * 16, :] = part
-    copies[2].wait()
-    copies[3].wait()
+    copies[0].wait()
 
     def second(row):
         back = dot(w_back_2[...], coupled[pl.ds(row, 3)].reshape(144, LON))
@@ -353,33 +329,29 @@
             turned_2[row, shift * CH : (shift + 1) * CH, :] = part
 
     loop(0, ROWS + 2, second)
-    copies[4].wait()
+    copies[1].wait()
 
     def across_rows(row):
         by_row[row] = dot(w_back_1[...], turned_2[row])
 
     loop(0, ROWS + 2, across_rows)
-    copies[5].wait()
 
     def middle(row):
-        near = hidden_1[pl.ds(row, 3)].reshape(3 * CH, LON)
+        near = hidden_1[pl.ds(row + 3, 3)].reshape(3 * CH, LON)
         sum_mid[...] += dot_cells(turned_2[row + 1], near)
 
     loop(0, ROWS, middle)
-    copies[6].wait()
 
     def outer(row):
-        near = hidden_2[pl.ds(row, 3)].reshape(3 * CH, LON)
+        near = hidden_2[pl.ds(row + 2, 3)].reshape(3 * CH, LON)
         sum_out[...] += dot_cells(coupled[row + 2], near)
 
     loop(0, ROWS, outer)
-    copies[7].wait()
-    copies[8].wait()
 
     def last(row):
         back = by_row[row + 2, :CH] + by_row[row + 1, CH : 2 * CH] + by_row[row, 2 * CH :]
         grad = (back * slope_1[row]).astype(BF16)
-        near = stack[pl.ds(row, 3)].reshape(9 * FIELDS, LON)
+        near = stack[pl.ds(row + 4, 3)].reshape(9 * FIELDS, LON)
         sum_in[...] += dot_cells(near, grad)
 
     loop(0, ROWS, last)
@@ -491,13 +463,6 @@
         copies=5,
     )(kernel_in.transpose(0, 2, 1), kernel_mid, kernel_out)
     saved = [
-        ((ROWS + 2, 3 * FIELDS, LON), BF16),
-        ((ROWS + 2, CH, LON), BF16),
-        ((ROWS, CH, LON), F32),
-        ((ROWS + 2, CH, LON), BF16),
-        ((ROWS + 2, CH, LON), F32),
-    ]
-    worked = [
         ((ROWS + 10, 3 * FIELDS, LON), BF16),
         ((ROWS + 8, CH, LON), BF16),
         ((ROWS, CH, LON), F32),
@@ -508,15 +473,13 @@
     send, pushed, kept, stack, hidden_1, slope_1, hidden_2, slope_2 = call(
         forward_kernel,
         [VMEM] * 3 + [HBM] + [VMEM] * 3,
-        [((SENT, LON), F32, VMEM), ((VARS, ROWS, LON), F32, VMEM), kept_shape + (HBM,)]
-        + [shape + (HBM,) for shape in saved],
-        [kept_shape] + worked
-        + [((2 * HALO, FIELDS, LON), F32), ((HALF, ROWS, LON), F32)],
-        copies=7,
+        [((SENT, LON), F32, VMEM), ((VARS, ROWS, LON), F32, VMEM), kept_shape + (VMEM,)]
+        + [shape + (VMEM,) for shape in saved],
+        [((2 * HALO, FIELDS, LON), F32), ((HALF, ROWS, LON), F32)],
+        copies=1,
         flops=10**9,
     )(far, near, own, members, w_in, w_mid, w_out)
     fields = spread(send, "member", MEMBERS)
-    fields_shape = ((MEMBERS, SENT, LON), F32)
     (swapped,) = call(
         distance_kernel,
         [VMEM] * 5,
@@ -529,11 +492,9 @@
     totals = spread(partials, "ring", RING)
     mine, theirs = call(
         backward_kernel,
-        [VMEM] * 3 + [HBM] * 9,
+        [VMEM] * 10 + [HBM] * 2,
         [((MEMBERS * CHUNK, 128), F32, VMEM)] * 2,
-        [fields_shape, kept_shape]
-        + saved
-        + [(shape, BF16) for shape in w_shapes[3:]]
+        [(shape, BF16) for shape in w_shapes[3:]]
         + [
             ((ROWS + 4, 48, LON), BF16),
             ((ROWS + 2, 3 * CH, LON), BF16),
@@ -543,7 +504,7 @@
             ((9 * FIELDS, CH), F32),
             ((6 * CH, 128), F32),
         ],
-        copies=9,
+        copies=2,
         flops=10**9,
     )(
         lat, totals, beside, fields, kept, stack, hidden_1, slope_1, hidden_2, slope_2,

time: 99.1 us -> 96.4 us (0.973)
  Pallas kernels: 13.9 us -> 11.3 us
    pallas_call x6, Pallas kernels: 13.9 us -> 11.3 us  [placed(): run(*[pltpu.with_memory_space_constraint(array, pltpu.HBM) if spec is HBM...]
where the time goes in v11:
time: 96.4 us; the launch traced here: 96 us
  blocking collectives  66.6 us (69%)
  starting transfers between devices  13.6 us (14%)
  Pallas kernels  11.3 us (12%)
  waiting for transfers between devices  2.75 us (3%)
    all_to_all x4, blocking collectives, spread(): return lax.all_to_all(copies, axes, 0, 0)  59 us
    pallas_call x6, Pallas kernels, placed(): run(*[pltpu.with_memory_space_constraint(array, pltpu.HBM) if spec is HBM...  11.3 us
    all_to_all x1, blocking collectives, per_device(): lax.all_to_all(mine.reshape(MEMBERS, CHUNK, 128), 'member', 0, 0)  7.57 us
    ppermute x1, starting transfers between devices, per_device(): far = lax.ppermute(edge_far, TILE, across + [(j, i) for i, j in across])  6.21 us
    ppermute x1, starting transfers between devices, per_device(): other = lax.ppermute(chunk, 'core', swap)  3.06 us
    ppermute x1, starting transfers between devices, per_device(): beside = lax.ppermute(swapped, 'core', swap)  2.32 us
  transfers between devices with their start and end apart: 5, of which 3 were waited for; matrix products, arithmetic and copies ran while one was open for 1% of the time, Pallas kernels for 2%

profile of v11, /device:TPU:1, one launch (start us, length us, event | category | flops | bytes accessed | tf_op | source)
XLA Modules:
  0.0 96.0 jit_solution(3668836488426233915)
XLA Ops:
  0.6 1.1 %shard_map.110 = (f32[8,16,512]{2,1,0:T(8,128)S(1)}, bf16[6,16,512]{2,1,0:T(8,128)(2,1)S(1)}, bf16[6,16,512]{2,1,0:T(8,128)(2,1)S(1)}) custom-call(f32[6,8,512]{2,1,0:T(8,128)} %bitcast.10, f32[6,8,512]{2,1,0:T(8,128)} %condition_in.1, f32[6,8,512]{2,1,0:T(8,128)} %observed.1), custom_call_target="tpu_custom_call" | custom-call | flops 1000000 | bytes 1000000 | tf_op jit(solution)/shard_map/pallas_call | solution.py:426
  1.7 6.2 %collective-permute-start = (bf16[6,16,512]{2,1,0:T(8,128)(2,1)S(1)}, bf16[6,16,512]{2,1,0:T(8,128)(2,1)S(1)}, u32[]{:S(2)}, u32[]{:S(2)}) collective-permute-start(bf16[6,16,512]{2,1,0:T(8,128)(2,1)S(1)} %get-tuple-element.29), channel_id=1, source_target_pairs={{1,2},{3,4},{5,6},{7,8},{9,10},{11,12},{13,14},{15,16},{17,18},{19... | collective-permute-start | bytes 294920 | tf_op jit(solution)/shard_map/ppermute | solution.py:451
  8.0 0.1 collective-permute-start.1
  8.1 2.0 %shard_map.111 = (bf16[64,144]{1,0:T(8,128)(2,1)S(1)}, bf16[192,192]{1,0:T(8,128)(2,1)S(1)}, bf16[48,192]{1,0:T(8,128)(2,1)S(1)}, bf16[64,144]{1,0:T(8,128)(2,1)}, bf16[192,192]{1,0:T(8,128)(2,1)}) custom-call(bf16[9,9,64]{2,1,0:T(8,128)(2,1)} %bitcast.15, bf16[9,64,64]{2,1,0:T(8,128)(2,1)} %kernel_mid_in.1, bf16[9,6,64]{2,1,0:T(8,128)(2,1)} %kernel_out_in.1), custom_call_target="tpu_custom_call" | custom-call | flops 1000000 | bytes 1000000 | tf_op jit(solution)/shard_map/pallas_call | solution.py:426
  10.1 0.7 dynamic-slice_bitcast_fusion
  10.8 0.0 collective-permute-done.1.near
  10.8 0.1 broadcast_in_dim.15.lat
  10.8 0.0 collective-permute-done.far
  10.9 3.4 %shard_map.112 = (f32[56,512]{1,0:T(8,128)S(1)}, f32[6,8,512]{2,1,0:T(8,128)}, f32[4,36,512]{2,1,0:T(8,128)S(1)}, bf16[18,48,512]{2,1,0:T(8,128)(2,1)S(1)}, bf16...) custom-call(bf16[6,16,512]{2,1,0:T(8,128)(2,1)S(1)} %collective-perm, ...), custom_call_target="tpu_custom_call" | custom-call | flops 1000000000 | bytes 1000000 | tf_op jit(solution)/shard_map/pallas_call | solution.py:426
  14.3 0.0 copy-start
  14.3 0.0 copy-start.1
  14.3 0.1 broadcast_in_dim.17
  14.4 16.8 %all_to_all.25.fields = f32[8,56,512]{2,1,0:T(8,128)S(1)} all-to-all(f32[8,56,512]{2,1,0:T(8,128)S(1)} %broadcast_in_dim.17), channel_id=1, replica_groups=mesh['member'=8,'ring'=16,'core'=2] {'member'}, dimensions={0} | all-to-all | bytes 1835008 | tf_op jit(solution)/shard_map/all_to_all | solution.py:33
  31.2 0.0 copy-done
  31.2 0.0 copy-done.1
  31.2 0.2 shard_map.113
  31.4 2.3 %collective-permute-start.2 = (f32[56,512]{1,0:T(8,128)S(1)}, f32[56,512]{1,0:T(8,128)S(1)}, u32[]{:S(2)}, u32[]{:S(2)}) collective-permute-start(f32[56,512]{1,0:T(8,128)S(1)} %shard_map.113), channel_id=1, source_target_pairs={{0,1},{1,0},{2,3},{3,2},{4,5},{5,4},{6,7},{7,6},{8,9},{9,8},{10,11... | collective-permute-start | bytes 344072 | tf_op jit(solution)/shard_map/ppermute | solution.py:490
  33.8 1.0 %collective-permute-done.2.near = f32[56,512]{1,0:T(8,128)S(1)} collective-permute-done((f32[56,512]{1,0:T(8,128)S(1)}, f32[56,512]{1,0:T(8,128)S(1)}, u32[]{:S(2)}, u32[]{:S(2)}) %collective-permute-start.2) | collective-permute-done | bytes 114720 | tf_op jit(solution)/shard_map/ppermute | solution.py:490
  34.7 20.8 %all_to_all.26.totals = f32[16,8,128]{2,1,0:T(8,128)S(1)} all-to-all(f32[16,8,128]{2,1,0:T(8,128)S(1)} %broadcast_in_dim.18), channel_id=1, replica_groups=mesh['member'=8,'ring'=16,'core'=2] {'ring'}, dimensions={0} | all-to-all | bytes 131072 | tf_op jit(solution)/shard_map/all_to_all | solution.py:33
  55.6 3.7 %shard_map.114 = (f32[192,128]{1,0:T(8,128)S(1)}, f32[192,128]{1,0:T(8,128)S(1)}) custom-call(f32[48,128]{1,0:T(8,128)S(1)} %broadcast_in_dim.15.lat, f32[16,8,128]{2,1,0:T(8,128)S(1)} %all_to_all.26.totals, f32[56,512]{1,0:T(8,128)S(1)} %collective-permute-done.2.near, f32[8,56,512]{2,1,0:T(8,128)S(1)} %all_to_all.25.fields, ...), custom_call_target="tpu_custom_call" | custom-call | flops 1000000000 | bytes 1000000 | tf_op jit(solution)/shard_map/pallas_call | solution.py:426
  59.3 1.9 %collective-permute-start.3 = (f32[192,128]{1,0:T(8,128)S(1)}, f32[192,128]{1,0:T(8,128)S(1)}, u32[]{:S(2)}, u32[]{:S(2)}) collective-permute-start(f32[192,128]{1,0:T(8,128)S(1)} %get-tuple-element.48), channel_id=1, source_target_pairs={{0,1},{1,0},{2,3},{3,2},{4,5},{5,4},{6,7},{7,6},{8,9},{9,8},{10,11... | collective-permute-start | bytes 294920 | tf_op jit(solution)/shard_map/ppermute | solution.py:513
  61.2 0.9 collective-permute-done.3
  62.2 7.6 %all_to_all.27 = f32[8,24,128]{2,1,0:T(8,128)S(1)} all-to-all(f32[8,24,128]{2,1,0:T(8,128)S(1)} %bitcast.13), channel_id=1, replica_groups=mesh['member'=8,'ring'=16,'core'=2] {'member'}, dimensions={0} | all-to-all | bytes 196608 | tf_op jit(solution)/shard_map/all_to_all | solution.py:514
  69.8 13.2 %all_to_all.28 = f32[16,24,128]{2,1,0:T(8,128)S(1)} all-to-all(f32[16,24,128]{2,1,0:T(8,128)S(1)} %broadcast_in_dim.19), channel_id=1, replica_groups=mesh['member'=8,'ring'=16,'core'=2] {'ring'}, dimensions={0} | all-to-all | bytes 393216 | tf_op jit(solution)/shard_map/all_to_all | solution.py:33
  83.0 3.1 %collective-permute-start.4 = (f32[24,128]{1,0:T(8,128)S(1)}, f32[24,128]{1,0:T(8,128)S(1)}, u32[]{:S(2)}, u32[]{:S(2)}) collective-permute-start(f32[24,128]{1,0:T(8,128)S(1)} %reduce_sum.19), channel_id=1, source_target_pairs={{0,1},{1,0},{2,3},{3,2},{4,5},{5,4},{6,7},{7,6},{8,9},{9,8},{10,11... | collective-permute-start | bytes 36872 | tf_op jit(solution)/shard_map/ppermute | solution.py:516
  86.1 0.8 collective-permute-done.4
  86.9 8.2 %all_to_all.29.chunks = f32[8,2,24,128]{3,2,1,0:T(8,128)S(1)} all-to-all(f32[8,2,24,128]{3,2,1,0:T(8,128)S(1)} %broadcast_in_dim.40), channel_id=1, replica_groups=mesh['member'=8,'ring'=16,'core'=2] {'member'}, dimensions={0} | all-to-all | bytes 393216 | tf_op jit(solution)/shard_map/all_to_all | solution.py:33
  95.1 0.9 shard_map.115
  (8 shorter events, 0.1 us)
Async XLA Ops:
  1.7 9.1 %collective-permute-start = (bf16[6,16,512]{2,1,0:T(8,128)(2,1)S(1)}, bf16[6,16,512]{2,1,0:T(8,128)(2,1)S(1)}, u32[]{:S(2)}, u32[]{:S(2)}) collective-permute-start(bf16[6,16,512]{2,1,0:T(8,128)(2,1)S(1)} %get-tuple-element.29), channel_id=1, source_target_pairs={{1,2},{3,4},{5,6},{7,8},{9,10},{11,12},{13,14},{15,16},{17,18},{19... | collective-permute-start | bytes 294920 | tf_op jit(solution)/shard_map/ppermute | solution.py:451
  8.0 2.8 %collective-permute-start.1 = (bf16[6,16,512]{2,1,0:T(8,128)(2,1)S(1)}, bf16[6,16,512]{2,1,0:T(8,128)(2,1)S(1)}, u32[]{:S(2)}, u32[]{:S(2)}) collective-permute-start(bf16[6,16,512]{2,1,0:T(8,128)(2,1)S(1)} %get-tuple-element.30), channel_id=1, source_target_pairs={{0,1},{1,0},{2,3},{3,2},{4,5},{5,4},{6,7},{7,6},{8,9},{9,8},{10,11... | collective-permute-start | bytes 294920 | tf_op jit(solution)/shard_map/ppermute | solution.py:452
  14.3 16.9 %copy-start = (f32[1,6,8,512]{3,2,1,0:T(8,128)S(1)}, f32[1,6,8,512]{3,2,1,0:T(8,128)}, u32[]{:S(2)}) copy-start(f32[1,6,8,512]{3,2,1,0:T(8,128)} %param.7) | copy-start | bytes 294916
  14.3 16.9 %copy-start.1 = (f32[6,8,512]{2,1,0:T(8,128)S(1)}, f32[6,8,512]{2,1,0:T(8,128)}, u32[]{:S(2)}) copy-start(f32[6,8,512]{2,1,0:T(8,128)} %observed.1) | copy-start | bytes 294916
  31.4 3.3 %collective-permute-start.2 = (f32[56,512]{1,0:T(8,128)S(1)}, f32[56,512]{1,0:T(8,128)S(1)}, u32[]{:S(2)}, u32[]{:S(2)}) collective-permute-start(f32[56,512]{1,0:T(8,128)S(1)} %shard_map.113), channel_id=1, source_target_pairs={{0,1},{1,0},{2,3},{3,2},{4,5},{5,4},{6,7},{7,6},{8,9},{9,8},{10,11... | collective-permute-start | bytes 344072 | tf_op jit(solution)/shard_map/ppermute | solution.py:490
  59.3 2.8 %collective-permute-start.3 = (f32[192,128]{1,0:T(8,128)S(1)}, f32[192,128]{1,0:T(8,128)S(1)}, u32[]{:S(2)}, u32[]{:S(2)}) collective-permute-start(f32[192,128]{1,0:T(8,128)S(1)} %get-tuple-element.48), channel_id=1, source_target_pairs={{0,1},{1,0},{2,3},{3,2},{4,5},{5,4},{6,7},{7,6},{8,9},{9,8},{10,11... | collective-permute-start | bytes 294920 | tf_op jit(solution)/shard_map/ppermute | solution.py:513
  83.0 3.9 %collective-permute-start.4 = (f32[24,128]{1,0:T(8,128)S(1)}, f32[24,128]{1,0:T(8,128)S(1)}, u32[]{:S(2)}, u32[]{:S(2)}) collective-permute-start(f32[24,128]{1,0:T(8,128)S(1)} %reduce_sum.19), channel_id=1, source_target_pairs={{0,1},{1,0},{2,3},{3,2},{4,5},{5,4},{6,7},{7,6},{8,9},{9,8},{10,11... | collective-permute-start | bytes 36872 | tf_op jit(solution)/shard_map/ppermute | solution.py:516

commit v12 on v11

--- a/solution.py
+++ b/solution.py
@@ -113,15 +113,10 @@
 
 def weights_kernel(
     kernel_in_in, kernel_mid_in, kernel_out_in, w_in, w_mid, w_out, w_back_2, w_back_1,
-    kernel_in, kernel_mid, kernel_out, flat_in, square, flat_out, back_2, back_1, held_2, held_1, sems,
+    kernel_in, kernel_mid, kernel_out, flat_in, square, flat_out, back_2, back_1, sems,
 ):
     pairs = [(kernel_in_in, kernel_in), (kernel_mid_in, kernel_mid), (kernel_out_in, kernel_out)]
-    copies = [
-        pltpu.make_async_copy(source, target, sems.at[2 + at])
-        for at, (source, target) in enumerate(pairs)
-    ]
-    for copy in copies:
-        copy.start()
+    copies = started(pairs, sems)
     flat_out[...] = jnp.zeros_like(flat_out)
     back_2[...] = jnp.zeros_like(back_2)
     for copy in copies:
@@ -142,19 +137,11 @@
         out = jnp.concatenate([out, jnp.zeros((8 - VARS, CH), F32)], 0).T
         back_2[:, back * 16 : back * 16 + HALF] = out[:, :HALF]
         back_2[:, back * 16 + 8 : back * 16 + 8 + HALF] = out[:, HALF:VARS]
-    held_2[...] = back_2[...].astype(BF16)
-    held_1[...] = back_1[...].astype(BF16)
-    copies = [
-        pltpu.make_async_copy(held_2, w_back_2, sems.at[0]),
-        pltpu.make_async_copy(held_1, w_back_1, sems.at[1]),
-    ]
-    for copy in copies:
-        copy.start()
+    w_back_2[...] = back_2[...].astype(BF16)
+    w_back_1[...] = back_1[...].astype(BF16)
     w_in[...] = flat_in[...].astype(BF16)
     w_mid[...] = square[...].astype(BF16)
     w_out[...] = flat_out[...].astype(BF16)
-    for copy in copies:
-        copy.wait()
 
 
 def forward_kernel(
@@ -275,12 +262,10 @@
 
 
 def backward_kernel(
-    lat, totals, near, fields, kept, stack, hidden_1, slope_1, hidden_2, slope_2, w_back_2_in, w_back_1_in,
+    lat, totals, near, fields, kept, stack, hidden_1, slope_1, hidden_2, slope_2, w_back_2, w_back_1,
     mine, theirs,
-    w_back_2, w_back_1,
-    coupled, turned_2, by_row, sum_out, sum_mid, sum_in, packed, sems,
+    coupled, turned_2, by_row, sum_out, sum_mid, sum_in, packed,
 ):
-    copies = started([(w_back_2_in, w_back_2), (w_back_1_in, w_back_1)], sems)
     me, base, core = lax.axis_index("member"), first_row(), lax.axis_index("core")
     sum_out[...] = jnp.zeros_like(sum_out)
     sum_mid[...] = jnp.zeros_like(sum_mid)
@@ -319,7 +304,6 @@
         for shift in range(3):
             part = turned(field, shift - 1).astype(BF16)
             coupled[row, shift * 16 : (shift + 1) * 16, :] = part
-    copies[0].wait()
 
     def second(row):
         back = dot(w_back_2[...], coupled[pl.ds(row, 3)].reshape(144, LON))
@@ -329,7 +313,6 @@
             turned_2[row, shift * CH : (shift + 1) * CH, :] = part
 
     loop(0, ROWS + 2, second)
-    copies[1].wait()
 
     def across_rows(row):
         by_row[row] = dot(w_back_1[...], turned_2[row])
@@ -455,12 +438,10 @@
     w_in, w_mid, w_out, w_back_2, w_back_1 = call(
         weights_kernel,
         [HBM] * 3,
-        [(shape, BF16, VMEM) for shape in w_shapes[:3]]
-        + [(shape, BF16, HBM) for shape in w_shapes[3:]],
+        [(shape, BF16, VMEM) for shape in w_shapes],
         [((9, INPUTS, CH), BF16), ((9, CH, CH), BF16), ((9, VARS, CH), BF16)]
-        + [(shape, F32) for shape in w_shapes]
-        + [(shape, BF16) for shape in w_shapes[3:]],
-        copies=5,
+        + [(shape, F32) for shape in w_shapes],
+        copies=3,
     )(kernel_in.transpose(0, 2, 1), kernel_mid, kernel_out)
     saved = [
         ((ROWS + 10, 3 * FIELDS, LON), BF16),
@@ -492,10 +473,9 @@
     totals = spread(partials, "ring", RING)
     mine, theirs = call(
         backward_kernel,
-        [VMEM] * 10 + [HBM] * 2,
+        [VMEM] * 12,
         [((MEMBERS * CHUNK, 128), F32, VMEM)] * 2,
-        [(shape, BF16) for shape in w_shapes[3:]]
-        + [
+        [
             ((ROWS + 4, 48, LON), BF16),
             ((ROWS + 2, 3 * CH, LON), BF16),
             ((ROWS + 2, 3 * CH, LON), F32),
@@ -504,7 +484,6 @@
             ((9 * FIELDS, CH), F32),
             ((6 * CH, 128), F32),
         ],
-        copies=2,
         flops=10**9,
     )(
         lat, totals, beside, fields, kept, stack, hidden_1, slope_1, hidden_2, slope_2,

time: 96.4 us -> 95.4 us (0.990)
  Pallas kernels: 11.3 us -> 9.84 us
  blocking collectives: 66.6 us -> 68 us
    pallas_call x6, Pallas kernels: 11.3 us -> 9.84 us  [placed(): run(*[pltpu.with_memory_space_constraint(array, pltpu.HBM) if spec is HBM...]
    all_to_all x4, blocking collectives: 59 us -> 60.4 us  [spread(): return lax.all_to_all(copies, axes, 0, 0)]
where the time goes in v12:
time: 95.4 us; the launch traced here: 95 us
  blocking collectives  68 us (71%)
  starting transfers between devices  12.8 us (13%)
  Pallas kernels  9.84 us (10%)
  waiting for transfers between devices  2.75 us (3%)
    all_to_all x4, blocking collectives, spread(): return lax.all_to_all(copies, axes, 0, 0)  60.4 us
    pallas_call x6, Pallas kernels, placed(): run(*[pltpu.with_memory_space_constraint(array, pltpu.HBM) if spec is HBM...  9.84 us
    all_to_all x1, blocking collectives, per_device(): lax.all_to_all(mine.reshape(MEMBERS, CHUNK, 128), 'member', 0, 0)  7.58 us
    ppermute x1, starting transfers between devices, per_device(): far = lax.ppermute(edge_far, TILE, across + [(j, i) for i, j in across])  6.21 us
    ppermute x1, starting transfers between devices, per_device(): other = lax.ppermute(chunk, 'core', swap)  3.06 us
  transfers between devices with their start and end apart: 5, of which 3 were waited for; matrix products, arithmetic and copies ran while one was open for 1% of the time, Pallas kernels for 2%

profile of v12, /device:TPU:1, one launch (start us, length us, event | category | flops | bytes accessed | tf_op | source)
XLA Modules:
  0.0 95.0 jit_solution(5362527631030277466)
XLA Ops:
  0.6 1.1 %shard_map.110 = (f32[8,16,512]{2,1,0:T(8,128)S(1)}, bf16[6,16,512]{2,1,0:T(8,128)(2,1)S(1)}, bf16[6,16,512]{2,1,0:T(8,128)(2,1)S(1)}) custom-call(f32[6,8,512]{2,1,0:T(8,128)} %bitcast.10, f32[6,8,512]{2,1,0:T(8,128)} %condition_in.1, f32[6,8,512]{2,1,0:T(8,128)} %observed.1), custom_call_target="tpu_custom_call" | custom-call | flops 1000000 | bytes 1000000 | tf_op jit(solution)/shard_map/pallas_call | solution.py:409
  1.7 6.2 %collective-permute-start = (bf16[6,16,512]{2,1,0:T(8,128)(2,1)S(1)}, bf16[6,16,512]{2,1,0:T(8,128)(2,1)S(1)}, u32[]{:S(2)}, u32[]{:S(2)}) collective-permute-start(bf16[6,16,512]{2,1,0:T(8,128)(2,1)S(1)} %get-tuple-element.29), channel_id=1, source_target_pairs={{1,2},{3,4},{5,6},{7,8},{9,10},{11,12},{13,14},{15,16},{17,18},{19... | collective-permute-start | bytes 294920 | tf_op jit(solution)/shard_map/ppermute | solution.py:434
  8.0 0.1 collective-permute-start.1
  8.1 1.4 %shard_map.111 = (bf16[64,144]{1,0:T(8,128)(2,1)S(1)}, bf16[192,192]{1,0:T(8,128)(2,1)S(1)}, bf16[48,192]{1,0:T(8,128)(2,1)S(1)}, bf16[64,144]{1,0:T(8,128)(2,1)S(1)}, bf16[192,192]{1,0:T(8,128)(2,1)S(1)}) custom-call(bf16[9,9,64]{2,1,0:T(8,128)(2,1)} %bitcast.15, bf16[9,64,64]{2,1,0:T(8,128)(2,1)} %kernel_mid_in.1, bf16[9,6,64]{2,1,0:T(8,128)(2,1)} %kernel_out_in.1), custom_call_target="tpu_custom_call" | custom-call | flops 1000000 | bytes 1000000 | tf_op jit(solution)/shard_map/pallas_call | solution.py:409
  9.5 0.7 dynamic-slice_bitcast_fusion
  10.2 0.0 collective-permute-done.1.near
  10.2 0.1 broadcast_in_dim.15.lat
  10.3 0.0 collective-permute-done.far
  10.3 3.4 %shard_map.112 = (f32[56,512]{1,0:T(8,128)S(1)}, f32[6,8,512]{2,1,0:T(8,128)}, f32[4,36,512]{2,1,0:T(8,128)S(1)}, bf16[18,48,512]{2,1,0:T(8,128)(2,1)S(1)}, bf16...) custom-call(bf16[6,16,512]{2,1,0:T(8,128)(2,1)S(1)} %collective-perm, ...), custom_call_target="tpu_custom_call" | custom-call | flops 1000000000 | bytes 1000000 | tf_op jit(solution)/shard_map/pallas_call | solution.py:409
  13.7 0.0 copy-start
  13.7 0.0 copy-start.1
  13.7 0.1 broadcast_in_dim.17
  13.8 18.2 %all_to_all.25.fields = f32[8,56,512]{2,1,0:T(8,128)S(1)} all-to-all(f32[8,56,512]{2,1,0:T(8,128)S(1)} %broadcast_in_dim.17), channel_id=1, replica_groups=mesh['member'=8,'ring'=16,'core'=2] {'member'}, dimensions={0} | all-to-all | bytes 1835008 | tf_op jit(solution)/shard_map/all_to_all | solution.py:33
  32.0 0.0 copy-done
  32.0 0.0 copy-done.1
  32.0 0.2 shard_map.113
  32.2 1.6 %collective-permute-start.2 = (f32[56,512]{1,0:T(8,128)S(1)}, f32[56,512]{1,0:T(8,128)S(1)}, u32[]{:S(2)}, u32[]{:S(2)}) collective-permute-start(f32[56,512]{1,0:T(8,128)S(1)} %shard_map.113), channel_id=1, source_target_pairs={{0,1},{1,0},{2,3},{3,2},{4,5},{5,4},{6,7},{7,6},{8,9},{9,8},{10,11... | collective-permute-start | bytes 344072 | tf_op jit(solution)/shard_map/ppermute | solution.py:471
  33.8 1.0 %collective-permute-done.2.near = f32[56,512]{1,0:T(8,128)S(1)} collective-permute-done((f32[56,512]{1,0:T(8,128)S(1)}, f32[56,512]{1,0:T(8,128)S(1)}, u32[]{:S(2)}, u32[]{:S(2)}) %collective-permute-start.2) | collective-permute-done | bytes 114720 | tf_op jit(solution)/shard_map/ppermute | solution.py:471
  34.7 20.8 %all_to_all.26.totals = f32[16,8,128]{2,1,0:T(8,128)S(1)} all-to-all(f32[16,8,128]{2,1,0:T(8,128)S(1)} %broadcast_in_dim.18), channel_id=1, replica_groups=mesh['member'=8,'ring'=16,'core'=2] {'ring'}, dimensions={0} | all-to-all | bytes 131072 | tf_op jit(solution)/shard_map/all_to_all | solution.py:33
  55.6 2.8 %shard_map.114 = (f32[192,128]{1,0:T(8,128)S(1)}, f32[192,128]{1,0:T(8,128)S(1)}) custom-call(f32[48,128]{1,0:T(8,128)S(1)} %broadcast_in_dim.15.lat, f32[16,8,128]{2,1,0:T(8,128)S(1)} %all_to_all.26.totals, f32[56,512]{1,0:T(8,128)S(1)} %collective-permute-done.2.near, f32[8,56,512]{2,1,0:T(8,128)S(1)} %all_to_all.25.fields, ...), custom_call_target="tpu_custom_call" | custom-call | flops 1000000000 | bytes 1000000 | tf_op jit(solution)/shard_map/pallas_call | solution.py:409
  58.4 1.8 %collective-permute-start.3 = (f32[192,128]{1,0:T(8,128)S(1)}, f32[192,128]{1,0:T(8,128)S(1)}, u32[]{:S(2)}, u32[]{:S(2)}) collective-permute-start(f32[192,128]{1,0:T(8,128)S(1)} %get-tuple-element.48), channel_id=1, source_target_pairs={{0,1},{1,0},{2,3},{3,2},{4,5},{5,4},{6,7},{7,6},{8,9},{9,8},{10,11... | collective-permute-start | bytes 294920 | tf_op jit(solution)/shard_map/ppermute | solution.py:492
  60.2 0.9 collective-permute-done.3
  61.2 7.6 %all_to_all.27 = f32[8,24,128]{2,1,0:T(8,128)S(1)} all-to-all(f32[8,24,128]{2,1,0:T(8,128)S(1)} %bitcast.13), channel_id=1, replica_groups=mesh['member'=8,'ring'=16,'core'=2] {'member'}, dimensions={0} | all-to-all | bytes 196608 | tf_op jit(solution)/shard_map/all_to_all | solution.py:493
  68.8 13.2 %all_to_all.28 = f32[16,24,128]{2,1,0:T(8,128)S(1)} all-to-all(f32[16,24,128]{2,1,0:T(8,128)S(1)} %broadcast_in_dim.19), channel_id=1, replica_groups=mesh['member'=8,'ring'=16,'core'=2] {'ring'}, dimensions={0} | all-to-all | bytes 393216 | tf_op jit(solution)/shard_map/all_to_all | solution.py:33
  82.1 3.1 %collective-permute-start.4 = (f32[24,128]{1,0:T(8,128)S(1)}, f32[24,128]{1,0:T(8,128)S(1)}, u32[]{:S(2)}, u32[]{:S(2)}) collective-permute-start(f32[24,128]{1,0:T(8,128)S(1)} %reduce_sum.19), channel_id=1, source_target_pairs={{0,1},{1,0},{2,3},{3,2},{4,5},{5,4},{6,7},{7,6},{8,9},{9,8},{10,11... | collective-permute-start | bytes 36872 | tf_op jit(solution)/shard_map/ppermute | solution.py:495
  85.1 0.8 collective-permute-done.4
  86.0 8.2 %all_to_all.29.chunks = f32[8,2,24,128]{3,2,1,0:T(8,128)S(1)} all-to-all(f32[8,2,24,128]{3,2,1,0:T(8,128)S(1)} %broadcast_in_dim.40), channel_id=1, replica_groups=mesh['member'=8,'ring'=16,'core'=2] {'member'}, dimensions={0} | all-to-all | bytes 393216 | tf_op jit(solution)/shard_map/all_to_all | solution.py:33
  94.2 0.9 shard_map.115
  (8 shorter events, 0.1 us)
Async XLA Ops:
  1.7 8.5 %collective-permute-start = (bf16[6,16,512]{2,1,0:T(8,128)(2,1)S(1)}, bf16[6,16,512]{2,1,0:T(8,128)(2,1)S(1)}, u32[]{:S(2)}, u32[]{:S(2)}) collective-permute-start(bf16[6,16,512]{2,1,0:T(8,128)(2,1)S(1)} %get-tuple-element.29), channel_id=1, source_target_pairs={{1,2},{3,4},{5,6},{7,8},{9,10},{11,12},{13,14},{15,16},{17,18},{19... | collective-permute-start | bytes 294920 | tf_op jit(solution)/shard_map/ppermute | solution.py:434
  8.0 2.2 %collective-permute-start.1 = (bf16[6,16,512]{2,1,0:T(8,128)(2,1)S(1)}, bf16[6,16,512]{2,1,0:T(8,128)(2,1)S(1)}, u32[]{:S(2)}, u32[]{:S(2)}) collective-permute-start(bf16[6,16,512]{2,1,0:T(8,128)(2,1)S(1)} %get-tuple-element.30), channel_id=1, source_target_pairs={{0,1},{1,0},{2,3},{3,2},{4,5},{5,4},{6,7},{7,6},{8,9},{9,8},{10,11... | collective-permute-start | bytes 294920 | tf_op jit(solution)/shard_map/ppermute | solution.py:435
  13.7 18.3 %copy-start = (f32[1,6,8,512]{3,2,1,0:T(8,128)S(1)}, f32[1,6,8,512]{3,2,1,0:T(8,128)}, u32[]{:S(2)}) copy-start(f32[1,6,8,512]{3,2,1,0:T(8,128)} %param.7) | copy-start | bytes 294916
  13.7 18.3 %copy-start.1 = (f32[6,8,512]{2,1,0:T(8,128)S(1)}, f32[6,8,512]{2,1,0:T(8,128)}, u32[]{:S(2)}) copy-start(f32[6,8,512]{2,1,0:T(8,128)} %observed.1) | copy-start | bytes 294916
  32.2 2.5 %collective-permute-start.2 = (f32[56,512]{1,0:T(8,128)S(1)}, f32[56,512]{1,0:T(8,128)S(1)}, u32[]{:S(2)}, u32[]{:S(2)}) collective-permute-start(f32[56,512]{1,0:T(8,128)S(1)} %shard_map.113), channel_id=1, source_target_pairs={{0,1},{1,0},{2,3},{3,2},{4,5},{5,4},{6,7},{7,6},{8,9},{9,8},{10,11... | collective-permute-start | bytes 344072 | tf_op jit(solution)/shard_map/ppermute | solution.py:471
  58.4 2.8 %collective-permute-start.3 = (f32[192,128]{1,0:T(8,128)S(1)}, f32[192,128]{1,0:T(8,128)S(1)}, u32[]{:S(2)}, u32[]{:S(2)}) collective-permute-start(f32[192,128]{1,0:T(8,128)S(1)} %get-tuple-element.48), channel_id=1, source_target_pairs={{0,1},{1,0},{2,3},{3,2},{4,5},{5,4},{6,7},{7,6},{8,9},{9,8},{10,11... | collective-permute-start | bytes 294920 | tf_op jit(solution)/shard_map/ppermute | solution.py:492
  82.1 3.9 %collective-permute-start.4 = (f32[24,128]{1,0:T(8,128)S(1)}, f32[24,128]{1,0:T(8,128)S(1)}, u32[]{:S(2)}, u32[]{:S(2)}) collective-permute-start(f32[24,128]{1,0:T(8,128)S(1)} %reduce_sum.19), channel_id=1, source_target_pairs={{0,1},{1,0},{2,3},{3,2},{4,5},{5,4},{6,7},{7,6},{8,9},{9,8},{10,11... | collective-permute-start | bytes 36872 | tf_op jit(solution)/shard_map/ppermute | solution.py:495

commit v13 on v12

--- a/solution.py
+++ b/solution.py
@@ -365,13 +365,10 @@
 
 
 def unpack_kernel(chunks, grad_in, grad_mid, grad_out, energy, packed):
-    core = lax.axis_index("core")
     for member in range(MEMBERS):
-        first, second = chunks[member, 0], chunks[member, 1]
-        at = member * CHUNK
-        packed[at : at + CHUNK, :] = jnp.where(core == 0, first, second)
-        at += MEMBERS * CHUNK
-        packed[at : at + CHUNK, :] = jnp.where(core == 0, second, first)
+        for half in range(2):
+            at = (half * MEMBERS + member) * CHUNK
+            packed[at : at + CHUNK, :] = chunks[member * 2 + half]
     for tap in range(9):
         at, side = place_mid(tap)
         grad_mid[tap] = packed[at : at + CH, side]
@@ -492,8 +489,7 @@
     mine = mine + lax.ppermute(theirs, "core", swap)
     chunk = jnp.sum(lax.all_to_all(mine.reshape(MEMBERS, CHUNK, 128), "member", 0, 0), 0)
     chunk = jnp.sum(spread(chunk, "ring", RING), 0)
-    other = lax.ppermute(chunk, "core", swap)
-    chunks = spread(jnp.stack([chunk, other]), "member", MEMBERS)
+    chunks = spread(chunk, ("member", "core"), 2 * MEMBERS)
     grad_in, grad_mid, grad_out, energy = call(
         unpack_kernel,
         [VMEM],

time: 95.4 us -> 95.7 us (level)
  blocking collectives: 68 us -> 72.2 us
  starting transfers between devices: 12.8 us -> 9.7 us
    all_to_all x4, blocking collectives: 60.4 us -> 64.6 us  [spread(): return lax.all_to_all(copies, axes, 0, 0)]
    ppermute x1 -> x0, starting transfers between devices: 3.06 us -> none  [per_device(): other = lax.ppermute(chunk, 'core', swap)]
  transfers between devices with their start and end apart: 5 -> 4, of which waited for: 3 -> 2; matrix products, arithmetic and copies ran while one was open for 1% -> 1% of each run, Pallas kernels for 2% -> 2%
where the time goes in v13:
time: 95.7 us; the launch traced here: 95.3 us
  blocking collectives  72.2 us (75%)
  Pallas kernels  9.83 us (10%)
  starting transfers between devices  9.7 us (10%)
  waiting for transfers between devices  1.91 us (2%)
    all_to_all x4, blocking collectives, spread(): return lax.all_to_all(copies, axes, 0, 0)  64.6 us
    pallas_call x6, Pallas kernels, placed(): run(*[pltpu.with_memory_space_constraint(array, pltpu.HBM) if spec is HBM...  9.83 us
    all_to_all x1, blocking collectives, per_device(): lax.all_to_all(mine.reshape(MEMBERS, CHUNK, 128), 'member', 0, 0)  7.58 us
    ppermute x1, starting transfers between devices, per_device(): far = lax.ppermute(edge_far, TILE, across + [(j, i) for i, j in across])  6.21 us
  transfers between devices with their start and end apart: 4, of which 2 were waited for; matrix products, arithmetic and copies ran while one was open for 1% of the time, Pallas kernels for 2%

profile of v13, /device:TPU:1, one launch (start us, length us, event | category | flops | bytes accessed | tf_op | source)
XLA Modules:
  0.0 95.3 jit_solution(6581601498525389892)
XLA Ops:
  0.6 1.1 %shard_map.110 = (f32[8,16,512]{2,1,0:T(8,128)S(1)}, bf16[6,16,512]{2,1,0:T(8,128)(2,1)S(1)}, bf16[6,16,512]{2,1,0:T(8,128)(2,1)S(1)}) custom-call(f32[6,8,512]{2,1,0:T(8,128)} %bitcast.8, f32[6,8,512]{2,1,0:T(8,128)} %condition_in.1, f32[6,8,512]{2,1,0:T(8,128)} %observed.1), custom_call_target="tpu_custom_call" | custom-call | flops 1000000 | bytes 1000000 | tf_op jit(solution)/shard_map/pallas_call | solution.py:406
  1.7 6.2 %collective-permute-start = (bf16[6,16,512]{2,1,0:T(8,128)(2,1)S(1)}, bf16[6,16,512]{2,1,0:T(8,128)(2,1)S(1)}, u32[]{:S(2)}, u32[]{:S(2)}) collective-permute-start(bf16[6,16,512]{2,1,0:T(8,128)(2,1)S(1)} %get-tuple-element.29), channel_id=1, source_target_pairs={{1,2},{3,4},{5,6},{7,8},{9,10},{11,12},{13,14},{15,16},{17,18},{19... | collective-permute-start | bytes 294920 | tf_op jit(solution)/shard_map/ppermute | solution.py:431
  8.0 0.1 collective-permute-start.1
  8.1 1.4 %shard_map.111 = (bf16[64,144]{1,0:T(8,128)(2,1)S(1)}, bf16[192,192]{1,0:T(8,128)(2,1)S(1)}, bf16[48,192]{1,0:T(8,128)(2,1)S(1)}, bf16[64,144]{1,0:T(8,128)(2,1)S(1)}, bf16[192,192]{1,0:T(8,128)(2,1)S(1)}) custom-call(bf16[9,9,64]{2,1,0:T(8,128)(2,1)} %bitcast.12, bf16[9,64,64]{2,1,0:T(8,128)(2,1)} %kernel_mid_in.1, bf16[9,6,64]{2,1,0:T(8,128)(2,1)} %kernel_out_in.1), custom_call_target="tpu_custom_call" | custom-call | flops 1000000 | bytes 1000000 | tf_op jit(solution)/shard_map/pallas_call | solution.py:406
  9.5 0.7 dynamic-slice_bitcast_fusion
  10.2 0.0 collective-permute-done.1.near
  10.2 0.1 broadcast_in_dim.15.lat
  10.3 0.0 collective-permute-done.far
  10.3 3.4 %shard_map.112 = (f32[56,512]{1,0:T(8,128)S(1)}, f32[6,8,512]{2,1,0:T(8,128)}, f32[4,36,512]{2,1,0:T(8,128)S(1)}, bf16[18,48,512]{2,1,0:T(8,128)(2,1)S(1)}, bf16...) custom-call(bf16[6,16,512]{2,1,0:T(8,128)(2,1)S(1)} %collective-perm, ...), custom_call_target="tpu_custom_call" | custom-call | flops 1000000000 | bytes 1000000 | tf_op jit(solution)/shard_map/pallas_call | solution.py:406
  13.7 0.0 copy-start
  13.7 0.0 copy-start.1
  13.7 0.1 broadcast_in_dim.17
  13.8 18.2 %all_to_all.25.fields = f32[8,56,512]{2,1,0:T(8,128)S(1)} all-to-all(f32[8,56,512]{2,1,0:T(8,128)S(1)} %broadcast_in_dim.17), channel_id=1, replica_groups=mesh['member'=8,'ring'=16,'core'=2] {'member'}, dimensions={0} | all-to-all | bytes 1835008 | tf_op jit(solution)/shard_map/all_to_all | solution.py:33
  32.0 0.0 copy-done
  32.0 0.0 copy-done.1
  32.0 0.2 shard_map.113
  32.2 1.6 %collective-permute-start.2 = (f32[56,512]{1,0:T(8,128)S(1)}, f32[56,512]{1,0:T(8,128)S(1)}, u32[]{:S(2)}, u32[]{:S(2)}) collective-permute-start(f32[56,512]{1,0:T(8,128)S(1)} %shard_map.113), channel_id=1, source_target_pairs={{0,1},{1,0},{2,3},{3,2},{4,5},{5,4},{6,7},{7,6},{8,9},{9,8},{10,11... | collective-permute-start | bytes 344072 | tf_op jit(solution)/shard_map/ppermute | solution.py:468
  33.8 1.0 %collective-permute-done.2.near = f32[56,512]{1,0:T(8,128)S(1)} collective-permute-done((f32[56,512]{1,0:T(8,128)S(1)}, f32[56,512]{1,0:T(8,128)S(1)}, u32[]{:S(2)}, u32[]{:S(2)}) %collective-permute-start.2) | collective-permute-done | bytes 114720 | tf_op jit(solution)/shard_map/ppermute | solution.py:468
  34.7 20.8 %all_to_all.26.totals = f32[16,8,128]{2,1,0:T(8,128)S(1)} all-to-all(f32[16,8,128]{2,1,0:T(8,128)S(1)} %broadcast_in_dim.18), channel_id=1, replica_groups=mesh['member'=8,'ring'=16,'core'=2] {'ring'}, dimensions={0} | all-to-all | bytes 131072 | tf_op jit(solution)/shard_map/all_to_all | solution.py:33
  55.6 2.8 %shard_map.114 = (f32[192,128]{1,0:T(8,128)S(1)}, f32[192,128]{1,0:T(8,128)S(1)}) custom-call(f32[48,128]{1,0:T(8,128)S(1)} %broadcast_in_dim.15.lat, f32[16,8,128]{2,1,0:T(8,128)S(1)} %all_to_all.26.totals, f32[56,512]{1,0:T(8,128)S(1)} %collective-permute-done.2.near, f32[8,56,512]{2,1,0:T(8,128)S(1)} %all_to_all.25.fields, ...), custom_call_target="tpu_custom_call" | custom-call | flops 1000000000 | bytes 1000000 | tf_op jit(solution)/shard_map/pallas_call | solution.py:406
  58.4 1.8 %collective-permute-start.3 = (f32[192,128]{1,0:T(8,128)S(1)}, f32[192,128]{1,0:T(8,128)S(1)}, u32[]{:S(2)}, u32[]{:S(2)}) collective-permute-start(f32[192,128]{1,0:T(8,128)S(1)} %get-tuple-element.48), channel_id=1, source_target_pairs={{0,1},{1,0},{2,3},{3,2},{4,5},{5,4},{6,7},{7,6},{8,9},{9,8},{10,11... | collective-permute-start | bytes 294920 | tf_op jit(solution)/shard_map/ppermute | solution.py:489
  60.2 0.9 collective-permute-done.3
  61.2 7.6 %all_to_all.27 = f32[8,24,128]{2,1,0:T(8,128)S(1)} all-to-all(f32[8,24,128]{2,1,0:T(8,128)S(1)} %bitcast.11), channel_id=1, replica_groups=mesh['member'=8,'ring'=16,'core'=2] {'member'}, dimensions={0} | all-to-all | bytes 196608 | tf_op jit(solution)/shard_map/all_to_all | solution.py:490
  68.8 13.2 %all_to_all.28 = f32[16,24,128]{2,1,0:T(8,128)S(1)} all-to-all(f32[16,24,128]{2,1,0:T(8,128)S(1)} %broadcast_in_dim.19), channel_id=1, replica_groups=mesh['member'=8,'ring'=16,'core'=2] {'ring'}, dimensions={0} | all-to-all | bytes 393216 | tf_op jit(solution)/shard_map/all_to_all | solution.py:33
  82.1 12.4 %all_to_all.29.chunks = f32[16,24,128]{2,1,0:T(8,128)S(1)} all-to-all(f32[16,24,128]{2,1,0:T(8,128)S(1)} %broadcast_in_dim.40), channel_id=1, replica_groups=mesh['member'=8,'ring'=16,'core'=2] {'member','core'}, dimensions={0} | all-to-all | bytes 393216 | tf_op jit(solution)/shard_map/all_to_all | solution.py:33
  94.5 0.9 shard_map.115
  (7 shorter events, 0.1 us)
Async XLA Ops:
  1.7 8.5 %collective-permute-start = (bf16[6,16,512]{2,1,0:T(8,128)(2,1)S(1)}, bf16[6,16,512]{2,1,0:T(8,128)(2,1)S(1)}, u32[]{:S(2)}, u32[]{:S(2)}) collective-permute-start(bf16[6,16,512]{2,1,0:T(8,128)(2,1)S(1)} %get-tuple-element.29), channel_id=1, source_target_pairs={{1,2},{3,4},{5,6},{7,8},{9,10},{11,12},{13,14},{15,16},{17,18},{19... | collective-permute-start | bytes 294920 | tf_op jit(solution)/shard_map/ppermute | solution.py:431
  8.0 2.2 %collective-permute-start.1 = (bf16[6,16,512]{2,1,0:T(8,128)(2,1)S(1)}, bf16[6,16,512]{2,1,0:T(8,128)(2,1)S(1)}, u32[]{:S(2)}, u32[]{:S(2)}) collective-permute-start(bf16[6,16,512]{2,1,0:T(8,128)(2,1)S(1)} %get-tuple-element.30), channel_id=1, source_target_pairs={{0,1},{1,0},{2,3},{3,2},{4,5},{5,4},{6,7},{7,6},{8,9},{9,8},{10,11... | collective-permute-start | bytes 294920 | tf_op jit(solution)/shard_map/ppermute | solution.py:432
  13.7 18.3 %copy-start = (f32[1,6,8,512]{3,2,1,0:T(8,128)S(1)}, f32[1,6,8,512]{3,2,1,0:T(8,128)}, u32[]{:S(2)}) copy-start(f32[1,6,8,512]{3,2,1,0:T(8,128)} %param.7) | copy-start | bytes 294916
  13.7 18.3 %copy-start.1 = (f32[6,8,512]{2,1,0:T(8,128)S(1)}, f32[6,8,512]{2,1,0:T(8,128)}, u32[]{:S(2)}) copy-start(f32[6,8,512]{2,1,0:T(8,128)} %observed.1) | copy-start | bytes 294916
  32.2 2.5 %collective-permute-start.2 = (f32[56,512]{1,0:T(8,128)S(1)}, f32[56,512]{1,0:T(8,128)S(1)}, u32[]{:S(2)}, u32[]{:S(2)}) collective-permute-start(f32[56,512]{1,0:T(8,128)S(1)} %shard_map.113), channel_id=1, source_target_pairs={{0,1},{1,0},{2,3},{3,2},{4,5},{5,4},{6,7},{7,6},{8,9},{9,8},{10,11... | collective-permute-start | bytes 344072 | tf_op jit(solution)/shard_map/ppermute | solution.py:468
  58.4 2.8 %collective-permute-start.3 = (f32[192,128]{1,0:T(8,128)S(1)}, f32[192,128]{1,0:T(8,128)S(1)}, u32[]{:S(2)}, u32[]{:S(2)}) collective-permute-start(f32[192,128]{1,0:T(8,128)S(1)} %get-tuple-element.48), channel_id=1, source_target_pairs={{0,1},{1,0},{2,3},{3,2},{4,5},{5,4},{6,7},{7,6},{8,9},{9,8},{10,11... | collective-permute-start | bytes 294920 | tf_op jit(solution)/shard_map/ppermute | solution.py:489
